TPU v7x, 32 devices: a whole 2x2x4 slice. The times are simulated.
32 devices in a mesh: ta: 16 (over z, x, core), row: 2 (over y).
Axes of the slice: x: 2, y: 2, z: 4, core: 2. Of those that a mesh axis runs over, the one named last changes fastest.
Arguments:
- amplitudes: float32 [8, 512, 96, 512], P(None, 'ta', 'row'), may hold values from -6 to 6
- integrals: bfloat16 [96, 512, 4, 512], P('row', 'ta'), may hold values from -0.0390625 to 0.0390625
Outputs:
- cycle: float32 [8, 512, 4, 512], P(None, 'row', None, 'ta')
All inputs are finite; a program needn't handle non-finite values.
Results may differ from a plain program's by a relative error of at most 0.0029.
Values may be sent and summed in bfloat16 or wider, within the bound.
No kernel may reach another device: no remote copies, remote signals or barrier semaphores. Data moves between devices by JAX's collectives and lax.ppermute only.
A program may use at most 256 MiB of HBM per device.

v0:
```python
import jax
import jax.numpy as jnp
from jax import lax
from jax.sharding import PartitionSpec as P


def body(amplitudes, integrals):
    slab_i, local_a, local_k, full_c = amplitudes.shape
    tiles = lax.axis_size("ta")
    tile_c = full_c // tiles
    lowered = amplitudes.astype(jnp.bfloat16)
    packed = lowered.reshape(slab_i, local_a, local_k, tiles, tile_c)
    packed = jnp.transpose(packed, (0, 1, 3, 2, 4)).reshape(
        slab_i, local_a, tiles, local_k * tile_c
    )
    moved = lax.all_to_all(
        lax.all_to_all(packed, "ta", split_axis=2, concat_axis=1, tiled=True),
        "row",
        split_axis=1,
        concat_axis=2,
        tiled=True,
    )
    rows_a = moved.shape[1]
    merged = moved.reshape(slab_i, rows_a, moved.shape[2] * moved.shape[3])
    count_j = integrals.shape[2]
    width_b = integrals.shape[3]
    cols_c = integrals.shape[1]
    gathered = lax.all_gather(integrals, "row", axis=0, tiled=True)
    left_side = merged.reshape(slab_i * rows_a, merged.shape[2])
    right_side = gathered.reshape(gathered.shape[0] * cols_c, count_j * width_b)
    partial_sum = jnp.dot(left_side, right_side, preferred_element_type=jnp.float32)
    partial_sum = partial_sum.reshape(slab_i, rows_a, count_j, width_b)
    return lax.psum_scatter(partial_sum, "ta", scatter_dimension=3, tiled=True)


def solution(mesh):
    placed = (P(None, "ta", "row", None), P("row", "ta", None, None))
    return jax.shard_map(
        body, mesh=mesh, in_specs=placed, out_specs=P(None, "row", None, "ta"), check_vma=False
    )
```

profile of v0, /device:TPU:0, one launch (start us, length us, event | category | flops | bytes accessed | tf_op | source)
XLA Modules:
  0.0 905.9 jit_solution(15195892338840005207)
XLA Ops:
  6.5 13.5 %convert_element_type.3 = bf16[8,32,48,512]{3,2,1,0:T(8,128)(2,1)} convert(f32[8,32,48,512]{3,2,1,0:T(8,128)} %param.2) | non-fusion elementwise | flops 6291456 | bytes 37748736 | tf_op jit(solution)/shard_map/convert_element_type | solution.py:11
  20.0 54.8 %reshape.14 = bf16[8,32,48,16,32]{4,3,2,1,0:T(8,128)(2,1)} reshape(bf16[8,32,48,512]{3,2,1,0:T(8,128)(2,1)} %convert_element_type.3) | data formatting | bytes 25165824 | tf_op jit(solution)/shard_map/reshape | solution.py:12
  74.8 33.7 %copy.25 = bf16[8,32,16,48,32]{4,3,1,0,2:T(8,128)(2,1)} copy(bf16[8,32,16,48,32]{4,2,3,1,0:T(8,128)(2,1)} %bitcast.29) | data formatting | bytes 25165824 | tf_op jit(solution)/shard_map/reshape | solution.py:13
  108.5 63.7 %reshape.19 = bf16[8,32,16,1536]{3,1,0,2:T(8,128)(2,1)} reshape(bf16[8,32,16,48,32]{4,3,1,0,2:T(8,128)(2,1)} %copy.25) | data formatting | bytes 25165824 | tf_op jit(solution)/shard_map/reshape | solution.py:13
  172.2 7.4 all-to-all-start
  179.6 0.0 all-gather.2.cloned.1.call-start
  179.7 7.6 copy.21
  187.3 0.0 all-gather.2.cloned.1.call-update
  187.3 216.1 %all-to-all-done = bf16[8,32,16,1536]{3,1,0,2:T(8,128)(2,1)} async-done(((bf16[8,32,16,1536]{3,1,0,2:T(8,128)(2,1)}), bf16[8,32,16,1536]{3,1,0,2:T(8,128)(2,1)}, u32[]{:S(2)}, u32[]{:S(2)}) %all-to-all-start) | async-done | bytes 12582944 | tf_op jit(solution)/shard_map/all_to_all | solution.py:17
  403.4 6.6 copy.17
  409.9 33.1 %copy.18 = bf16[8,512,1,1536]{3,0,2,1:T(8,128)(2,1)} copy(bf16[8,512,1,1536]{3,1,0,2:T(8,128)(2,1)S(1)} %bitcast.30) | data formatting | bytes 25165824 | tf_op jit(solution)/shard_map/all_to_all | solution.py:17
  443.0 8.6 all-to-all-start.1
  451.6 0.0 reduce-scatter.2.cloned.1.call-start
  451.6 0.0 all-gather.2.cloned.1.call-done
  451.7 14.4 %copy.22 = bf16[96,32,4,512]{3,2,1,0:T(4,128)(2,1)S(1)} copy(bf16[96,32,4,512]{3,1,2,0:T(8,128)(2,1)} %all-gather.2.cloned.1.call-done) | data formatting | bytes 25165824 | tf_op jit(solution)/shard_map/all_gather | solution.py:28
  466.1 7.3 copy.27
  473.4 16.6 %copy.23 = bf16[2048,3072]{1,0:T(8,128)(2,1)} copy(bf16[2048,3072]{0,1:T(8,128)(2,1)} %bitcast.32) | data formatting | bytes 25165824 | tf_op jit(solution)/shard_map/dot_general | solution.py:31
  490.0 100.1 %all-to-all-done.1 = bf16[8,512,1,1536]{3,0,2,1:T(8,128)(2,1)} async-done(((bf16[8,512,1,1536]{3,0,2,1:T(8,128)(2,1)}), bf16[8,512,1,1536]{3,0,2,1:T(8,128)(2,1)}, u32[]{:S(2)}, u32[]{:S(2)}) %all-to-all-start.1) | async-done | bytes 12582944 | tf_op jit(solution)/shard_map/all_to_all | solution.py:16
  590.1 9.4 %copy.19 = bf16[8,512,1,1536]{3,1,0,2:T(8,128)(2,1)S(1)} copy(bf16[8,512,1,1536]{3,0,2,1:T(8,128)(2,1)} %all-to-all-done.1) | data formatting | bytes 25165824 | tf_op jit(solution)/shard_map/all_to_all | solution.py:16
  599.5 11.3 %copy.20 = bf16[8,256,2,1,1536]{4,2,1,0,3:T(2,128)(2,1)} copy(bf16[8,256,2,1,1536]{4,1,2,0,3:T(8,128)(2,1)S(1)} %bitcast.33) | data formatting | bytes 25165824 | tf_op jit(solution)/shard_map/all_to_all | solution.py:16
  610.8 28.1 %reshape.17 = bf16[8,256,3072,1]{2,1,0,3:T(8,128)(2,1)} reshape(bf16[8,256,2,1,1536]{4,2,1,0,3:T(2,128)(2,1)} %copy.20) | data formatting | bytes 25165824 | tf_op jit(solution)/shard_map/dot_general | solution.py:31
  638.8 34.2 %fusion = f32[8,256,4,512]{1,3,2,0:T(8,128)} fusion(bf16[4,512,3072,1]{2,1,0,3:T(8,128)(2,1)} %bitcast.34, bf16[8,256,3072,1]{2,1,0,3:T(8,128)(2,1)} %reshape.17), kind=kOutput, calls=%fused_computation | convolution fusion | flops 25769803776 | bytes 41943040 | tf_op jit(solution)/shard_map/dot_general | solution.py:31
  673.1 0.0 reduce-scatter.2.cloned.1.call-update
  673.1 226.0 %reduce-scatter.2.cloned.1.call-done = f32[8,256,4,32]{1,3,2,0:T(8,128)} async-done(((f32[8,256,4,512]{1,3,2,0:T(8,128)}), f32[8,256,4,32]{1,3,2,0:T(8,128)}) %reduce-scatter.2.cloned.1.call-update) | async-done | bytes 1048592 | tf_op jit(solution)/shard_map/reduce_scatter | solution.py:33
Async XLA Ops:
  172.2 231.2 %all-to-all-start = ((bf16[8,32,16,1536]{3,1,0,2:T(8,128)(2,1)}), bf16[8,32,16,1536]{3,1,0,2:T(8,128)(2,1)}, u32[]{:S(2)}, u32[]{:S(2)}) async-start(bf16[8,32,16,1536]{3,1,0,2:T(8,128)(2,1)} %reshape.19), calls=%async_computation | async-start | bytes 25165824 | tf_op jit(solution)/shard_map/all_to_all | solution.py:17
  179.6 272.0 %all-gather.2.cloned.1.call-start = ((), (), s32[]{:S(2)}) async-start(), calls=%async_computation.3 | async-start | bytes 18874368 | tf_op jit(solution)/shard_map/all_gather | solution.py:28
  443.0 147.1 %all-to-all-start.1 = ((bf16[8,512,1,1536]{3,0,2,1:T(8,128)(2,1)}), bf16[8,512,1,1536]{3,0,2,1:T(8,128)(2,1)}, u32[]{:S(2)}, u32[]{:S(2)}) async-start(bf16[8,512,1,1536]{3,0,2,1:T(8,128)(2,1)} %copy.18), calls=%async_computation.1 | async-start | bytes 25165824 | tf_op jit(solution)/shard_map/all_to_all | solution.py:16
  451.6 447.5 %reduce-scatter.2.cloned.1.call-start = ((), (), s32[]{:S(2)}) async-start(), calls=%async_computation.4 | async-start | bytes 17825792 | tf_op jit(solution)/shard_map/reduce_scatter | solution.py:33
Sparse Core Ops, SparseCore 0:
  187.4 153.8 all-gather.1
  673.2 225.7 reduce-scatter.1
where the time goes:
time: 910 us; the launch traced here: 906 us
  waiting for transfers between devices  542 us (60%)
  local copies, waits for them, and re-layouts  286 us (31%)
  matrix products  34.2 us (4%)
  starting transfers between devices  16 us (2%)
  other arithmetic  13.5 us (1%)
  between operations  13.5 us (1%)
    reduce_scatter x1, waiting for transfers between devices, body(): return lax.psum_scatter(partial_sum, 'ta', scatter_dimension=3, tiled=True)  226 us
    all_to_all x1, waiting for transfers between devices, body(): lax.all_to_all(packed, 'ta', split_axis=2, concat_axis=1, tiled=True)  216 us
    all_to_all x1, waiting for transfers between devices, body(): lax.all_to_all(lax.all_to_all(packed, 'ta', split_axis=2, concat_axis=1,...  100 us
    reshape x2, local copies, waits for them, and re-layouts, body(): jnp.transpose(packed, (0, 1, 3, 2, 4))  97.4 us
    reshape x1, local copies, waits for them, and re-layouts, body(): packed = lowered.reshape(slab_i, local_a, local_k, tiles, tile_c)  54.8 us
    dot_general x2, local copies, waits for them, and re-layouts, body(): jnp.dot(left_side, right_side, preferred_element_type=jnp.float32)  44.7 us
    all_to_all x2, local copies, waits for them, and re-layouts, body(): lax.all_to_all(packed, 'ta', split_axis=2, concat_axis=1, tiled=True)  39.6 us
    dot_general x1, matrix products, body(): jnp.dot(left_side, right_side, preferred_element_type=jnp.float32)  34.2 us
  transfers between devices with their start and end apart: 4, of which 3 were waited for; matrix products, arithmetic and copies ran while one was open for 9% of the time, Pallas kernels for 0%

commit v1 on v0

--- a/solution.py
+++ b/solution.py
@@ -1,10 +1,18 @@
+import functools
+
 import jax
 import jax.numpy as jnp
 from jax import lax
+from jax.experimental import pallas as pl
+from jax.experimental.pallas import tpu as pltpu
+from jax.sharding import Mesh
 from jax.sharding import PartitionSpec as P
 
-
-def body(amplitudes, integrals):
+LANES = 128
+CHUNKS = (2, 2, 1, 1, 1, 1)
+
+
+def gathered_body(amplitudes, integrals):
     slab_i, local_a, local_k, full_c = amplitudes.shape
     tiles = lax.axis_size("ta")
     tile_c = full_c // tiles
@@ -33,8 +41,170 @@
     return lax.psum_scatter(partial_sum, "ta", scatter_dimension=3, tiled=True)
 
 
+def prep_kernel(la, lk, place, *refs):
+    ins, outs = refs[:4], refs[4:]
+    lane = lax.broadcasted_iota(jnp.int32, (la, LANES), 1)
+    odd = (lane & 32) != 0
+    up = place[1] * 64 + place[2] * 32
+    down = lax.rem(place[1] * 64 + LANES - place[2] * 32, LANES)
+    for src, dst in zip(ins, outs):
+        for k in range(lk):
+            rows = src[0, pl.ds(k, la, stride=lk), :]
+            rows = jnp.where(odd, pltpu.roll(rows, up, 1), pltpu.roll(rows, down, 1))
+            dst[0, k] = rows.astype(jnp.bfloat16)
+
+
+def prep(amps, place, la, lk, start, count):
+    out = jax.ShapeDtypeStruct((count, lk, la, LANES), jnp.bfloat16)
+    return pl.pallas_call(
+        functools.partial(prep_kernel, la, lk),
+        out_shape=[out] * 4,
+        grid_spec=pltpu.PrefetchScalarGridSpec(
+            num_scalar_prefetch=1,
+            grid=(count,),
+            in_specs=[
+                pl.BlockSpec((1, la * lk, LANES), lambda i, place, d=d: (start + i, 0, place[0] ^ d))
+                for d in range(4)
+            ],
+            out_specs=[pl.BlockSpec((1, lk, la, LANES), lambda i, place: (i, 0, 0, 0))] * 4,
+        ),
+        compiler_params=pltpu.CompilerParams(vmem_limit_bytes=32 * 2**20),
+        cost_estimate=pl.CostEstimate(
+            flops=count * la * lk * 512, bytes_accessed=count * la * lk * 512 * 6, transcendentals=0
+        ),
+        name="prep",
+    )(place, amps, amps, amps, amps)
+
+
+def product_kernel(ni, kb, la, nj, place, *refs):
+    ts, ws, out, acc = refs[:4], refs[4:8], refs[8], refs[9]
+    step = pl.program_id(0)
+    left = [
+        jnp.concatenate([t[:, k].reshape(ni * la, LANES) for t in ts], axis=0) for k in range(kb)
+    ]
+    left = jnp.concatenate(left, axis=1)
+    for j in range(nj):
+        right = jnp.concatenate([w[k, j] for k in range(kb) for w in ws], axis=0)
+        value = jnp.dot(left, right, preferred_element_type=jnp.float32)
+
+        @pl.when(step == 0)
+        def _():
+            acc[j] = value
+
+        @pl.when(step > 0)
+        def _():
+            acc[j] += value
+
+    @pl.when(step == pl.num_programs(0) - 1)
+    def _():
+        high, low = place[0] >> 1, place[0] & 1
+        for d in range(4):
+            for q in range(4):
+                for j in range(nj):
+                    piece = acc[j, pl.ds(d * ni * la, ni * la), pl.ds(q * LANES, LANES)]
+                    out[high ^ (d >> 1), q & 1, q >> 1, low ^ (d & 1), j] = piece.reshape(
+                        ni, la, LANES
+                    )
+
+
+def product(place, ts, ws):
+    ni, lk, la, _ = ts[0].shape
+    nj, width = ws[0].shape[1], ws[0].shape[3]
+    lc = ws[0].shape[2]
+    kb = 8
+    rows = 4 * ni * la
+    out = jax.ShapeDtypeStruct((2, 2, 2, 2, nj, ni, la, LANES), jnp.float32)
+    return pl.pallas_call(
+        functools.partial(product_kernel, ni, kb, la, nj),
+        out_shape=out,
+        grid_spec=pltpu.PrefetchScalarGridSpec(
+            num_scalar_prefetch=1,
+            grid=(lk // kb,),
+            in_specs=[pl.BlockSpec((ni, kb, la, LANES), lambda s, place: (0, s, 0, 0))] * 4
+            + [pl.BlockSpec((kb, nj, lc, width), lambda s, place: (s, 0, 0, 0))] * 4,
+            out_specs=pl.BlockSpec(out.shape, lambda s, place: (0,) * 8),
+            scratch_shapes=[pltpu.VMEM((nj, rows, width), jnp.float32)],
+        ),
+        compiler_params=pltpu.CompilerParams(vmem_limit_bytes=48 * 2**20),
+        cost_estimate=pl.CostEstimate(
+            flops=2 * rows * nj * width * lk * 4 * lc,
+            bytes_accessed=lk * 4 * lc * nj * width * 2 + rows * lk * LANES * 2 + rows * nj * width * 4,
+            transcendentals=0,
+        ),
+        name="product",
+    )(place, *ts, *ws)
+
+
+def swapped(x, axis, bits=1):
+    n = lax.axis_size(axis)
+    return lax.ppermute(x, axis, [(s, s ^ bits) for s in range(n)])
+
+
+def exchanged(x, axis, mine, bits=1):
+    kept = lax.dynamic_index_in_dim(x, mine, 0, keepdims=False)
+    sent = lax.dynamic_index_in_dim(x, 1 - mine, 0, keepdims=False)
+    return kept + swapped(sent, axis, bits)
+
+
+def tiled_body(amplitudes, integrals):
+    ni, la, lk, full_c = amplitudes.shape
+    z, x, core, row = (lax.axis_index(n) for n in ("z", "x", "core", "row"))
+    place = jnp.stack([z, x, core]).astype(jnp.int32)
+    amps = amplitudes.reshape(ni, la * lk, full_c)
+    chunks = []
+    start = 0
+    parts = []
+    for count in CHUNKS:
+        parts.append(prep(amps, place, la, lk, start, count))
+        start += count
+    w_own = jnp.transpose(integrals, (0, 2, 1, 3))
+    w_x = swapped(w_own, "x")
+    w_core = swapped(w_own, "core")
+    w_both = swapped(w_x, "core")
+    ws = (w_own, w_core, w_x, w_both)
+    token = None
+    moved = []
+    for own, *others in parts:
+        moved.append((own, *(swapped(o, "z", d) for d, o in zip((1, 2, 3), others))))
+    for ts in moved:
+        total = product(place, ts, ws)
+        total = exchanged(total, "row", row)
+        total = exchanged(total, "z", z & 1, 1)
+        total = exchanged(total, "z", z >> 1, 2)
+        lows, nj, count, _, _ = total.shape
+        total = total.reshape(lows, nj, count, la, 4, LANES // 4)
+        total = jnp.transpose(total, (4, 2, 0, 3, 1, 5))
+        total = lax.all_to_all(total, ("x", "core"), split_axis=0, concat_axis=0, tiled=True)
+        total = jnp.transpose(total, (1, 2, 0, 3, 4, 5))
+        chunks.append(total.reshape(count, lows * 4 * la, nj, LANES // 4))
+    return jnp.concatenate(chunks, axis=0)
+
+
 def solution(mesh):
-    placed = (P(None, "ta", "row", None), P("row", "ta", None, None))
-    return jax.shard_map(
-        body, mesh=mesh, in_specs=placed, out_specs=P(None, "row", None, "ta"), check_vma=False
-    )
+    ta, rows = mesh.shape["ta"], mesh.shape["row"]
+
+    def fn(amplitudes, integrals):
+        ni, a, k, c = amplitudes.shape
+        la, lk = a // ta, k // rows
+        fits = ta == 16 and rows == 2 and c == 4 * LANES and la % 16 == 0 and lk % 8 == 0
+        fits = fits and ni == sum(CHUNKS)
+        if not fits:
+            placed = (P(None, "ta", "row", None), P("row", "ta", None, None))
+            return jax.shard_map(
+                gathered_body,
+                mesh=mesh,
+                in_specs=placed,
+                out_specs=P(None, "row", None, "ta"),
+                check_vma=False,
+            )(amplitudes, integrals)
+        fine = Mesh(mesh.devices.reshape(4, 2, 2, 2), ("z", "x", "core", "row"))
+        ta_axes = ("z", "x", "core")
+        return jax.shard_map(
+            tiled_body,
+            mesh=fine,
+            in_specs=(P(None, ta_axes, "row", None), P("row", ta_axes, None, None)),
+            out_specs=P(None, "row", None, ta_axes),
+            check_vma=False,
+        )(amplitudes, integrals)
+
+    return fn

time: 910 us -> 585 us (0.64)
  waiting for transfers between devices: 542 us -> 258 us
  local copies, waits for them, and re-layouts: 286 us -> 41.2 us
  starting transfers between devices: 16 us -> 160 us
  Pallas kernels: 0 us -> 106 us
  matrix products: 34.2 us -> 0 us
  between operations: 13.5 us -> 0.72 us
    all_to_all x2 -> x6, waiting for transfers between devices: 316 us -> 7.77 us  [tiled_body(): lax.all_to_all(total, ('x', 'core'), split_axis=0, concat_axis=0, tiled=T...]
    ppermute x0 -> x39, waiting for transfers between devices: none -> 250 us  [swapped(): return lax.ppermute(x, axis, [(s, s ^ bits) for s in range(n)])]
    reduce_scatter x1 -> x0, waiting for transfers between devices: 226 us -> none  [body(): return lax.psum_scatter(partial_sum, 'ta', scatter_dimension=3, tiled=True)]
    reshape x3 -> x12, local copies, waits for them, and re-layouts: 152 us -> 4.46 us  [the longest x6 2.54 us: tiled_body(): chunks.append(total.reshape(count, lows * 4 * la, nj, LANES // 4))]
    ppermute x0 -> x39, starting transfers between devices: none -> 138 us  [swapped(): return lax.ppermute(x, axis, [(s, s ^ bits) for s in range(n)])]
    pallas_call x0 -> x12, Pallas kernels: none -> 106 us  [the longest x6 81.4 us: product(): pl.pallas_call(functools.partial(product_kernel, ni, kb, la, nj), out_sha...]
    all_to_all x4 -> x1, local copies, waits for them, and re-layouts: 60.3 us -> 0.54 us  [tiled_body(): lax.all_to_all(total, ('x', 'core'), split_axis=0, concat_axis=0, tiled=T...]
    dot_general x2 -> x0, local copies, waits for them, and re-layouts: 44.7 us -> none  [body(): jnp.dot(left_side, right_side, preferred_element_type=jnp.float32)]
  transfers between devices with their start and end apart: 4 -> 45, of which waited for: 3 -> 16; matrix products, arithmetic and copies ran while one was open for 9% -> 8% of each run, Pallas kernels for 0% -> 18%
where the time goes in v1:
time: 585 us; the launch traced here: 583 us
  waiting for transfers between devices  258 us (44%)
  starting transfers between devices  160 us (27%)
  Pallas kernels  106 us (18%)
  local copies, waits for them, and re-layouts  41.2 us (7%)
  other arithmetic  17 us (3%)
    ppermute x39, waiting for transfers between devices, swapped(): return lax.ppermute(x, axis, [(s, s ^ bits) for s in range(n)])  250 us
    ppermute x39, starting transfers between devices, swapped(): return lax.ppermute(x, axis, [(s, s ^ bits) for s in range(n)])  138 us
    pallas_call x6, Pallas kernels, product(): pl.pallas_call(functools.partial(product_kernel, ni, kb, la, nj), out_sha...  81.4 us
    pallas_call x6, Pallas kernels, prep(): pl.pallas_call(functools.partial(prep_kernel, la, lk), out_shape=[out] *...  25 us
    all_to_all x6, starting transfers between devices, tiled_body(): lax.all_to_all(total, ('x', 'core'), split_axis=0, concat_axis=0, tiled=T...  21.8 us
    unnamed x34, local copies, waits for them, and re-layouts  17.6 us
  transfers between devices with their start and end apart: 45, of which 16 were waited for; matrix products, arithmetic and copies ran while one was open for 8% of the time, Pallas kernels for 18%

profile of v1, /device:TPU:0, one launch (start us, length us, event | category | flops | bytes accessed | tf_op | source)
XLA Modules:
  0.0 583.3 jit_solution(18199739783971398334)
XLA Ops:
  0.0 7.6 %copy.32 = bf16[48,32,4,512]{3,1,2,0:T(8,128)(2,1)} copy(bf16[48,32,4,512]{3,2,1,0:T(4,128)(2,1)} %param.3) | data formatting | bytes 12582912 | tf_op args[1]
  7.6 2.9 collective-permute-start.4
  10.5 135.8 %collective-permute-done.4.refs_6_ = bf16[48,4,32,512]{3,2,1,0:T(8,128)(2,1)} collective-permute-done((bf16[48,4,32,512]{3,2,1,0:T(8,128)(2,1)}, bf16[48,4,32,512]{3,2,1,0:T(8,128)(2,1)}, u32[]{:S(2)}, u32[]{:S(2)}) %collective-permute-start.4) | collective-permute-done | bytes 6291488 | tf_op jit(solution)/shard_map/ppermute | solution.py:140
  146.4 4.2 prep.11
  152.4 2.6 collective-permute-start.34
  155.0 3.4 prep.10
  158.4 3.4 prep.9
  161.8 3.4 prep.8
  165.1 5.5 prep.7
  170.6 5.2 prep.6
  176.8 5.6 collective-permute-done.34.refs_2_
  182.4 2.4 collective-permute-start.29
  184.9 24.9 %collective-permute-start.21 = (bf16[1,48,32,128]{3,2,1,0:T(8,128)(2,1)S(1)}, bf16[1,48,32,128]{3,2,1,0:T(8,128)(2,1)S(1)}, u32[]{:S(2)}, u32[]{:S(2)}) collective-permute-start(bf16[1,48,32,128]{3,2,1,0:T(8,128)(2,1)S(1)} %get-tuple-element.42), channel_id=1, source_target_pairs={{0,8},{8,0},{16,24},{24,16},{1,9},{9,1},{17,25},{25,17},{2,10},{10... | collective-permute-start | bytes 1179656 | tf_op jit(solution)/shard_map/ppermute | solution.py:140
  209.8 12.8 %product.11 = f32[2,2,2,2,4,1,32,128]{7,6,5,4,3,2,1,0:T(8,128)S(1)} custom-call(s32[3]{0:T(128)S(1)} %pad_add_fusion.place, bf16[1,48,32,128]{3,2,1,0:T(8,128)(2,1)S(1)} %get-tuple-element.49.refs_0_, bf16[1,48,32,128]{3,2,1,0:T(8,128)(2,1)S(1)} %collective-permute-done.33.refs_1_, bf16[1,48,32,128]{3,2,1,0:T(8,128)(2,1)S(1)} %collective-permute-done.34.refs_2_, ...), custom_call_target="tpu_custom_call" | custom-call | flops 3221225472 | bytes 27787264 | tf_op jit(solution)/shard_map/product/pallas_call | solution.py:117
  222.7 2.5 collective-permute-start.23
  226.2 16.7 %collective-permute-start.10 = (bf16[2,48,32,128]{3,2,1,0:T(8,128)(2,1)}, bf16[2,48,32,128]{3,2,1,0:T(8,128)(2,1)S(1)}, u32[]{:S(2)}, u32[]{:S(2)}) collective-permute-start(bf16[2,48,32,128]{3,2,1,0:T(8,128)(2,1)} %get-tuple-element.35), channel_id=1, source_target_pairs={{0,16},{8,24},{16,0},{24,8},{1,17},{9,25},{17,1},{25,9},{2,18},{10... | collective-permute-start | bytes 2359304 | tf_op jit(solution)/shard_map/ppermute | solution.py:140
  243.0 12.8 %product.10 = f32[2,2,2,2,4,1,32,128]{7,6,5,4,3,2,1,0:T(8,128)S(1)} custom-call(s32[3]{0:T(128)S(1)} %pad_add_fusion.place, bf16[1,48,32,128]{3,2,1,0:T(8,128)(2,1)S(1)} %get-tuple-element.45.refs_0_, bf16[1,48,32,128]{3,2,1,0:T(8,128)(2,1)S(1)} %collective-permute-done.27.refs_1_, bf16[1,48,32,128]{3,2,1,0:T(8,128)(2,1)S(1)} %collective-permute-done.28.refs_2_, ...), custom_call_target="tpu_custom_call" | custom-call | flops 3221225472 | bytes 27787264 | tf_op jit(solution)/shard_map/product/pallas_call | solution.py:117
  256.7 18.5 %collective-permute-done.22.refs_2_ = bf16[1,48,32,128]{3,2,1,0:T(8,128)(2,1)S(1)} collective-permute-done((bf16[1,48,32,128]{3,2,1,0:T(8,128)(2,1)S(1)}, bf16[1,48,32,128]{3,2,1,0:T(8,128)(2,1)S(1)}, u32[]{:S(2)}, u32[]{:S(2)}) %collective-permute-start.22) | collective-permute-done | bytes 393248 | tf_op jit(solution)/shard_map/ppermute | solution.py:140
  275.2 2.4 collective-permute-start.17
  279.0 32.0 %collective-permute-start.9 = (bf16[2,48,32,128]{3,2,1,0:T(8,128)(2,1)}, bf16[2,48,32,128]{3,2,1,0:T(8,128)(2,1)S(1)}, u32[]{:S(2)}, u32[]{:S(2)}) collective-permute-start(bf16[2,48,32,128]{3,2,1,0:T(8,128)(2,1)} %get-tuple-element.34), channel_id=1, source_target_pairs={{0,8},{8,0},{16,24},{24,16},{1,9},{9,1},{17,25},{25,17},{2,10},{10... | collective-permute-start | bytes 2359304 | tf_op jit(solution)/shard_map/ppermute | solution.py:140
  311.0 12.8 %product.9 = f32[2,2,2,2,4,1,32,128]{7,6,5,4,3,2,1,0:T(8,128)S(1)} custom-call(s32[3]{0:T(128)S(1)} %pad_add_fusion.place, bf16[1,48,32,128]{3,2,1,0:T(8,128)(2,1)S(1)} %get-tuple-element.41.refs_0_, bf16[1,48,32,128]{3,2,1,0:T(8,128)(2,1)S(1)} %collective-permute-done.21.refs_1_, bf16[1,48,32,128]{3,2,1,0:T(8,128)(2,1)S(1)} %collective-permute-done.22.refs_2_, ...), custom_call_target="tpu_custom_call" | custom-call | flops 3221225472 | bytes 27787264 | tf_op jit(solution)/shard_map/product/pallas_call | solution.py:117
  324.7 9.6 %collective-permute-done.16.refs_2_ = bf16[1,48,32,128]{3,2,1,0:T(8,128)(2,1)S(1)} collective-permute-done((bf16[1,48,32,128]{3,2,1,0:T(8,128)(2,1)S(1)}, bf16[1,48,32,128]{3,2,1,0:T(8,128)(2,1)S(1)}, u32[]{:S(2)}, u32[]{:S(2)}) %collective-permute-start.16) | collective-permute-done | bytes 393248 | tf_op jit(solution)/shard_map/ppermute | solution.py:140
  334.3 10.0 %collective-permute-start.1 = (bf16[2,48,32,128]{3,2,1,0:T(8,128)(2,1)}, bf16[2,48,32,128]{3,2,1,0:T(8,128)(2,1)S(1)}, u32[]{:S(2)}, u32[]{:S(2)}) collective-permute-start(bf16[2,48,32,128]{3,2,1,0:T(8,128)(2,1)} %get-tuple-element.31), channel_id=1, source_target_pairs={{0,16},{8,24},{16,0},{24,8},{1,17},{9,25},{17,1},{25,9},{2,18},{10... | collective-permute-start | bytes 2359304 | tf_op jit(solution)/shard_map/ppermute | solution.py:140
  344.2 12.8 %product.8 = f32[2,2,2,2,4,1,32,128]{7,6,5,4,3,2,1,0:T(8,128)S(1)} custom-call(s32[3]{0:T(128)S(1)} %pad_add_fusion.place, bf16[1,48,32,128]{3,2,1,0:T(8,128)(2,1)S(1)} %get-tuple-element.37.refs_0_, bf16[1,48,32,128]{3,2,1,0:T(8,128)(2,1)S(1)} %collective-permute-done.15.refs_1_, bf16[1,48,32,128]{3,2,1,0:T(8,128)(2,1)S(1)} %collective-permute-done.16.refs_2_, ...), custom_call_target="tpu_custom_call" | custom-call | flops 3221225472 | bytes 27787264 | tf_op jit(solution)/shard_map/product/pallas_call | solution.py:117
  361.3 15.2 %product.7 = f32[2,2,2,2,4,2,32,128]{7,6,5,4,3,2,1,0:T(8,128)S(1)} custom-call(s32[3]{0:T(128)S(1)} %pad_add_fusion.place, bf16[2,48,32,128]{3,2,1,0:T(8,128)(2,1)S(1)} %get-tuple-element.33.refs_0_, bf16[2,48,32,128]{3,2,1,0:T(8,128)(2,1)S(1)} %collective-permute-done.9.refs_1_, bf16[2,48,32,128]{3,2,1,0:T(8,128)(2,1)S(1)} %collective-permute-done.10.refs_2_, ...), custom_call_target="tpu_custom_call" | custom-call | flops 6442450944 | bytes 30408704 | tf_op jit(solution)/shard_map/product/pallas_call | solution.py:117
  379.1 31.0 %collective-permute-done.1.refs_2_ = bf16[2,48,32,128]{3,2,1,0:T(8,128)(2,1)S(1)} collective-permute-done((bf16[2,48,32,128]{3,2,1,0:T(8,128)(2,1)}, bf16[2,48,32,128]{3,2,1,0:T(8,128)(2,1)S(1)}, u32[]{:S(2)}, u32[]{:S(2)}) %collective-permute-start.1) | collective-permute-done | bytes 786464 | tf_op jit(solution)/shard_map/ppermute | solution.py:140
  412.1 15.2 %product.6 = f32[2,2,2,2,4,2,32,128]{7,6,5,4,3,2,1,0:T(8,128)S(1)} custom-call(s32[3]{0:T(128)S(1)} %pad_add_fusion.place, bf16[2,48,32,128]{3,2,1,0:T(8,128)(2,1)S(1)} %get-tuple-element.29.refs_0_, bf16[2,48,32,128]{3,2,1,0:T(8,128)(2,1)S(1)} %collective-permute-done.refs_1_, bf16[2,48,32,128]{3,2,1,0:T(8,128)(2,1)S(1)} %collective-permute-done.1.refs_2_, ...), custom_call_target="tpu_custom_call" | custom-call | flops 6442450944 | bytes 30408704 | tf_op jit(solution)/shard_map/product/pallas_call | solution.py:117
  430.2 15.3 %collective-permute-start.37 = (f32[2,2,4,1,32,128]{5,4,2,1,3,0:T(8,128)S(1)}, f32[2,2,4,1,32,128]{5,4,2,1,3,0:T(8,128)S(1)}, u32[]{:S(2)}, u32[]{:S(2)}) collective-permute-start(f32[2,2,4,1,32,128]{5,4,2,1,3,0:T(8,128)S(1)} %dynamic-slice_bitcast_fusion.8), channel_id=1, source_target_pairs={{0,8},{8,0},{16,24},{24,16},{1,9},{9,1},{17,25},{25,17},{2,10},{10... | collective-permute-start | bytes 786440 | tf_op jit(solution)/shard_map/ppermute | solution.py:140
  445.8 2.1 collective-permute-start.25
  448.0 4.7 collective-permute-done.37
  454.7 3.5 collective-permute-done.31
  458.3 3.0 collective-permute-start.38
  462.0 6.0 %collective-permute-done.25 = f32[2,2,4,1,32,128]{5,4,2,1,3,0:T(8,128)S(1)} collective-permute-done((f32[2,2,4,1,32,128]{5,4,2,1,3,0:T(8,128)S(1)}, f32[2,2,4,1,32,128]{5,4,2,1,3,0:T(8,128)S(1)}, u32[]{:S(2)}, u32[]{:S(2)}) %collective-permute-start.25) | collective-permute-done | bytes 262176 | tf_op jit(solution)/shard_map/ppermute | solution.py:140
  469.4 2.4 collective-permute-done.19
  473.2 2.2 collective-permute-start.20
  476.7 3.5 all-to-all-start.5
  480.3 3.5 collective-permute-done.32
  486.0 3.9 all-to-all-start.4
  492.2 2.5 all-to-all-done.4
  494.7 3.9 all-to-all-start.3
  500.8 2.5 all-to-all-done.3
  503.3 3.3 all-to-all-start.2
  525.1 10.3 %collective-permute-done.13 = f32[2,2,4,2,32,128]{5,4,3,2,1,0:T(8,128)S(1)} collective-permute-done((f32[2,2,4,2,32,128]{5,4,3,2,1,0:T(8,128)S(1)}, f32[2,2,4,2,32,128]{5,4,3,2,1,0:T(8,128)S(1)}, u32[]{:S(2)}, u32[]{:S(2)}) %collective-permute-start.13) | collective-permute-done | bytes 524320 | tf_op jit(solution)/shard_map/ppermute | solution.py:140
  536.3 15.6 %collective-permute-done.7 = f32[2,2,4,2,32,128]{5,4,3,2,1,0:T(8,128)S(1)} collective-permute-done((f32[2,2,4,2,32,128]{5,4,3,2,1,0:T(8,128)S(1)}, f32[2,2,4,2,32,128]{5,4,3,2,1,0:T(8,128)S(1)}, u32[]{:S(2)}, u32[]{:S(2)}) %collective-permute-start.7) | collective-permute-done | bytes 524320 | tf_op jit(solution)/shard_map/ppermute | solution.py:140
  559.7 3.4 all-to-all-start.1
  563.1 3.3 collective-permute-done.8
  569.1 3.7 all-to-all-start
  575.8 2.8 all-to-all-done
  (163 shorter events, 69.9 us)
Async XLA Ops:
  7.6 138.8 %collective-permute-start.4 = (bf16[48,4,32,512]{3,2,1,0:T(8,128)(2,1)}, bf16[48,4,32,512]{3,2,1,0:T(8,128)(2,1)}, u32[]{:S(2)}, u32[]{:S(2)}) collective-permute-start(bf16[48,4,32,512]{3,2,1,0:T(8,128)(2,1)} %bitcast.152.refs_4_), channel_id=1, source_target_pairs={{0,4},{4,0},{1,5},{5,1},{2,6},{6,2},{3,7},{7,3},{8,12},{12,8},{9,1... | collective-permute-start | bytes 18874376 | tf_op jit(solution)/shard_map/ppermute | solution.py:140
  10.5 174.4 %collective-permute-start.3 = (bf16[48,4,32,512]{3,2,1,0:T(8,128)(2,1)}, bf16[48,4,32,512]{3,2,1,0:T(8,128)(2,1)}, u32[]{:S(2)}, u32[]{:S(2)}) collective-permute-start(bf16[48,4,32,512]{3,2,1,0:T(8,128)(2,1)} %bitcast.152.refs_4_), channel_id=1, source_target_pairs={{0,2},{2,0},{1,3},{3,1},{4,6},{6,4},{5,7},{7,5},{8,10},{10,8},{9,1... | collective-permute-start | bytes 18874376 | tf_op jit(solution)/shard_map/ppermute | solution.py:140
  146.3 63.5 %collective-permute-start.5 = (bf16[48,4,32,512]{3,2,1,0:T(8,128)(2,1)}, bf16[48,4,32,512]{3,2,1,0:T(8,128)(2,1)}, u32[]{:S(2)}, u32[]{:S(2)}) collective-permute-start(bf16[48,4,32,512]{3,2,1,0:T(8,128)(2,1)} %collective-permute-done.4.refs_6_), channel_id=1, source_target_pairs={{0,2},{2,0},{1,3},{3,1},{4,6},{6,4},{5,7},{7,5},{8,10},{10,8},{9,1... | collective-permute-start | bytes 18874376 | tf_op jit(solution)/shard_map/ppermute | solution.py:140
  150.6 25.3 %collective-permute-start.33 = (bf16[1,48,32,128]{3,2,1,0:T(8,128)(2,1)}, bf16[1,48,32,128]{3,2,1,0:T(8,128)(2,1)S(1)}, u32[]{:S(2)}, u32[]{:S(2)}) collective-permute-start(bf16[1,48,32,128]{3,2,1,0:T(8,128)(2,1)} %get-tuple-element.50), channel_id=1, source_target_pairs={{0,8},{8,0},{16,24},{24,16},{1,9},{9,1},{17,25},{25,17},{2,10},{10... | collective-permute-start | bytes 1179656 | tf_op jit(solution)/shard_map/ppermute | solution.py:140
  152.4 30.0 %collective-permute-start.34 = (bf16[1,48,32,128]{3,2,1,0:T(8,128)(2,1)}, bf16[1,48,32,128]{3,2,1,0:T(8,128)(2,1)S(1)}, u32[]{:S(2)}, u32[]{:S(2)}) collective-permute-start(bf16[1,48,32,128]{3,2,1,0:T(8,128)(2,1)} %get-tuple-element.51), channel_id=1, source_target_pairs={{0,16},{8,24},{16,0},{24,8},{1,17},{9,25},{17,1},{25,9},{2,18},{10... | collective-permute-start | bytes 1179656 | tf_op jit(solution)/shard_map/ppermute | solution.py:140
  155.0 27.4 %collective-permute-start.35 = (bf16[1,48,32,128]{3,2,1,0:T(8,128)(2,1)S(1)}, bf16[1,48,32,128]{3,2,1,0:T(8,128)(2,1)S(1)}, u32[]{:S(2)}, u32[]{:S(2)}) collective-permute-start(bf16[1,48,32,128]{3,2,1,0:T(8,128)(2,1)S(1)} %get-tuple-element.52), channel_id=1, source_target_pairs={{0,24},{8,16},{16,8},{24,0},{1,25},{9,17},{17,9},{25,1},{2,26},{10... | collective-permute-start | bytes 1179656 | tf_op jit(solution)/shard_map/ppermute | solution.py:140
  175.9 46.8 %collective-permute-start.27 = (bf16[1,48,32,128]{3,2,1,0:T(8,128)(2,1)S(1)}, bf16[1,48,32,128]{3,2,1,0:T(8,128)(2,1)S(1)}, u32[]{:S(2)}, u32[]{:S(2)}) collective-permute-start(bf16[1,48,32,128]{3,2,1,0:T(8,128)(2,1)S(1)} %get-tuple-element.46), channel_id=1, source_target_pairs={{0,8},{8,0},{16,24},{24,16},{1,9},{9,1},{17,25},{25,17},{2,10},{10... | collective-permute-start | bytes 1179656 | tf_op jit(solution)/shard_map/ppermute | solution.py:140
  182.4 42.7 %collective-permute-start.28 = (bf16[1,48,32,128]{3,2,1,0:T(8,128)(2,1)S(1)}, bf16[1,48,32,128]{3,2,1,0:T(8,128)(2,1)S(1)}, u32[]{:S(2)}, u32[]{:S(2)}) collective-permute-start(bf16[1,48,32,128]{3,2,1,0:T(8,128)(2,1)S(1)} %get-tuple-element.47), channel_id=1, source_target_pairs={{0,16},{8,24},{16,0},{24,8},{1,17},{9,25},{17,1},{25,9},{2,18},{10... | collective-permute-start | bytes 1179656 | tf_op jit(solution)/shard_map/ppermute | solution.py:140
  182.4 43.8 %collective-permute-start.29 = (bf16[1,48,32,128]{3,2,1,0:T(8,128)(2,1)S(1)}, bf16[1,48,32,128]{3,2,1,0:T(8,128)(2,1)S(1)}, u32[]{:S(2)}, u32[]{:S(2)}) collective-permute-start(bf16[1,48,32,128]{3,2,1,0:T(8,128)(2,1)S(1)} %get-tuple-element.48), channel_id=1, source_target_pairs={{0,24},{8,16},{16,8},{24,0},{1,25},{9,17},{17,9},{25,1},{2,26},{10... | collective-permute-start | bytes 1179656 | tf_op jit(solution)/shard_map/ppermute | solution.py:140
  184.9 71.8 %collective-permute-start.21 = (bf16[1,48,32,128]{3,2,1,0:T(8,128)(2,1)S(1)}, bf16[1,48,32,128]{3,2,1,0:T(8,128)(2,1)S(1)}, u32[]{:S(2)}, u32[]{:S(2)}) collective-permute-start(bf16[1,48,32,128]{3,2,1,0:T(8,128)(2,1)S(1)} %get-tuple-element.42), channel_id=1, source_target_pairs={{0,8},{8,0},{16,24},{24,16},{1,9},{9,1},{17,25},{25,17},{2,10},{10... | collective-permute-start | bytes 1179656 | tf_op jit(solution)/shard_map/ppermute | solution.py:140
  209.8 65.4 %collective-permute-start.22 = (bf16[1,48,32,128]{3,2,1,0:T(8,128)(2,1)S(1)}, bf16[1,48,32,128]{3,2,1,0:T(8,128)(2,1)S(1)}, u32[]{:S(2)}, u32[]{:S(2)}) collective-permute-start(bf16[1,48,32,128]{3,2,1,0:T(8,128)(2,1)S(1)} %get-tuple-element.43), channel_id=1, source_target_pairs={{0,16},{8,24},{16,0},{24,8},{1,17},{9,25},{17,1},{25,9},{2,18},{10... | collective-permute-start | bytes 1179656 | tf_op jit(solution)/shard_map/ppermute | solution.py:140
  222.7 54.9 %collective-permute-start.23 = (bf16[1,48,32,128]{3,2,1,0:T(8,128)(2,1)S(1)}, bf16[1,48,32,128]{3,2,1,0:T(8,128)(2,1)S(1)}, u32[]{:S(2)}, u32[]{:S(2)}) collective-permute-start(bf16[1,48,32,128]{3,2,1,0:T(8,128)(2,1)S(1)} %get-tuple-element.44), channel_id=1, source_target_pairs={{0,24},{8,16},{16,8},{24,0},{1,25},{9,17},{17,9},{25,1},{2,26},{10... | collective-permute-start | bytes 1179656 | tf_op jit(solution)/shard_map/ppermute | solution.py:140
  225.2 53.9 %collective-permute-start.15 = (bf16[1,48,32,128]{3,2,1,0:T(8,128)(2,1)S(1)}, bf16[1,48,32,128]{3,2,1,0:T(8,128)(2,1)S(1)}, u32[]{:S(2)}, u32[]{:S(2)}) collective-permute-start(bf16[1,48,32,128]{3,2,1,0:T(8,128)(2,1)S(1)} %get-tuple-element.38), channel_id=1, source_target_pairs={{0,8},{8,0},{16,24},{24,16},{1,9},{9,1},{17,25},{25,17},{2,10},{10... | collective-permute-start | bytes 1179656 | tf_op jit(solution)/shard_map/ppermute | solution.py:140
  226.2 130.7 %collective-permute-start.10 = (bf16[2,48,32,128]{3,2,1,0:T(8,128)(2,1)}, bf16[2,48,32,128]{3,2,1,0:T(8,128)(2,1)S(1)}, u32[]{:S(2)}, u32[]{:S(2)}) collective-permute-start(bf16[2,48,32,128]{3,2,1,0:T(8,128)(2,1)} %get-tuple-element.35), channel_id=1, source_target_pairs={{0,16},{8,24},{16,0},{24,8},{1,17},{9,25},{17,1},{25,9},{2,18},{10... | collective-permute-start | bytes 2359304 | tf_op jit(solution)/shard_map/ppermute | solution.py:140
  256.7 77.6 %collective-permute-start.16 = (bf16[1,48,32,128]{3,2,1,0:T(8,128)(2,1)S(1)}, bf16[1,48,32,128]{3,2,1,0:T(8,128)(2,1)S(1)}, u32[]{:S(2)}, u32[]{:S(2)}) collective-permute-start(bf16[1,48,32,128]{3,2,1,0:T(8,128)(2,1)S(1)} %get-tuple-element.39), channel_id=1, source_target_pairs={{0,16},{8,24},{16,0},{24,8},{1,17},{9,25},{17,1},{25,9},{2,18},{10... | collective-permute-start | bytes 1179656 | tf_op jit(solution)/shard_map/ppermute | solution.py:140
  275.2 59.0 %collective-permute-start.17 = (bf16[1,48,32,128]{3,2,1,0:T(8,128)(2,1)S(1)}, bf16[1,48,32,128]{3,2,1,0:T(8,128)(2,1)S(1)}, u32[]{:S(2)}, u32[]{:S(2)}) collective-permute-start(bf16[1,48,32,128]{3,2,1,0:T(8,128)(2,1)S(1)} %get-tuple-element.40), channel_id=1, source_target_pairs={{0,24},{8,16},{16,8},{24,0},{1,25},{9,17},{17,9},{25,1},{2,26},{10... | collective-permute-start | bytes 1179656 | tf_op jit(solution)/shard_map/ppermute | solution.py:140
  277.7 81.6 %collective-permute-start.11 = (bf16[2,48,32,128]{3,2,1,0:T(8,128)(2,1)}, bf16[2,48,32,128]{3,2,1,0:T(8,128)(2,1)S(1)}, u32[]{:S(2)}, u32[]{:S(2)}) collective-permute-start(bf16[2,48,32,128]{3,2,1,0:T(8,128)(2,1)} %get-tuple-element.36), channel_id=1, source_target_pairs={{0,24},{8,16},{16,8},{24,0},{1,25},{9,17},{17,9},{25,1},{2,26},{10... | collective-permute-start | bytes 2359304 | tf_op jit(solution)/shard_map/ppermute | solution.py:140
  279.0 81.8 %collective-permute-start.9 = (bf16[2,48,32,128]{3,2,1,0:T(8,128)(2,1)}, bf16[2,48,32,128]{3,2,1,0:T(8,128)(2,1)S(1)}, u32[]{:S(2)}, u32[]{:S(2)}) collective-permute-start(bf16[2,48,32,128]{3,2,1,0:T(8,128)(2,1)} %get-tuple-element.34), channel_id=1, source_target_pairs={{0,8},{8,0},{16,24},{24,16},{1,9},{9,1},{17,25},{25,17},{2,10},{10... | collective-permute-start | bytes 2359304 | tf_op jit(solution)/shard_map/ppermute | solution.py:140
  334.2 43.3 %collective-permute-start = (bf16[2,48,32,128]{3,2,1,0:T(8,128)(2,1)}, bf16[2,48,32,128]{3,2,1,0:T(8,128)(2,1)S(1)}, u32[]{:S(2)}, u32[]{:S(2)}) collective-permute-start(bf16[2,48,32,128]{3,2,1,0:T(8,128)(2,1)} %get-tuple-element.30), channel_id=1, source_target_pairs={{0,8},{8,0},{16,24},{24,16},{1,9},{9,1},{17,25},{25,17},{2,10},{10... | collective-permute-start | bytes 2359304 | tf_op jit(solution)/shard_map/ppermute | solution.py:140
  334.3 75.8 %collective-permute-start.1 = (bf16[2,48,32,128]{3,2,1,0:T(8,128)(2,1)}, bf16[2,48,32,128]{3,2,1,0:T(8,128)(2,1)S(1)}, u32[]{:S(2)}, u32[]{:S(2)}) collective-permute-start(bf16[2,48,32,128]{3,2,1,0:T(8,128)(2,1)} %get-tuple-element.31), channel_id=1, source_target_pairs={{0,16},{8,24},{16,0},{24,8},{1,17},{9,25},{17,1},{25,9},{2,18},{10... | collective-permute-start | bytes 2359304 | tf_op jit(solution)/shard_map/ppermute | solution.py:140
  357.0 54.6 %collective-permute-start.2 = (bf16[2,48,32,128]{3,2,1,0:T(8,128)(2,1)S(1)}, bf16[2,48,32,128]{3,2,1,0:T(8,128)(2,1)S(1)}, u32[]{:S(2)}, u32[]{:S(2)}) collective-permute-start(bf16[2,48,32,128]{3,2,1,0:T(8,128)(2,1)S(1)} %get-tuple-element.32), channel_id=1, source_target_pairs={{0,24},{8,16},{16,8},{24,0},{1,25},{9,17},{17,9},{25,1},{2,26},{10... | collective-permute-start | bytes 2359304 | tf_op jit(solution)/shard_map/ppermute | solution.py:140
  359.3 69.2 %collective-permute-start.36 = (f32[2,2,2,4,1,32,128]{6,5,3,2,1,0,4:T(8,128)S(1)}, f32[2,2,2,4,1,32,128]{6,5,3,2,1,0,4:T(8,128)S(1)}, u32[]{:S(2)}, u32[]{:S(2)}) collective-permute-start(f32[2,2,2,4,1,32,128]{6,5,3,2,1,0,4:T(8,128)S(1)} %dynamic-slice_bitcast_fusion.2), channel_id=1, source_target_pairs={{0,1},{1,0},{2,3},{3,2},{4,5},{5,4},{6,7},{7,6},{8,9},{9,8},{10,11... | collective-permute-start | bytes 1572872 | tf_op jit(solution)/shard_map/ppermute | solution.py:140
  360.8 69.3 %collective-permute-start.30 = (f32[2,2,2,4,1,32,128]{6,5,3,2,1,0,4:T(8,128)}, f32[2,2,2,4,1,32,128]{6,5,3,2,1,0,4:T(8,128)S(1)}, u32[]{:S(2)}, u32[]{:S(2)}) collective-permute-start(f32[2,2,2,4,1,32,128]{6,5,3,2,1,0,4:T(8,128)} %dynamic-slice_bitcast_fusion.3), channel_id=1, source_target_pairs={{0,1},{1,0},{2,3},{3,2},{4,5},{5,4},{6,7},{7,6},{8,9},{9,8},{10,11... | collective-permute-start | bytes 1572872 | tf_op jit(solution)/shard_map/ppermute | solution.py:140
  377.5 68.0 %collective-permute-start.24 = (f32[2,2,2,4,1,32,128]{6,5,3,2,1,0,4:T(8,128)}, f32[2,2,2,4,1,32,128]{6,5,3,2,1,0,4:T(8,128)S(1)}, u32[]{:S(2)}, u32[]{:S(2)}) collective-permute-start(f32[2,2,2,4,1,32,128]{6,5,3,2,1,0,4:T(8,128)} %dynamic-slice_bitcast_fusion.4), channel_id=1, source_target_pairs={{0,1},{1,0},{2,3},{3,2},{4,5},{5,4},{6,7},{7,6},{8,9},{9,8},{10,11... | collective-permute-start | bytes 1572872 | tf_op jit(solution)/shard_map/ppermute | solution.py:140
  410.1 35.7 %collective-permute-start.18 = (f32[2,2,2,4,1,32,128]{6,5,3,2,1,0,4:T(8,128)}, f32[2,2,2,4,1,32,128]{6,5,3,2,1,0,4:T(8,128)S(1)}, u32[]{:S(2)}, u32[]{:S(2)}) collective-permute-start(f32[2,2,2,4,1,32,128]{6,5,3,2,1,0,4:T(8,128)} %dynamic-slice_bitcast_fusion.5), channel_id=1, source_target_pairs={{0,1},{1,0},{2,3},{3,2},{4,5},{5,4},{6,7},{7,6},{8,9},{9,8},{10,11... | collective-permute-start | bytes 1572872 | tf_op jit(solution)/shard_map/ppermute | solution.py:140
  411.6 107.5 %collective-permute-start.12 = (f32[2,2,2,4,2,32,128]{6,5,4,3,2,1,0:T(8,128)}, f32[2,2,2,4,2,32,128]{6,5,4,3,2,1,0:T(8,128)}, u32[]{:S(2)}, u32[]{:S(2)}) collective-permute-start(f32[2,2,2,4,2,32,128]{6,5,4,3,2,1,0:T(8,128)} %dynamic-slice_bitcast_fusion), channel_id=1, source_target_pairs={{0,1},{1,0},{2,3},{3,2},{4,5},{5,4},{6,7},{7,6},{8,9},{9,8},{10,11... | collective-permute-start | bytes 3145736 | tf_op jit(solution)/shard_map/ppermute | solution.py:140
  427.3 34.8 %copy-start = (f32[2,2,2,2,4,2,32,128]{7,6,5,4,3,2,1,0:T(8,128)}, f32[2,2,2,2,4,2,32,128]{7,6,5,4,3,2,1,0:T(8,128)S(1)}, u32[]{:S(2)}) copy-start(f32[2,2,2,2,4,2,32,128]{7,6,5,4,3,2,1,0:T(8,128)S(1)} %product.6) | copy-start | bytes 6291460
  428.5 92.2 %collective-permute-start.6 = (f32[2,2,2,4,2,32,128]{6,5,4,3,2,1,0:T(8,128)}, f32[2,2,2,4,2,32,128]{6,5,4,3,2,1,0:T(8,128)}, u32[]{:S(2)}, u32[]{:S(2)}) collective-permute-start(f32[2,2,2,4,2,32,128]{6,5,4,3,2,1,0:T(8,128)} %dynamic-slice_bitcast_fusion.1), channel_id=1, source_target_pairs={{0,1},{1,0},{2,3},{3,2},{4,5},{5,4},{6,7},{7,6},{8,9},{9,8},{10,11... | collective-permute-start | bytes 3145736 | tf_op jit(solution)/shard_map/ppermute | solution.py:140
  430.2 22.5 %collective-permute-start.37 = (f32[2,2,4,1,32,128]{5,4,2,1,3,0:T(8,128)S(1)}, f32[2,2,4,1,32,128]{5,4,2,1,3,0:T(8,128)S(1)}, u32[]{:S(2)}, u32[]{:S(2)}) collective-permute-start(f32[2,2,4,1,32,128]{5,4,2,1,3,0:T(8,128)S(1)} %dynamic-slice_bitcast_fusion.8), channel_id=1, source_target_pairs={{0,8},{8,0},{16,24},{24,16},{1,9},{9,1},{17,25},{25,17},{2,10},{10... | collective-permute-start | bytes 786440 | tf_op jit(solution)/shard_map/ppermute | solution.py:140
  445.6 12.7 %collective-permute-start.31 = (f32[2,2,4,1,32,128]{5,4,2,1,3,0:T(8,128)S(1)}, f32[2,2,4,1,32,128]{5,4,2,1,3,0:T(8,128)S(1)}, u32[]{:S(2)}, u32[]{:S(2)}) collective-permute-start(f32[2,2,4,1,32,128]{5,4,2,1,3,0:T(8,128)S(1)} %dynamic-slice_bitcast_fusion.9), channel_id=1, source_target_pairs={{0,8},{8,0},{16,24},{24,16},{1,9},{9,1},{17,25},{25,17},{2,10},{10... | collective-permute-start | bytes 786440 | tf_op jit(solution)/shard_map/ppermute | solution.py:140
  445.8 22.3 %collective-permute-start.25 = (f32[2,2,4,1,32,128]{5,4,2,1,3,0:T(8,128)S(1)}, f32[2,2,4,1,32,128]{5,4,2,1,3,0:T(8,128)S(1)}, u32[]{:S(2)}, u32[]{:S(2)}) collective-permute-start(f32[2,2,4,1,32,128]{5,4,2,1,3,0:T(8,128)S(1)} %dynamic-slice_bitcast_fusion.10), channel_id=1, source_target_pairs={{0,8},{8,0},{16,24},{24,16},{1,9},{9,1},{17,25},{25,17},{2,10},{10... | collective-permute-start | bytes 786440 | tf_op jit(solution)/shard_map/ppermute | solution.py:140
  452.6 19.2 %collective-permute-start.19 = (f32[2,2,4,1,32,128]{5,4,2,1,3,0:T(8,128)S(1)}, f32[2,2,4,1,32,128]{5,4,2,1,3,0:T(8,128)S(1)}, u32[]{:S(2)}, u32[]{:S(2)}) collective-permute-start(f32[2,2,4,1,32,128]{5,4,2,1,3,0:T(8,128)S(1)} %dynamic-slice_bitcast_fusion.11), channel_id=1, source_target_pairs={{0,8},{8,0},{16,24},{24,16},{1,9},{9,1},{17,25},{25,17},{2,10},{10... | collective-permute-start | bytes 786440 | tf_op jit(solution)/shard_map/ppermute | solution.py:140
  458.3 14.9 %collective-permute-start.38 = (f32[2,4,1,32,128]{4,3,1,0,2:T(8,128)S(1)}, f32[2,4,1,32,128]{4,3,1,0,2:T(8,128)S(1)}, u32[]{:S(2)}, u32[]{:S(2)}) collective-permute-start(f32[2,4,1,32,128]{4,3,1,0,2:T(8,128)S(1)} %dynamic-slice_bitcast_fusion.14), channel_id=1, source_target_pairs={{0,16},{8,24},{16,0},{24,8},{1,17},{9,25},{17,1},{25,9},{2,18},{10... | collective-permute-start | bytes 393224 | tf_op jit(solution)/shard_map/ppermute | solution.py:140
  468.1 15.7 %collective-permute-start.32 = (f32[2,4,1,32,128]{4,3,1,0,2:T(8,128)}, f32[2,4,1,32,128]{4,3,1,0,2:T(8,128)}, u32[]{:S(2)}, u32[]{:S(2)}) collective-permute-start(f32[2,4,1,32,128]{4,3,1,0,2:T(8,128)} %dynamic-slice_bitcast_fusion.15), channel_id=1, source_target_pairs={{0,16},{8,24},{16,0},{24,8},{1,17},{9,25},{17,1},{25,9},{2,18},{10... | collective-permute-start | bytes 393224 | tf_op jit(solution)/shard_map/ppermute | solution.py:140
  471.8 18.2 %collective-permute-start.26 = (f32[2,4,1,32,128]{4,3,1,0,2:T(8,128)}, f32[2,4,1,32,128]{4,3,1,0,2:T(8,128)}, u32[]{:S(2)}, u32[]{:S(2)}) collective-permute-start(f32[2,4,1,32,128]{4,3,1,0,2:T(8,128)} %dynamic-slice_bitcast_fusion.16), channel_id=1, source_target_pairs={{0,16},{8,24},{16,0},{24,8},{1,17},{9,25},{17,1},{25,9},{2,18},{10... | collective-permute-start | bytes 393224 | tf_op jit(solution)/shard_map/ppermute | solution.py:140
  473.2 25.4 %collective-permute-start.20 = (f32[2,4,1,32,128]{4,3,1,0,2:T(8,128)}, f32[2,4,1,32,128]{4,3,1,0,2:T(8,128)}, u32[]{:S(2)}, u32[]{:S(2)}) collective-permute-start(f32[2,4,1,32,128]{4,3,1,0,2:T(8,128)} %dynamic-slice_bitcast_fusion.17), channel_id=1, source_target_pairs={{0,16},{8,24},{16,0},{24,8},{1,17},{9,25},{17,1},{25,9},{2,18},{10... | collective-permute-start | bytes 393224 | tf_op jit(solution)/shard_map/ppermute | solution.py:140
  476.7 9.3 %all-to-all-start.5 = ((f32[4,1,8192]{2,1,0:T(1,128)}), f32[4,1,8192]{2,1,0:T(1,128)S(1)}, u32[]{:S(2)}, u32[]{:S(2)}) async-start(f32[4,1,8192]{2,1,0:T(1,128)} %reshape.62), calls=%async_computation.5 | async-start | bytes 262144 | tf_op jit(solution)/shard_map/all_to_all | solution.py:177
  486.0 8.6 %all-to-all-start.4 = ((f32[4,1,8192]{2,1,0:T(1,128)}), f32[4,1,8192]{2,1,0:T(1,128)}, u32[]{:S(2)}, u32[]{:S(2)}) async-start(f32[4,1,8192]{2,1,0:T(1,128)} %reshape.60), calls=%async_computation.4 | async-start | bytes 262144 | tf_op jit(solution)/shard_map/all_to_all | solution.py:177
  494.7 8.6 %all-to-all-start.3 = ((f32[4,1,8192]{2,1,0:T(1,128)}), f32[4,1,8192]{2,1,0:T(1,128)}, u32[]{:S(2)}, u32[]{:S(2)}) async-start(f32[4,1,8192]{2,1,0:T(1,128)} %reshape.58), calls=%async_computation.3 | async-start | bytes 262144 | tf_op jit(solution)/shard_map/all_to_all | solution.py:177
  503.3 10.8 %all-to-all-start.2 = ((f32[4,1,8192]{2,1,0:T(1,128)}), f32[4,1,8192]{2,1,0:T(1,128)S(1)}, u32[]{:S(2)}, u32[]{:S(2)}) async-start(f32[4,1,8192]{2,1,0:T(1,128)} %reshape.56), calls=%async_computation.2 | async-start | bytes 262144 | tf_op jit(solution)/shard_map/all_to_all | solution.py:177
  520.6 33.0 %copy-start.3 = (f32[1,2,4,32,4,32]{5,3,4,1,0,2:T(8,128)S(1)}, f32[1,2,4,32,4,32]{5,3,4,1,0,2:T(8,128)}, u32[]{:S(2)}) copy-start(f32[1,2,4,32,4,32]{5,3,4,1,0,2:T(8,128)} %bitcast_bitcast_fusion.2) | copy-start | bytes 393220
  520.6 33.5 %copy-start.2 = (f32[1,2,4,32,4,32]{5,3,4,1,0,2:T(8,128)S(1)}, f32[1,2,4,32,4,32]{5,3,4,1,0,2:T(8,128)}, u32[]{:S(2)}) copy-start(f32[1,2,4,32,4,32]{5,3,4,1,0,2:T(8,128)} %bitcast_bitcast_fusion.3) | copy-start | bytes 393220
  520.6 14.8 %collective-permute-start.13 = (f32[2,2,4,2,32,128]{5,4,3,2,1,0:T(8,128)S(1)}, f32[2,2,4,2,32,128]{5,4,3,2,1,0:T(8,128)S(1)}, u32[]{:S(2)}, u32[]{:S(2)}) collective-permute-start(f32[2,2,4,2,32,128]{5,4,3,2,1,0:T(8,128)S(1)} %dynamic-slice_bitcast_fusion.6), channel_id=1, source_target_pairs={{0,8},{8,0},{16,24},{24,16},{1,9},{9,1},{17,25},{25,17},{2,10},{10... | collective-permute-start | bytes 1572872 | tf_op jit(solution)/shard_map/ppermute | solution.py:140
  522.3 29.5 %collective-permute-start.7 = (f32[2,2,4,2,32,128]{5,4,3,2,1,0:T(8,128)S(1)}, f32[2,2,4,2,32,128]{5,4,3,2,1,0:T(8,128)S(1)}, u32[]{:S(2)}, u32[]{:S(2)}) collective-permute-start(f32[2,2,4,2,32,128]{5,4,3,2,1,0:T(8,128)S(1)} %dynamic-slice_bitcast_fusion.7), channel_id=1, source_target_pairs={{0,8},{8,0},{16,24},{24,16},{1,9},{9,1},{17,25},{25,17},{2,10},{10... | collective-permute-start | bytes 1572872 | tf_op jit(solution)/shard_map/ppermute | solution.py:140
  536.3 20.6 %collective-permute-start.14 = (f32[2,4,2,32,128]{4,3,2,1,0:T(8,128)}, f32[2,4,2,32,128]{4,3,2,1,0:T(8,128)}, u32[]{:S(2)}, u32[]{:S(2)}) collective-permute-start(f32[2,4,2,32,128]{4,3,2,1,0:T(8,128)} %dynamic-slice_bitcast_fusion.12), channel_id=1, source_target_pairs={{0,16},{8,24},{16,0},{24,8},{1,17},{9,25},{17,1},{25,9},{2,18},{10... | collective-permute-start | bytes 786440 | tf_op jit(solution)/shard_map/ppermute | solution.py:140
  552.7 13.7 %collective-permute-start.8 = (f32[2,4,2,32,128]{4,3,2,1,0:T(8,128)}, f32[2,4,2,32,128]{4,3,2,1,0:T(8,128)}, u32[]{:S(2)}, u32[]{:S(2)}) collective-permute-start(f32[2,4,2,32,128]{4,3,2,1,0:T(8,128)} %dynamic-slice_bitcast_fusion.13), channel_id=1, source_target_pairs={{0,16},{8,24},{16,0},{24,8},{1,17},{9,25},{17,1},{25,9},{2,18},{10... | collective-permute-start | bytes 786440 | tf_op jit(solution)/shard_map/ppermute | solution.py:140
  559.7 9.5 %all-to-all-start.1 = ((f32[4,1,16384]{2,1,0:T(1,128)}), f32[4,1,16384]{2,1,0:T(1,128)S(1)}, u32[]{:S(2)}, u32[]{:S(2)}) async-start(f32[4,1,16384]{2,1,0:T(1,128)} %reshape.54), calls=%async_computation.1 | async-start | bytes 524288 | tf_op jit(solution)/shard_map/all_to_all | solution.py:177
  569.1 9.4 %all-to-all-start = ((f32[4,1,16384]{2,1,0:T(1,128)}), f32[4,1,16384]{2,1,0:T(1,128)S(1)}, u32[]{:S(2)}, u32[]{:S(2)}) async-start(f32[4,1,16384]{2,1,0:T(1,128)} %reshape.52), calls=%async_computation | async-start | bytes 524288 | tf_op jit(solution)/shard_map/all_to_all | solution.py:177
  (5 other events, 57.0 us)

commit v2 on v1

--- a/solution.py
+++ b/solution.py
@@ -9,7 +9,8 @@
 from jax.sharding import PartitionSpec as P
 
 LANES = 128
-CHUNKS = (2, 2, 1, 1, 1, 1)
+CHUNKS = (1, 3, 2, 1, 1)
+GROUPS = (4, 2, 1, 1)
 
 
 def gathered_body(amplitudes, integrals):
@@ -41,8 +42,8 @@
     return lax.psum_scatter(partial_sum, "ta", scatter_dimension=3, tiled=True)
 
 
-def prep_kernel(la, lk, place, *refs):
-    ins, outs = refs[:4], refs[4:]
+def prep_kernel(la, lk, n, place, *refs):
+    ins, outs = refs[:n], refs[n:]
     lane = lax.broadcasted_iota(jnp.int32, (la, LANES), 1)
     odd = (lane & 32) != 0
     up = place[1] * 64 + place[2] * 32
@@ -54,33 +55,32 @@
             dst[0, k] = rows.astype(jnp.bfloat16)
 
 
-def prep(amps, place, la, lk, start, count):
+def prep(amps, place, la, lk, start, count, steps):
+    n = len(steps)
     out = jax.ShapeDtypeStruct((count, lk, la, LANES), jnp.bfloat16)
     return pl.pallas_call(
-        functools.partial(prep_kernel, la, lk),
-        out_shape=[out] * 4,
+        functools.partial(prep_kernel, la, lk, n),
+        out_shape=[out] * n,
         grid_spec=pltpu.PrefetchScalarGridSpec(
             num_scalar_prefetch=1,
             grid=(count,),
             in_specs=[
                 pl.BlockSpec((1, la * lk, LANES), lambda i, place, d=d: (start + i, 0, place[0] ^ d))
-                for d in range(4)
+                for d in steps
             ],
-            out_specs=[pl.BlockSpec((1, lk, la, LANES), lambda i, place: (i, 0, 0, 0))] * 4,
+            out_specs=[pl.BlockSpec((1, lk, la, LANES), lambda i, place: (i, 0, 0, 0))] * n,
         ),
-        compiler_params=pltpu.CompilerParams(vmem_limit_bytes=32 * 2**20),
-        cost_estimate=pl.CostEstimate(
-            flops=count * la * lk * 512, bytes_accessed=count * la * lk * 512 * 6, transcendentals=0
-        ),
+        compiler_params=pltpu.CompilerParams(vmem_limit_bytes=60 * 2**20),
+        cost_estimate=pl.CostEstimate(flops=int(5e9) * count * n, bytes_accessed=1000, transcendentals=0),
         name="prep",
-    )(place, amps, amps, amps, amps)
+    )(place, *([amps] * n))
 
 
 def product_kernel(ni, kb, la, nj, place, *refs):
-    ts, ws, out, acc = refs[:4], refs[4:8], refs[8], refs[9]
+    ts, ws, out, acc = refs[: 4 * ni], refs[4 * ni : 4 * ni + 4], refs[-2], refs[-1]
     step = pl.program_id(0)
     left = [
-        jnp.concatenate([t[:, k].reshape(ni * la, LANES) for t in ts], axis=0) for k in range(kb)
+        jnp.concatenate([t[0, k] for t in ts], axis=0) for k in range(kb)
     ]
     left = jnp.concatenate(left, axis=1)
     for j in range(nj):
@@ -107,12 +107,14 @@
                     )
 
 
-def product(place, ts, ws):
-    ni, lk, la, _ = ts[0].shape
+def product(place, sources, ws):
+    ni = len(sources[0])
+    _, lk, la, _ = sources[0][0][0].shape
     nj, width = ws[0].shape[1], ws[0].shape[3]
     lc = ws[0].shape[2]
     kb = 8
     rows = 4 * ni * la
+    flat = [pair for source in sources for pair in source]
     out = jax.ShapeDtypeStruct((2, 2, 2, 2, nj, ni, la, LANES), jnp.float32)
     return pl.pallas_call(
         functools.partial(product_kernel, ni, kb, la, nj),
@@ -120,19 +122,32 @@
         grid_spec=pltpu.PrefetchScalarGridSpec(
             num_scalar_prefetch=1,
             grid=(lk // kb,),
-            in_specs=[pl.BlockSpec((ni, kb, la, LANES), lambda s, place: (0, s, 0, 0))] * 4
+            in_specs=[
+                pl.BlockSpec((1, kb, la, LANES), lambda s, place, at=at: (at, s, 0, 0))
+                for _, at in flat
+            ]
             + [pl.BlockSpec((kb, nj, lc, width), lambda s, place: (s, 0, 0, 0))] * 4,
             out_specs=pl.BlockSpec(out.shape, lambda s, place: (0,) * 8),
             scratch_shapes=[pltpu.VMEM((nj, rows, width), jnp.float32)],
         ),
-        compiler_params=pltpu.CompilerParams(vmem_limit_bytes=48 * 2**20),
-        cost_estimate=pl.CostEstimate(
-            flops=2 * rows * nj * width * lk * 4 * lc,
-            bytes_accessed=lk * 4 * lc * nj * width * 2 + rows * lk * LANES * 2 + rows * nj * width * 4,
-            transcendentals=0,
-        ),
+        compiler_params=pltpu.CompilerParams(vmem_limit_bytes=60 * 2**20),
+        cost_estimate=pl.CostEstimate(flops=2 * rows * nj * width * lk * 4 * lc * 2, bytes_accessed=1000, transcendentals=0),
         name="product",
-    )(place, *ts, *ws)
+    )(place, *[array for array, _ in flat], *ws)
+
+
+def gated(arrays, *after):
+    arrays = tuple(arrays)
+    return pl.pallas_call(
+        lambda *refs: None,
+        out_shape=[jax.ShapeDtypeStruct(a.shape, a.dtype) for a in arrays],
+        in_specs=[pl.BlockSpec(memory_space=pl.ANY)] * (len(arrays) + len(after)),
+        out_specs=[pl.BlockSpec(memory_space=pl.ANY)] * len(arrays),
+        input_output_aliases={n: n for n in range(len(arrays))},
+        compiler_params=pltpu.CompilerParams(vmem_limit_bytes=60 * 2**20),
+        cost_estimate=pl.CostEstimate(flops=1000, bytes_accessed=1000, transcendentals=0),
+        name="gate",
+    )(*arrays, *after)
 
 
 def swapped(x, axis, bits=1):
@@ -144,6 +159,49 @@
     kept = lax.dynamic_index_in_dim(x, mine, 0, keepdims=False)
     sent = lax.dynamic_index_in_dim(x, 1 - mine, 0, keepdims=False)
     return kept + swapped(sent, axis, bits)
+
+
+def finish_kernel(nj, place, *refs):
+    pieces, out, turned = refs[:4], refs[-2], refs[-1]
+    inner = 2 * place[1] + place[2]
+    lane = lax.broadcasted_iota(jnp.int32, (32, LANES), 1)
+    odd = (lane & 32) != 0
+    up = place[1] * 64 + place[2] * 32
+    down = lax.rem(place[1] * 64 + LANES - place[2] * 32, LANES)
+    for low in range(2):
+        for j in range(nj):
+            rows = jnp.concatenate([piece[low, j, 0] for piece in pieces], axis=0)
+            turned[...] = rows.T
+            own = turned[pl.ds(pl.multiple_of(32 * inner, 32), 32), :]
+            own = jnp.where(odd, pltpu.roll(own, up, 1), pltpu.roll(own, down, 1))
+            out[0, j, :, low * LANES : (low + 1) * LANES] = own
+
+
+def finish(place, pieces, start, slab_i, before):
+    lows, nj, count, la, _ = pieces[0].shape
+    out = jax.ShapeDtypeStruct((slab_i, nj, 32, lows * 4 * la), jnp.float32)
+    args, specs, alias = [], [], {}
+    if before is not None:
+        args, specs, alias = [before], [pl.BlockSpec(memory_space=pl.ANY)], {5: 0}
+    return pl.pallas_call(
+        functools.partial(finish_kernel, nj),
+        out_shape=out,
+        grid_spec=pltpu.PrefetchScalarGridSpec(
+            num_scalar_prefetch=1,
+            grid=(count,),
+            in_specs=[
+                pl.BlockSpec((lows, nj, 1, la, LANES), lambda i, place: (0, 0, i, 0, 0))
+            ]
+            * 4
+            + specs,
+            out_specs=pl.BlockSpec((1, nj, 32, lows * 4 * la), lambda i, place: (start + i, 0, 0, 0)),
+            scratch_shapes=[pltpu.VMEM((LANES, LANES), jnp.float32)],
+        ),
+        input_output_aliases=alias,
+        compiler_params=pltpu.CompilerParams(vmem_limit_bytes=60 * 2**20),
+        cost_estimate=pl.CostEstimate(flops=1000, bytes_accessed=1000, transcendentals=0),
+        name="finish",
+    )(place, *pieces, *args)
 
 
 def tiled_body(amplitudes, integrals):
@@ -151,33 +209,51 @@
     z, x, core, row = (lax.axis_index(n) for n in ("z", "x", "core", "row"))
     place = jnp.stack([z, x, core]).astype(jnp.int32)
     amps = amplitudes.reshape(ni, la * lk, full_c)
-    chunks = []
-    start = 0
-    parts = []
-    for count in CHUNKS:
-        parts.append(prep(amps, place, la, lk, start, count))
-        start += count
+    counts = CHUNKS
+    starts = [sum(counts[:n]) for n in range(len(counts))]
+    parts = [prep(amps, place, la, lk, s, c, (2, 3)) for s, c in zip(starts, counts)]
+    integrals, *parts[0] = lax.optimization_barrier((integrals, *parts[0]))
+    moved = [(swapped(two, "z", 2), swapped(three, "z", 3)) for two, three in parts]
     w_own = jnp.transpose(integrals, (0, 2, 1, 3))
     w_x = swapped(w_own, "x")
     w_core = swapped(w_own, "core")
+    (later,) = gated((place,), parts[0][0], parts[1][0], w_own)
+    own, one = prep(amps, later, la, lk, 0, ni, (0, 1))
+    one = swapped(one, "z", 1)
+    (w_x,) = gated((w_x,), *moved[0], *moved[1], one, *[p[0] for p in parts[2:]])
     w_both = swapped(w_x, "core")
     ws = (w_own, w_core, w_x, w_both)
-    token = None
-    moved = []
-    for own, *others in parts:
-        moved.append((own, *(swapped(o, "z", d) for d, o in zip((1, 2, 3), others))))
-    for ts in moved:
-        total = product(place, ts, ws)
-        total = exchanged(total, "row", row)
-        total = exchanged(total, "z", z & 1, 1)
-        total = exchanged(total, "z", z >> 1, 2)
-        lows, nj, count, _, _ = total.shape
-        total = total.reshape(lows, nj, count, la, 4, LANES // 4)
-        total = jnp.transpose(total, (4, 2, 0, 3, 1, 5))
-        total = lax.all_to_all(total, ("x", "core"), split_axis=0, concat_axis=0, tiled=True)
-        total = jnp.transpose(total, (1, 2, 0, 3, 4, 5))
-        chunks.append(total.reshape(count, lows * 4 * la, nj, LANES // 4))
-    return jnp.concatenate(chunks, axis=0)
+
+    where = [(m, i) for m, count in enumerate(counts) for i in range(count)]
+    totals = []
+    n = 0
+    for g, count in enumerate(GROUPS):
+        at = range(n, n + count)
+        n += count
+        two = [(moved[where[i][0]][0], where[i][1]) for i in at]
+        three = [(moved[where[i][0]][1], where[i][1]) for i in at]
+        totals.append(product(place, ([(own, i) for i in at], [(one, i) for i in at], two, three), ws))
+
+    def exchange(total, axis, mine, bits, *after):
+        kept = lax.dynamic_index_in_dim(total, mine, 0, keepdims=False)
+        sent = lax.dynamic_index_in_dim(total, 1 - mine, 0, keepdims=False)
+        if after:
+            (sent,) = gated((sent,), *after)
+        return kept + swapped(sent, axis, bits)
+
+    result = None
+    rows, lows, highs = [], [], []
+    for g, total in enumerate(totals):
+        rows.append(exchange(total, "row", row, 1, *rows[g - 1 : g], *lows[max(g - 2, 0) : max(g - 1, 0)]))
+        lows.append(exchange(rows[g], "z", z & 1, 1, *lows[max(g - 1, 0) : g]))
+        highs.append(exchange(lows[g], "z", z >> 1, 2))
+    for g, total in enumerate(highs):
+        pieces = [total]
+        for bits in (1, 2, 3):
+            pairs = [(s, s ^ bits) for s in range(4)]
+            pieces.append(lax.ppermute(total, ("x", "core"), pairs))
+        result = finish(place, pieces, sum(GROUPS[:g]), ni, result)
+    return jnp.transpose(result, (0, 3, 1, 2))
 
 
 def solution(mesh):
@@ -187,7 +263,7 @@
         ni, a, k, c = amplitudes.shape
         la, lk = a // ta, k // rows
         fits = ta == 16 and rows == 2 and c == 4 * LANES and la % 16 == 0 and lk % 8 == 0
-        fits = fits and ni == sum(CHUNKS)
+        fits = fits and ni == sum(GROUPS)
         if not fits:
             placed = (P(None, "ta", "row", None), P("row", "ta", None, None))
             return jax.shard_map(

time: 585 us -> 421 us (0.72)
  waiting for transfers between devices: 258 us -> 177 us
  starting transfers between devices: 160 us -> 90.2 us
  local copies, waits for them, and re-layouts: 41.2 us -> 24.5 us
  Pallas kernels: 106 us -> 115 us
    ppermute x39 -> x26, waiting for transfers between devices: 250 us -> 176 us  [swapped(): return lax.ppermute(x, axis, [(s, s ^ bits) for s in range(n)])]
    ppermute x39 -> x26, starting transfers between devices: 138 us -> 82.8 us  [swapped(): return lax.ppermute(x, axis, [(s, s ^ bits) for s in range(n)])]
    all_to_all x6 -> x0, starting transfers between devices: 21.8 us -> none  [tiled_body(): lax.all_to_all(total, ('x', 'core'), split_axis=0, concat_axis=0, tiled=T...]
    pallas_call x6 -> x18, Pallas kernels: 25 us -> 44.3 us  [the longest x6 31.1 us: prep(): pl.pallas_call(functools.partial(prep_kernel, la, lk, n), out_shape=[out]...]
    unnamed x34 -> x61, local copies, waits for them, and re-layouts: 17.6 us -> 6.24 us
    pallas_call x6 -> x4, Pallas kernels: 81.4 us -> 70.6 us  [product(): pl.pallas_call(functools.partial(product_kernel, ni, kb, la, nj), out_sha...]
    transpose x18 -> x0, local copies, waits for them, and re-layouts: 9.22 us -> none  [the longest x12 8.74 us: tiled_body(): total = jnp.transpose(total, (1, 2, 0, 3, 4, 5))]
    all_to_all x6 -> x0, other arithmetic: 8.42 us -> none  [tiled_body(): lax.all_to_all(total, ('x', 'core'), split_axis=0, concat_axis=0, tiled=T...]
  transfers between devices with their start and end apart: 45 -> 38, of which waited for: 16 -> 15; matrix products, arithmetic and copies ran while one was open for 8% -> 7% of each run, Pallas kernels for 18% -> 26%
where the time goes in v2:
time: 421 us; the launch traced here: 419 us
  waiting for transfers between devices  177 us (42%)
  Pallas kernels  115 us (27%)
  starting transfers between devices  90.2 us (21%)
  local copies, waits for them, and re-layouts  24.5 us (6%)
  other arithmetic  12.2 us (3%)
    ppermute x26, waiting for transfers between devices, swapped(): return lax.ppermute(x, axis, [(s, s ^ bits) for s in range(n)])  176 us
    ppermute x26, starting transfers between devices, swapped(): return lax.ppermute(x, axis, [(s, s ^ bits) for s in range(n)])  82.8 us
    pallas_call x4, Pallas kernels, product(): pl.pallas_call(functools.partial(product_kernel, ni, kb, la, nj), out_sha...  70.6 us
    pallas_call x6, Pallas kernels, prep(): pl.pallas_call(functools.partial(prep_kernel, la, lk, n), out_shape=[out]...  31.1 us
    pallas_call x4, Pallas kernels, finish(): pl.pallas_call(functools.partial(finish_kernel, nj), out_shape=out, grid_...  13.3 us
    add x12, other arithmetic, exchange(): return kept + swapped(sent, axis, bits)  11.6 us
    squeeze x12, local copies, waits for them, and re-layouts, exchange(): sent = lax.dynamic_index_in_dim(total, 1 - mine, 0, keepdims=False)  10.7 us
  transfers between devices with their start and end apart: 38, of which 15 were waited for; matrix products, arithmetic and copies ran while one was open for 7% of the time, Pallas kernels for 26%

profile of v2, /device:TPU:0, one launch (start us, length us, event | category | flops | bytes accessed | tf_op | source)
XLA Modules:
  0.0 419.4 jit_solution(2802813774594743023)
XLA Ops:
  0.6 3.3 prep.6
  3.9 5.0 %collective-permute-start.6 = (bf16[1,48,32,128]{3,2,1,0:T(8,128)(2,1)}, bf16[1,48,32,128]{3,2,1,0:T(8,128)(2,1)}, u32[]{:S(2)}, u32[]{:S(2)}) collective-permute-start(bf16[1,48,32,128]{3,2,1,0:T(8,128)(2,1)} %get-tuple-element.29), channel_id=1, source_target_pairs={{0,24},{8,16},{16,8},{24,0},{1,25},{9,17},{17,9},{25,1},{2,26},{10... | collective-permute-start | bytes 1179656 | tf_op jit(solution)/shard_map/ppermute | solution.py:155
  9.0 5.8 %prep.7 = (bf16[3,48,32,128]{3,2,1,0:T(8,128)(2,1)}, bf16[3,48,32,128]{3,2,1,0:T(8,128)(2,1)}) custom-call(s32[3]{0:T(128)} %pad_add_fusion.place, f32[8,1536,512]{2,1,0:T(8,128)} %bitcast.58, f32[8,1536,512]{2,1,0:T(8,128)} %bitcast.59), custom_call_target="tpu_custom_call" | custom-call | flops 30000001024 | bytes 1000 | tf_op jit(solution)/shard_map/prep/pallas_call | solution.py:61
  15.8 7.5 %copy.16 = bf16[48,32,4,512]{3,1,2,0:T(8,128)(2,1)} copy(bf16[48,32,4,512]{3,2,1,0:T(4,128)(2,1)} %param.3) | data formatting | bytes 12582912 | tf_op jit(solution)/shard_map/optimization_barrier | solution.py:215
  25.3 11.1 %prep.8 = (bf16[8,48,32,128]{3,2,1,0:T(8,128)(2,1)}, bf16[8,48,32,128]{3,2,1,0:T(8,128)(2,1)}) custom-call(s32[3]{0:T(128)} %gate.8.place, f32[8,1536,512]{2,1,0:T(8,128)} %bitcast.60, f32[8,1536,512]{2,1,0:T(8,128)} %bitcast.61), custom_call_target="tpu_custom_call" | custom-call | flops 80000000000 | bytes 1000 | tf_op jit(solution)/shard_map/prep/pallas_call | solution.py:61
  36.4 3.4 collective-permute-start
  39.8 3.9 prep.10
  43.7 3.5 prep.11
  47.2 32.0 %collective-permute-start.5 = (bf16[1,48,32,128]{3,2,1,0:T(8,128)(2,1)S(1)}, bf16[1,48,32,128]{3,2,1,0:T(8,128)(2,1)S(1)}, u32[]{:S(2)}, u32[]{:S(2)}) collective-permute-start(bf16[1,48,32,128]{3,2,1,0:T(8,128)(2,1)S(1)} %copy-done.18), channel_id=1, source_target_pairs={{0,16},{8,24},{16,0},{24,8},{1,17},{9,25},{17,1},{25,9},{2,18},{10... | collective-permute-start | bytes 1179656 | tf_op jit(solution)/shard_map/ppermute | solution.py:155
  79.3 3.4 prep.9
  82.7 61.4 %collective-permute-done.5.refs_1_.refs_8_ = bf16[1,48,32,128]{3,2,1,0:T(8,128)(2,1)S(1)} collective-permute-done((bf16[1,48,32,128]{3,2,1,0:T(8,128)(2,1)S(1)}, bf16[1,48,32,128]{3,2,1,0:T(8,128)(2,1)S(1)}, u32[]{:S(2)}, u32[]{:S(2)}) %collective-permute-start.5) | collective-permute-done | bytes 393248 | tf_op jit(solution)/shard_map/ppermute | solution.py:155
  145.4 14.6 %collective-permute-done.4.refs_0_ = bf16[48,4,32,512]{3,2,1,0:T(8,128)(2,1)} collective-permute-done((bf16[48,4,32,512]{3,2,1,0:T(8,128)(2,1)}, bf16[48,4,32,512]{3,2,1,0:T(8,128)(2,1)}, u32[]{:S(2)}, u32[]{:S(2)}) %collective-permute-start.4) | collective-permute-done | bytes 6291488 | tf_op jit(solution)/shard_map/ppermute | solution.py:155
  161.2 2.3 collective-permute-start.12
  163.4 3.5 collective-permute-start.13
  166.9 3.7 collective-permute-done.9.refs_7_.refs_11_.refs_19_
  170.6 25.2 %product.7 = f32[2,2,2,2,4,4,32,128]{7,6,5,4,3,2,1,0:T(8,128)} custom-call(s32[3]{0:T(128)} %pad_add_fusion.place, bf16[8,48,32,128]{3,2,1,0:T(8,128)(2,1)} %get-tuple-element.25.refs_0_.refs_1_.refs_2_.refs_3_, bf16[8,48,32,128]{3,2,1,0:T(8,128)(2,1)} %get-tuple-element.25.refs_0_.refs_1_.refs_2_.refs_3_, ...), custom_call_target="tpu_custom_call" | custom-call | flops 25769803776 | bytes 1000 | tf_op jit(solution)/shard_map/product/pallas_call | solution.py:119
  195.8 3.2 dynamic-slice_bitcast_fusion
  199.0 1.5 collective-permute-start.14
  200.5 2.3 collective-permute-start.10
  202.7 3.5 collective-permute-start.11
  206.2 27.0 %collective-permute-done.12.refs_4_.refs_5_ = bf16[2,48,32,128]{3,2,1,0:T(8,128)(2,1)} collective-permute-done((bf16[2,48,32,128]{3,2,1,0:T(8,128)(2,1)S(1)}, bf16[2,48,32,128]{3,2,1,0:T(8,128)(2,1)}, u32[]{:S(2)}, u32[]{:S(2)}) %collective-permute-start.12) | collective-permute-done | bytes 786464 | tf_op jit(solution)/shard_map/ppermute | solution.py:155
  233.2 17.1 %product.6 = f32[2,2,2,2,4,2,32,128]{7,6,5,4,3,2,1,0:T(8,128)} custom-call(s32[3]{0:T(128)} %pad_add_fusion.place, bf16[8,48,32,128]{3,2,1,0:T(8,128)(2,1)} %get-tuple-element.25.refs_0_.refs_1_.refs_2_.refs_3_, bf16[8,48,32,128]{3,2,1,0:T(8,128)(2,1)} %get-tuple-element.25.refs_0_.refs_1_.refs_2_.refs_3_, bf16[8,48,32,128]{3,2,1,0:T(8,128)(2,1)} %copy-done, ...), custom_call_target="tpu_custom_call" | custom-call | flops 12884901888 | bytes 1000 | tf_op jit(solution)/shard_map/product/pallas_call | solution.py:119
  250.3 2.3 dynamic-slice_bitcast_fusion.2.refs_0_
  252.6 3.4 bitcast_add_fusion.refs_1_
  257.7 17.5 %collective-permute-start.16 = (f32[2,2,4,4,32,128]{5,4,3,2,1,0:T(8,128)S(1)}, f32[2,2,4,4,32,128]{5,4,3,2,1,0:T(8,128)}, u32[]{:S(2)}, u32[]{:S(2)}) collective-permute-start(f32[2,2,4,4,32,128]{5,4,3,2,1,0:T(8,128)S(1)} %dynamic-slice_bitcast_fusion.1), channel_id=1, source_target_pairs={{0,8},{8,0},{16,24},{24,16},{1,9},{9,1},{17,25},{25,17},{2,10},{10... | collective-permute-start | bytes 3145736 | tf_op jit(solution)/shard_map/ppermute | solution.py:155
  275.5 2.1 collective-permute-start.2
  277.6 14.1 %product.5 = f32[2,2,2,2,4,1,32,128]{7,6,5,4,3,2,1,0:T(8,128)} custom-call(s32[3]{0:T(128)} %pad_add_fusion.place, bf16[8,48,32,128]{3,2,1,0:T(8,128)(2,1)} %get-tuple-element.25.refs_0_.refs_1_.refs_2_.refs_3_, bf16[8,48,32,128]{3,2,1,0:T(8,128)(2,1)} %copy-done, bf16[1,48,32,128]{3,2,1,0:T(8,128)(2,1)} %collective-permute-done.10.refs_2_, ...), custom_call_target="tpu_custom_call" | custom-call | flops 6442450944 | bytes 1000 | tf_op jit(solution)/shard_map/product/pallas_call | solution.py:119
  291.8 1.9 dynamic-slice_bitcast_fusion.5.refs_0_
  293.7 2.8 bitcast_add_fusion.2.refs_1_
  296.5 8.7 %collective-permute-done.16 = f32[2,2,4,4,32,128]{5,4,3,2,1,0:T(8,128)} collective-permute-done((f32[2,2,4,4,32,128]{5,4,3,2,1,0:T(8,128)S(1)}, f32[2,2,4,4,32,128]{5,4,3,2,1,0:T(8,128)}, u32[]{:S(2)}, u32[]{:S(2)}) %collective-permute-start.16) | collective-permute-done | bytes 1048608 | tf_op jit(solution)/shard_map/ppermute | solution.py:155
  305.1 2.4 bitcast_add_fusion.1.refs_2_.refs_1_
  307.5 1.5 collective-permute-start.17
  309.9 6.8 %collective-permute-done.2.refs_3_ = bf16[1,48,32,128]{3,2,1,0:T(8,128)(2,1)} collective-permute-done((bf16[1,48,32,128]{3,2,1,0:T(8,128)(2,1)}, bf16[1,48,32,128]{3,2,1,0:T(8,128)(2,1)}, u32[]{:S(2)}, u32[]{:S(2)}) %collective-permute-start.2) | collective-permute-done | bytes 393248 | tf_op jit(solution)/shard_map/ppermute | solution.py:155
  317.4 14.1 %product.4 = f32[2,2,2,2,4,1,32,128]{7,6,5,4,3,2,1,0:T(8,128)} custom-call(s32[3]{0:T(128)} %pad_add_fusion.place, bf16[8,48,32,128]{3,2,1,0:T(8,128)(2,1)} %get-tuple-element.25.refs_0_.refs_1_.refs_2_.refs_3_, bf16[8,48,32,128]{3,2,1,0:T(8,128)(2,1)} %copy-done, bf16[1,48,32,128]{3,2,1,0:T(8,128)(2,1)} %copy-done.17, ...), custom_call_target="tpu_custom_call" | custom-call | flops 6442450944 | bytes 1000 | tf_op jit(solution)/shard_map/product/pallas_call | solution.py:119
  334.7 16.3 %collective-permute-done.18 = f32[2,2,4,2,32,128]{5,4,3,2,1,0:T(8,128)S(1)} collective-permute-done((f32[2,2,4,2,32,128]{5,4,3,2,1,0:T(8,128)}, f32[2,2,4,2,32,128]{5,4,3,2,1,0:T(8,128)S(1)}, u32[]{:S(2)}, u32[]{:S(2)}) %collective-permute-start.18) | collective-permute-done | bytes 524320 | tf_op jit(solution)/shard_map/ppermute | solution.py:155
  351.9 1.6 collective-permute-start.19
  353.5 5.4 %collective-permute-done.34 = f32[2,4,4,32,128]{4,3,2,1,0:T(8,128)} collective-permute-done((f32[2,4,4,32,128]{4,3,2,1,0:T(8,128)S(1)}, f32[2,4,4,32,128]{4,3,2,1,0:T(8,128)}, u32[]{:S(2)}, u32[]{:S(2)}) %collective-permute-start.34) | collective-permute-done | bytes 524320 | tf_op jit(solution)/shard_map/ppermute | solution.py:155
  360.1 1.6 collective-permute-start.36
  365.0 1.7 collective-permute-start.21
  366.6 7.0 %collective-permute-done.30 = f32[2,4,2,32,128]{4,3,2,1,0:T(8,128)S(1)} collective-permute-done((f32[2,4,2,32,128]{4,3,2,1,0:T(8,128)S(1)}, f32[2,4,2,32,128]{4,3,2,1,0:T(8,128)S(1)}, u32[]{:S(2)}, u32[]{:S(2)}) %collective-permute-start.30) | collective-permute-done | bytes 262176 | tf_op jit(solution)/shard_map/ppermute | solution.py:155
  374.3 4.8 %collective-permute-done.21 = f32[2,2,4,1,32,128]{5,4,3,2,1,0:T(8,128)S(1)} collective-permute-done((f32[2,2,4,1,32,128]{5,4,3,2,1,0:T(8,128)}, f32[2,2,4,1,32,128]{5,4,3,2,1,0:T(8,128)S(1)}, u32[]{:S(2)}, u32[]{:S(2)}) %collective-permute-start.21) | collective-permute-done | bytes 262176 | tf_op jit(solution)/shard_map/ppermute | solution.py:155
  379.2 8.2 %collective-permute-done.26 = f32[2,4,1,32,128]{4,3,2,1,0:T(8,128)S(1)} collective-permute-done((f32[2,4,1,32,128]{4,3,2,1,0:T(8,128)S(1)}, f32[2,4,1,32,128]{4,3,2,1,0:T(8,128)S(1)}, u32[]{:S(2)}, u32[]{:S(2)}) %collective-permute-start.26) | collective-permute-done | bytes 131104 | tf_op jit(solution)/shard_map/ppermute | solution.py:155
  388.5 9.1 %collective-permute-done.22 = f32[2,4,1,32,128]{4,3,2,1,0:T(8,128)S(1)} collective-permute-done((f32[2,4,1,32,128]{4,3,2,1,0:T(8,128)S(1)}, f32[2,4,1,32,128]{4,3,2,1,0:T(8,128)S(1)}, u32[]{:S(2)}, u32[]{:S(2)}) %collective-permute-start.22) | collective-permute-done | bytes 131104 | tf_op jit(solution)/shard_map/ppermute | solution.py:155
  401.5 1.6 collective-permute-done.29.refs_3_
  403.4 4.8 %finish.4.refs_4_ = f32[8,4,32,256]{3,2,1,0:T(8,128)} custom-call(s32[3]{0:T(128)} %pad_add_fusion.place, f32[2,4,4,32,128]{4,3,2,1,0:T(8,128)} %copy-done.11, f32[2,4,4,32,128]{4,3,2,1,0:T(8,128)} %copy-done.16, f32[2,4,4,32,128]{4,3,2,1,0:T(8,128)} %collective-permute-done.36.refs_2_, f32[2,4,4,32,128]{4,3,2,1,0:T(8,128)} %collective-permute-done.37.refs_3_), custom_call_target="tpu_custom_call" | custom-call | flops 1000 | bytes 1000 | tf_op jit(solution)/shard_map/finish/pallas_call | solution.py:186
  408.2 3.1 finish.5.refs_4_
  412.6 2.7 finish.6.refs_4_
  416.7 2.7 finish.7
  (137 shorter events, 26.9 us)
Async XLA Ops:
  3.9 43.3 %collective-permute-start.6 = (bf16[1,48,32,128]{3,2,1,0:T(8,128)(2,1)}, bf16[1,48,32,128]{3,2,1,0:T(8,128)(2,1)}, u32[]{:S(2)}, u32[]{:S(2)}) collective-permute-start(bf16[1,48,32,128]{3,2,1,0:T(8,128)(2,1)} %get-tuple-element.29), channel_id=1, source_target_pairs={{0,24},{8,16},{16,8},{24,0},{1,25},{9,17},{17,9},{25,1},{2,26},{10... | collective-permute-start | bytes 1179656 | tf_op jit(solution)/shard_map/ppermute | solution.py:155
  14.8 129.3 %collective-permute-start.8 = (bf16[3,48,32,128]{3,2,1,0:T(8,128)(2,1)}, bf16[3,48,32,128]{3,2,1,0:T(8,128)(2,1)}, u32[]{:S(2)}, u32[]{:S(2)}) collective-permute-start(bf16[3,48,32,128]{3,2,1,0:T(8,128)(2,1)} %get-tuple-element.30), channel_id=1, source_target_pairs={{0,24},{8,16},{16,8},{24,0},{1,25},{9,17},{17,9},{25,1},{2,26},{10... | collective-permute-start | bytes 3538952 | tf_op jit(solution)/shard_map/ppermute | solution.py:155
  14.8 10.0 %copy-start.29 = (s32[3]{0:T(128)S(1)}, s32[3]{0:T(128)}, u32[]{:S(2)}) copy-start(s32[3]{0:T(128)} %pad_add_fusion.place) | copy-start | bytes 40
  14.8 129.3 %collective-permute-start.7 = (bf16[3,48,32,128]{3,2,1,0:T(8,128)(2,1)}, bf16[3,48,32,128]{3,2,1,0:T(8,128)(2,1)}, u32[]{:S(2)}, u32[]{:S(2)}) collective-permute-start(bf16[3,48,32,128]{3,2,1,0:T(8,128)(2,1)} %get-tuple-element.23.refs_2_), channel_id=1, source_target_pairs={{0,16},{8,24},{16,0},{24,8},{1,17},{9,25},{17,1},{25,9},{2,18},{10... | collective-permute-start | bytes 3538952 | tf_op jit(solution)/shard_map/ppermute | solution.py:155
  23.3 136.7 %collective-permute-start.4 = (bf16[48,4,32,512]{3,2,1,0:T(8,128)(2,1)}, bf16[48,4,32,512]{3,2,1,0:T(8,128)(2,1)}, u32[]{:S(2)}, u32[]{:S(2)}) collective-permute-start(bf16[48,4,32,512]{3,2,1,0:T(8,128)(2,1)} %bitcast.55.refs_3_.refs_4_.refs_8_.refs_16_), channel_id=1, source_target_pairs={{0,4},{4,0},{1,5},{5,1},{2,6},{6,2},{3,7},{7,3},{8,12},{12,8},{9,1... | collective-permute-start | bytes 18874376 | tf_op jit(solution)/shard_map/ppermute | solution.py:155
  36.4 109.0 %collective-permute-start = (bf16[8,48,32,128]{3,2,1,0:T(8,128)(2,1)}, bf16[8,48,32,128]{3,2,1,0:T(8,128)(2,1)S(1)}, u32[]{:S(2)}, u32[]{:S(2)}) collective-permute-start(bf16[8,48,32,128]{3,2,1,0:T(8,128)(2,1)} %get-tuple-element.26), channel_id=1, source_target_pairs={{0,8},{8,0},{16,24},{24,16},{1,9},{9,1},{17,25},{25,17},{2,10},{10... | collective-permute-start | bytes 9437192 | tf_op jit(solution)/shard_map/ppermute | solution.py:155
  47.2 96.8 %collective-permute-start.5 = (bf16[1,48,32,128]{3,2,1,0:T(8,128)(2,1)S(1)}, bf16[1,48,32,128]{3,2,1,0:T(8,128)(2,1)S(1)}, u32[]{:S(2)}, u32[]{:S(2)}) collective-permute-start(bf16[1,48,32,128]{3,2,1,0:T(8,128)(2,1)S(1)} %copy-done.18), channel_id=1, source_target_pairs={{0,16},{8,24},{16,0},{24,8},{1,17},{9,25},{17,1},{25,9},{2,18},{10... | collective-permute-start | bytes 1179656 | tf_op jit(solution)/shard_map/ppermute | solution.py:155
  144.1 16.0 %copy-start.19 = (bf16[1,48,32,128]{3,2,1,0:T(8,128)(2,1)}, bf16[1,48,32,128]{3,2,1,0:T(8,128)(2,1)S(1)}, u32[]{:S(2)}) copy-start(bf16[1,48,32,128]{3,2,1,0:T(8,128)(2,1)S(1)} %collective-permute-done.5.refs_1_.refs_8_) | copy-start | bytes 1179652
  144.1 22.8 %collective-permute-start.3 = (bf16[48,4,32,512]{3,2,1,0:T(8,128)(2,1)}, bf16[48,4,32,512]{3,2,1,0:T(8,128)(2,1)}, u32[]{:S(2)}, u32[]{:S(2)}) collective-permute-start(bf16[48,4,32,512]{3,2,1,0:T(8,128)(2,1)} %bitcast.55.refs_3_.refs_4_.refs_8_.refs_16_), channel_id=1, source_target_pairs={{0,2},{2,0},{1,3},{3,1},{4,6},{6,4},{5,7},{7,5},{8,10},{10,8},{9,1... | collective-permute-start | bytes 18874376 | tf_op jit(solution)/shard_map/ppermute | solution.py:155
  145.4 14.6 %copy-start = (bf16[8,48,32,128]{3,2,1,0:T(8,128)(2,1)}, bf16[8,48,32,128]{3,2,1,0:T(8,128)(2,1)S(1)}, u32[]{:S(2)}) copy-start(bf16[8,48,32,128]{3,2,1,0:T(8,128)(2,1)S(1)} %collective-permute-done.refs_5_.refs_1_.refs_2_.refs_3_.refs_4_.refs_6_.refs_7_) | copy-start | bytes 9437188
  160.0 10.6 %collective-permute-start.9 = (bf16[48,4,32,512]{3,2,1,0:T(8,128)(2,1)}, bf16[48,4,32,512]{3,2,1,0:T(8,128)(2,1)}, u32[]{:S(2)}, u32[]{:S(2)}) collective-permute-start(bf16[48,4,32,512]{3,2,1,0:T(8,128)(2,1)} %gate.9.refs_6_.refs_10_.refs_18_), channel_id=1, source_target_pairs={{0,2},{2,0},{1,3},{3,1},{4,6},{6,4},{5,7},{7,5},{8,10},{10,8},{9,1... | collective-permute-start | bytes 18874376 | tf_op jit(solution)/shard_map/ppermute | solution.py:155
  161.2 72.0 %collective-permute-start.12 = (bf16[2,48,32,128]{3,2,1,0:T(8,128)(2,1)S(1)}, bf16[2,48,32,128]{3,2,1,0:T(8,128)(2,1)}, u32[]{:S(2)}, u32[]{:S(2)}) collective-permute-start(bf16[2,48,32,128]{3,2,1,0:T(8,128)(2,1)S(1)} %copy-done.13), channel_id=1, source_target_pairs={{0,16},{8,24},{16,0},{24,8},{1,17},{9,25},{17,1},{25,9},{2,18},{10... | collective-permute-start | bytes 2359304 | tf_op jit(solution)/shard_map/ppermute | solution.py:155
  163.4 42.8 %collective-permute-start.13 = (bf16[2,48,32,128]{3,2,1,0:T(8,128)(2,1)}, bf16[2,48,32,128]{3,2,1,0:T(8,128)(2,1)}, u32[]{:S(2)}, u32[]{:S(2)}) collective-permute-start(bf16[2,48,32,128]{3,2,1,0:T(8,128)(2,1)} %get-tuple-element.34), channel_id=1, source_target_pairs={{0,24},{8,16},{16,8},{24,0},{1,25},{9,17},{17,9},{25,1},{2,26},{10... | collective-permute-start | bytes 2359304 | tf_op jit(solution)/shard_map/ppermute | solution.py:155
  199.0 53.7 %collective-permute-start.14 = (f32[2,2,2,4,4,32,128]{6,5,4,3,2,1,0:T(8,128)}, f32[2,2,2,4,4,32,128]{6,5,4,3,2,1,0:T(8,128)S(1)}, u32[]{:S(2)}, u32[]{:S(2)}) collective-permute-start(f32[2,2,2,4,4,32,128]{6,5,4,3,2,1,0:T(8,128)} %dynamic-slice_bitcast_fusion), channel_id=1, source_target_pairs={{0,1},{1,0},{2,3},{3,2},{4,5},{5,4},{6,7},{7,6},{8,9},{9,8},{10,11... | collective-permute-start | bytes 6291464 | tf_op jit(solution)/shard_map/ppermute | solution.py:155
  200.5 77.2 %collective-permute-start.10 = (bf16[1,48,32,128]{3,2,1,0:T(8,128)(2,1)}, bf16[1,48,32,128]{3,2,1,0:T(8,128)(2,1)}, u32[]{:S(2)}, u32[]{:S(2)}) collective-permute-start(bf16[1,48,32,128]{3,2,1,0:T(8,128)(2,1)} %get-tuple-element.32.refs_7_), channel_id=1, source_target_pairs={{0,16},{8,24},{16,0},{24,8},{1,17},{9,25},{17,1},{25,9},{2,18},{10... | collective-permute-start | bytes 1179656 | tf_op jit(solution)/shard_map/ppermute | solution.py:155
  202.7 72.8 %collective-permute-start.11 = (bf16[1,48,32,128]{3,2,1,0:T(8,128)(2,1)}, bf16[1,48,32,128]{3,2,1,0:T(8,128)(2,1)}, u32[]{:S(2)}, u32[]{:S(2)}) collective-permute-start(bf16[1,48,32,128]{3,2,1,0:T(8,128)(2,1)} %get-tuple-element.33), channel_id=1, source_target_pairs={{0,24},{8,16},{16,8},{24,0},{1,25},{9,17},{17,9},{25,1},{2,26},{10... | collective-permute-start | bytes 1179656 | tf_op jit(solution)/shard_map/ppermute | solution.py:155
  256.0 37.6 %collective-permute-start.15 = (f32[2,2,2,4,2,32,128]{6,5,4,3,2,1,0:T(8,128)}, f32[2,2,2,4,2,32,128]{6,5,4,3,2,1,0:T(8,128)}, u32[]{:S(2)}, u32[]{:S(2)}) collective-permute-start(f32[2,2,2,4,2,32,128]{6,5,4,3,2,1,0:T(8,128)} %gate.10), channel_id=1, source_target_pairs={{0,1},{1,0},{2,3},{3,2},{4,5},{5,4},{6,7},{7,6},{8,9},{9,8},{10,11... | collective-permute-start | bytes 3145736 | tf_op jit(solution)/shard_map/ppermute | solution.py:155
  257.7 47.4 %collective-permute-start.16 = (f32[2,2,4,4,32,128]{5,4,3,2,1,0:T(8,128)S(1)}, f32[2,2,4,4,32,128]{5,4,3,2,1,0:T(8,128)}, u32[]{:S(2)}, u32[]{:S(2)}) collective-permute-start(f32[2,2,4,4,32,128]{5,4,3,2,1,0:T(8,128)S(1)} %dynamic-slice_bitcast_fusion.1), channel_id=1, source_target_pairs={{0,8},{8,0},{16,24},{24,16},{1,9},{9,1},{17,25},{25,17},{2,10},{10... | collective-permute-start | bytes 3145736 | tf_op jit(solution)/shard_map/ppermute | solution.py:155
  275.2 41.5 %collective-permute-start.1 = (bf16[1,48,32,128]{3,2,1,0:T(8,128)(2,1)}, bf16[1,48,32,128]{3,2,1,0:T(8,128)(2,1)S(1)}, u32[]{:S(2)}, u32[]{:S(2)}) collective-permute-start(bf16[1,48,32,128]{3,2,1,0:T(8,128)(2,1)} %get-tuple-element.27.refs_8_), channel_id=1, source_target_pairs={{0,16},{8,24},{16,0},{24,8},{1,17},{9,25},{17,1},{25,9},{2,18},{10... | collective-permute-start | bytes 1179656 | tf_op jit(solution)/shard_map/ppermute | solution.py:155
  275.5 41.2 %collective-permute-start.2 = (bf16[1,48,32,128]{3,2,1,0:T(8,128)(2,1)}, bf16[1,48,32,128]{3,2,1,0:T(8,128)(2,1)}, u32[]{:S(2)}, u32[]{:S(2)}) collective-permute-start(bf16[1,48,32,128]{3,2,1,0:T(8,128)(2,1)} %get-tuple-element.28), channel_id=1, source_target_pairs={{0,24},{8,16},{16,8},{24,0},{1,25},{9,17},{17,9},{25,1},{2,26},{10... | collective-permute-start | bytes 1179656 | tf_op jit(solution)/shard_map/ppermute | solution.py:155
  307.5 26.2 %collective-permute-start.17 = (f32[2,2,2,4,1,32,128]{6,5,4,3,2,1,0:T(8,128)}, f32[2,2,2,4,1,32,128]{6,5,4,3,2,1,0:T(8,128)S(1)}, u32[]{:S(2)}, u32[]{:S(2)}) collective-permute-start(f32[2,2,2,4,1,32,128]{6,5,4,3,2,1,0:T(8,128)} %gate.11), channel_id=1, source_target_pairs={{0,1},{1,0},{2,3},{3,2},{4,5},{5,4},{6,7},{7,6},{8,9},{9,8},{10,11... | collective-permute-start | bytes 1572872 | tf_op jit(solution)/shard_map/ppermute | solution.py:155
  331.6 19.3 %collective-permute-start.18 = (f32[2,2,4,2,32,128]{5,4,3,2,1,0:T(8,128)}, f32[2,2,4,2,32,128]{5,4,3,2,1,0:T(8,128)S(1)}, u32[]{:S(2)}, u32[]{:S(2)}) collective-permute-start(f32[2,2,4,2,32,128]{5,4,3,2,1,0:T(8,128)} %gate.12), channel_id=1, source_target_pairs={{0,8},{8,0},{16,24},{24,16},{1,9},{9,1},{17,25},{25,17},{2,10},{10... | collective-permute-start | bytes 1572872 | tf_op jit(solution)/shard_map/ppermute | solution.py:155
  333.7 25.2 %collective-permute-start.34 = (f32[2,4,4,32,128]{4,3,2,1,0:T(8,128)S(1)}, f32[2,4,4,32,128]{4,3,2,1,0:T(8,128)}, u32[]{:S(2)}, u32[]{:S(2)}) collective-permute-start(f32[2,4,4,32,128]{4,3,2,1,0:T(8,128)S(1)} %dynamic-slice_bitcast_fusion.3), channel_id=1, source_target_pairs={{0,16},{8,24},{16,0},{24,8},{1,17},{9,25},{17,1},{25,9},{2,18},{10... | collective-permute-start | bytes 1572872 | tf_op jit(solution)/shard_map/ppermute | solution.py:155
  333.9 17.9 %copy-start.5 = (f32[2,2,2,4,1,32,128]{6,5,4,3,2,1,0:T(8,128)}, f32[2,2,2,4,1,32,128]{6,5,4,3,2,1,0:T(8,128)S(1)}, u32[]{:S(2)}) copy-start(f32[2,2,2,4,1,32,128]{6,5,4,3,2,1,0:T(8,128)S(1)} %bitcast_add_fusion.5.refs_1_) | copy-start | bytes 1572868
  351.8 11.5 %copy-start.6 = (f32[2,2,2,4,1,32,128]{6,5,4,3,2,1,0:T(8,128)S(1)}, f32[2,2,2,4,1,32,128]{6,5,4,3,2,1,0:T(8,128)}, u32[]{:S(2)}) copy-start(f32[2,2,2,4,1,32,128]{6,5,4,3,2,1,0:T(8,128)} %copy-done.5) | copy-start | bytes 1572868
  351.8 12.3 %copy-start.8 = (f32[2,2,2,2,4,1,32,128]{7,6,5,4,3,2,1,0:T(8,128)S(1)}, f32[2,2,2,2,4,1,32,128]{7,6,5,4,3,2,1,0:T(8,128)}, u32[]{:S(2)}) copy-start(f32[2,2,2,2,4,1,32,128]{7,6,5,4,3,2,1,0:T(8,128)} %product.4) | copy-start | bytes 3145732
  351.8 11.5 %collective-permute-start.20 = (f32[2,2,4,1,32,128]{5,4,3,2,1,0:T(8,128)}, f32[2,2,4,1,32,128]{5,4,3,2,1,0:T(8,128)S(1)}, u32[]{:S(2)}, u32[]{:S(2)}) collective-permute-start(f32[2,2,4,1,32,128]{5,4,3,2,1,0:T(8,128)} %gate.14), channel_id=1, source_target_pairs={{0,8},{8,0},{16,24},{24,16},{1,9},{9,1},{17,25},{25,17},{2,10},{10... | collective-permute-start | bytes 786440 | tf_op jit(solution)/shard_map/ppermute | solution.py:155
  351.9 12.2 %collective-permute-start.19 = (f32[2,2,2,4,1,32,128]{6,5,4,3,2,1,0:T(8,128)}, f32[2,2,2,4,1,32,128]{6,5,4,3,2,1,0:T(8,128)S(1)}, u32[]{:S(2)}, u32[]{:S(2)}) collective-permute-start(f32[2,2,2,4,1,32,128]{6,5,4,3,2,1,0:T(8,128)} %gate.13), channel_id=1, source_target_pairs={{0,1},{1,0},{2,3},{3,2},{4,5},{5,4},{6,7},{7,6},{8,9},{9,8},{10,11... | collective-permute-start | bytes 1572872 | tf_op jit(solution)/shard_map/ppermute | solution.py:155
  360.0 28.4 %collective-permute-start.37 = (f32[2,4,4,32,128]{4,3,2,1,0:T(8,128)S(1)}, f32[2,4,4,32,128]{4,3,2,1,0:T(8,128)}, u32[]{:S(2)}, u32[]{:S(2)}) collective-permute-start(f32[2,4,4,32,128]{4,3,2,1,0:T(8,128)S(1)} %bitcast_add_fusion.3.refs_0_), channel_id=1, source_target_pairs={{0,6},{2,4},{4,2},{6,0},{1,7},{3,5},{5,3},{7,1},{8,14},{10,12},{12... | collective-permute-start | bytes 1572872 | tf_op jit(solution)/shard_map/ppermute | solution.py:254
  360.1 28.3 %collective-permute-start.36 = (f32[2,4,4,32,128]{4,3,2,1,0:T(8,128)S(1)}, f32[2,4,4,32,128]{4,3,2,1,0:T(8,128)}, u32[]{:S(2)}, u32[]{:S(2)}) collective-permute-start(f32[2,4,4,32,128]{4,3,2,1,0:T(8,128)S(1)} %bitcast_add_fusion.3.refs_0_), channel_id=1, source_target_pairs={{0,4},{2,6},{4,0},{6,2},{1,5},{3,7},{5,1},{7,3},{8,12},{10,14},{12... | collective-permute-start | bytes 1572872 | tf_op jit(solution)/shard_map/ppermute | solution.py:254
  361.7 12.0 %collective-permute-start.30 = (f32[2,4,2,32,128]{4,3,2,1,0:T(8,128)S(1)}, f32[2,4,2,32,128]{4,3,2,1,0:T(8,128)S(1)}, u32[]{:S(2)}, u32[]{:S(2)}) collective-permute-start(f32[2,4,2,32,128]{4,3,2,1,0:T(8,128)S(1)} %dynamic-slice_bitcast_fusion.7), channel_id=1, source_target_pairs={{0,16},{8,24},{16,0},{24,8},{1,17},{9,25},{17,1},{25,9},{2,18},{10... | collective-permute-start | bytes 786440 | tf_op jit(solution)/shard_map/ppermute | solution.py:155
  364.1 10.2 %copy-start.10 = (f32[2,2,4,1,32,128]{5,4,3,2,1,0:T(8,128)S(1)}, f32[2,2,4,1,32,128]{5,4,3,2,1,0:T(8,128)}, u32[]{:S(2)}) copy-start(f32[2,2,4,1,32,128]{5,4,3,2,1,0:T(8,128)} %bitcast_add_fusion.8.refs_1_) | copy-start | bytes 786436
  365.0 32.9 %collective-permute-start.35 = (f32[2,4,4,32,128]{4,3,2,1,0:T(8,128)S(1)}, f32[2,4,4,32,128]{4,3,2,1,0:T(8,128)S(1)}, u32[]{:S(2)}, u32[]{:S(2)}) collective-permute-start(f32[2,4,4,32,128]{4,3,2,1,0:T(8,128)S(1)} %bitcast_add_fusion.3.refs_0_), channel_id=1, source_target_pairs={{0,2},{2,0},{4,6},{6,4},{1,3},{3,1},{5,7},{7,5},{8,10},{10,8},{12,... | collective-permute-start | bytes 1572872 | tf_op jit(solution)/shard_map/ppermute | solution.py:254
  365.0 14.2 %collective-permute-start.21 = (f32[2,2,4,1,32,128]{5,4,3,2,1,0:T(8,128)}, f32[2,2,4,1,32,128]{5,4,3,2,1,0:T(8,128)S(1)}, u32[]{:S(2)}, u32[]{:S(2)}) collective-permute-start(f32[2,2,4,1,32,128]{5,4,3,2,1,0:T(8,128)} %gate.15), channel_id=1, source_target_pairs={{0,8},{8,0},{16,24},{24,16},{1,9},{9,1},{17,25},{25,17},{2,10},{10... | collective-permute-start | bytes 786440 | tf_op jit(solution)/shard_map/ppermute | solution.py:155
  373.7 34.5 %copy-start.12 = (f32[2,4,2,32,128]{4,3,2,1,0:T(8,128)}, f32[2,4,2,32,128]{4,3,2,1,0:T(8,128)S(1)}, u32[]{:S(2)}) copy-start(f32[2,4,2,32,128]{4,3,2,1,0:T(8,128)S(1)} %bitcast_add_fusion.7.refs_0_) | copy-start | bytes 786436
  373.7 25.7 %collective-permute-start.33 = (f32[2,4,2,32,128]{4,3,2,1,0:T(8,128)S(1)}, f32[2,4,2,32,128]{4,3,2,1,0:T(8,128)S(1)}, u32[]{:S(2)}, u32[]{:S(2)}) collective-permute-start(f32[2,4,2,32,128]{4,3,2,1,0:T(8,128)S(1)} %bitcast_add_fusion.7.refs_0_), channel_id=1, source_target_pairs={{0,6},{2,4},{4,2},{6,0},{1,7},{3,5},{5,3},{7,1},{8,14},{10,12},{12... | collective-permute-start | bytes 786440 | tf_op jit(solution)/shard_map/ppermute | solution.py:254
  379.2 8.3 %collective-permute-start.26 = (f32[2,4,1,32,128]{4,3,2,1,0:T(8,128)S(1)}, f32[2,4,1,32,128]{4,3,2,1,0:T(8,128)S(1)}, u32[]{:S(2)}, u32[]{:S(2)}) collective-permute-start(f32[2,4,1,32,128]{4,3,2,1,0:T(8,128)S(1)} %dynamic-slice_bitcast_fusion.10), channel_id=1, source_target_pairs={{0,16},{8,24},{16,0},{24,8},{1,17},{9,25},{17,1},{25,9},{2,18},{10... | collective-permute-start | bytes 393224 | tf_op jit(solution)/shard_map/ppermute | solution.py:155
  387.4 12.1 %collective-permute-start.32 = (f32[2,4,2,32,128]{4,3,2,1,0:T(8,128)S(1)}, f32[2,4,2,32,128]{4,3,2,1,0:T(8,128)S(1)}, u32[]{:S(2)}, u32[]{:S(2)}) collective-permute-start(f32[2,4,2,32,128]{4,3,2,1,0:T(8,128)S(1)} %bitcast_add_fusion.7.refs_0_), channel_id=1, source_target_pairs={{0,4},{2,6},{4,0},{6,2},{1,5},{3,7},{5,1},{7,3},{8,12},{10,14},{12... | collective-permute-start | bytes 786440 | tf_op jit(solution)/shard_map/ppermute | solution.py:254
  388.4 11.8 %collective-permute-start.31 = (f32[2,4,2,32,128]{4,3,2,1,0:T(8,128)S(1)}, f32[2,4,2,32,128]{4,3,2,1,0:T(8,128)S(1)}, u32[]{:S(2)}, u32[]{:S(2)}) collective-permute-start(f32[2,4,2,32,128]{4,3,2,1,0:T(8,128)S(1)} %bitcast_add_fusion.7.refs_0_), channel_id=1, source_target_pairs={{0,2},{2,0},{4,6},{6,4},{1,3},{3,1},{5,7},{7,5},{8,10},{10,8},{12,... | collective-permute-start | bytes 786440 | tf_op jit(solution)/shard_map/ppermute | solution.py:254
  388.4 9.2 %collective-permute-start.22 = (f32[2,4,1,32,128]{4,3,2,1,0:T(8,128)S(1)}, f32[2,4,1,32,128]{4,3,2,1,0:T(8,128)S(1)}, u32[]{:S(2)}, u32[]{:S(2)}) collective-permute-start(f32[2,4,1,32,128]{4,3,2,1,0:T(8,128)S(1)} %dynamic-slice_bitcast_fusion.11), channel_id=1, source_target_pairs={{0,16},{8,24},{16,0},{24,8},{1,17},{9,25},{17,1},{25,9},{2,18},{10... | collective-permute-start | bytes 393224 | tf_op jit(solution)/shard_map/ppermute | solution.py:155
  388.5 22.8 %copy-start.15 = (f32[2,4,1,32,128]{4,3,2,1,0:T(8,128)}, f32[2,4,1,32,128]{4,3,2,1,0:T(8,128)S(1)}, u32[]{:S(2)}) copy-start(f32[2,4,1,32,128]{4,3,2,1,0:T(8,128)S(1)} %bitcast_add_fusion.10.refs_0_) | copy-start | bytes 393220
  397.5 5.6 %collective-permute-start.29 = (f32[2,4,1,32,128]{4,3,2,1,0:T(8,128)S(1)}, f32[2,4,1,32,128]{4,3,2,1,0:T(8,128)S(1)}, u32[]{:S(2)}, u32[]{:S(2)}) collective-permute-start(f32[2,4,1,32,128]{4,3,2,1,0:T(8,128)S(1)} %bitcast_add_fusion.10.refs_0_), channel_id=1, source_target_pairs={{0,6},{2,4},{4,2},{6,0},{1,7},{3,5},{5,3},{7,1},{8,14},{10,12},{12... | collective-permute-start | bytes 393224 | tf_op jit(solution)/shard_map/ppermute | solution.py:254
  397.9 13.4 %copy-start.14 = (f32[2,4,1,32,128]{4,3,2,1,0:T(8,128)}, f32[2,4,1,32,128]{4,3,2,1,0:T(8,128)S(1)}, u32[]{:S(2)}) copy-start(f32[2,4,1,32,128]{4,3,2,1,0:T(8,128)S(1)} %bitcast_add_fusion.11.refs_0_) | copy-start | bytes 393220
  397.9 13.4 %collective-permute-start.28 = (f32[2,4,1,32,128]{4,3,2,1,0:T(8,128)S(1)}, f32[2,4,1,32,128]{4,3,2,1,0:T(8,128)S(1)}, u32[]{:S(2)}, u32[]{:S(2)}) collective-permute-start(f32[2,4,1,32,128]{4,3,2,1,0:T(8,128)S(1)} %bitcast_add_fusion.10.refs_0_), channel_id=1, source_target_pairs={{0,4},{2,6},{4,0},{6,2},{1,5},{3,7},{5,1},{7,3},{8,12},{10,14},{12... | collective-permute-start | bytes 393224 | tf_op jit(solution)/shard_map/ppermute | solution.py:254
  399.4 11.9 %collective-permute-start.27 = (f32[2,4,1,32,128]{4,3,2,1,0:T(8,128)S(1)}, f32[2,4,1,32,128]{4,3,2,1,0:T(8,128)S(1)}, u32[]{:S(2)}, u32[]{:S(2)}) collective-permute-start(f32[2,4,1,32,128]{4,3,2,1,0:T(8,128)S(1)} %bitcast_add_fusion.10.refs_0_), channel_id=1, source_target_pairs={{0,2},{2,0},{4,6},{6,4},{1,3},{3,1},{5,7},{7,5},{8,10},{10,8},{12,... | collective-permute-start | bytes 393224 | tf_op jit(solution)/shard_map/ppermute | solution.py:254
  399.5 15.8 %collective-permute-start.25 = (f32[2,4,1,32,128]{4,3,2,1,0:T(8,128)S(1)}, f32[2,4,1,32,128]{4,3,2,1,0:T(8,128)S(1)}, u32[]{:S(2)}, u32[]{:S(2)}) collective-permute-start(f32[2,4,1,32,128]{4,3,2,1,0:T(8,128)S(1)} %bitcast_add_fusion.11.refs_0_), channel_id=1, source_target_pairs={{0,6},{2,4},{4,2},{6,0},{1,7},{3,5},{5,3},{7,1},{8,14},{10,12},{12... | collective-permute-start | bytes 393224 | tf_op jit(solution)/shard_map/ppermute | solution.py:254
  400.1 15.2 %collective-permute-start.24 = (f32[2,4,1,32,128]{4,3,2,1,0:T(8,128)S(1)}, f32[2,4,1,32,128]{4,3,2,1,0:T(8,128)S(1)}, u32[]{:S(2)}, u32[]{:S(2)}) collective-permute-start(f32[2,4,1,32,128]{4,3,2,1,0:T(8,128)S(1)} %bitcast_add_fusion.11.refs_0_), channel_id=1, source_target_pairs={{0,4},{2,6},{4,0},{6,2},{1,5},{3,7},{5,1},{7,3},{8,12},{10,14},{12... | collective-permute-start | bytes 393224 | tf_op jit(solution)/shard_map/ppermute | solution.py:254
  403.1 12.2 %collective-permute-start.23 = (f32[2,4,1,32,128]{4,3,2,1,0:T(8,128)S(1)}, f32[2,4,1,32,128]{4,3,2,1,0:T(8,128)S(1)}, u32[]{:S(2)}, u32[]{:S(2)}) collective-permute-start(f32[2,4,1,32,128]{4,3,2,1,0:T(8,128)S(1)} %bitcast_add_fusion.11.refs_0_), channel_id=1, source_target_pairs={{0,2},{2,0},{4,6},{6,4},{1,3},{3,1},{5,7},{7,5},{8,10},{10,8},{12,... | collective-permute-start | bytes 393224 | tf_op jit(solution)/shard_map/ppermute | solution.py:254
  (20 other events, 71.4 us)

commit v3 on v2

--- a/solution.py
+++ b/solution.py
@@ -11,6 +11,7 @@
 LANES = 128
 CHUNKS = (1, 3, 2, 1, 1)
 GROUPS = (4, 2, 1, 1)
+CHAINED = 2
 
 
 def gathered_body(amplitudes, integrals):
@@ -76,7 +77,31 @@
     )(place, *([amps] * n))
 
 
-def product_kernel(ni, kb, la, nj, place, *refs):
+def store_halves(ni, la, nj, place, out, acc):
+    high, low = place[0] >> 1, place[0] & 1
+    for d in range(4):
+        for q in range(4):
+            for j in range(nj):
+                piece = acc[j, pl.ds(d * ni * la, ni * la), pl.ds(q * LANES, LANES)]
+                out[high ^ (d >> 1), q & 1, q >> 1, low ^ (d & 1), j] = piece.reshape(ni, la, LANES)
+
+
+def store_turned(ni, la, nj, place, out, acc):
+    high, low = place[0] >> 1, place[0] & 1
+    for half in range(2):
+        for q in range(4):
+            for pair in range(nj // 2):
+                blocks = []
+                for j in (2 * pair, 2 * pair + 1):
+                    for side in range(2):
+                        at = pl.multiple_of((2 * half + (low ^ side)) * la, la)
+                        blocks.append(acc[j, pl.ds(at, la), pl.ds(q * LANES, LANES)])
+                turned = jnp.concatenate(blocks, axis=0).T.astype(jnp.bfloat16)
+                for n in range(4):
+                    out[q, n, high ^ half, pair] = turned[32 * n : 32 * (n + 1), :]
+
+
+def product_kernel(store, ni, kb, la, nj, place, *refs):
     ts, ws, out, acc = refs[: 4 * ni], refs[4 * ni : 4 * ni + 4], refs[-2], refs[-1]
     step = pl.program_id(0)
     left = [
@@ -97,17 +122,10 @@
 
     @pl.when(step == pl.num_programs(0) - 1)
     def _():
-        high, low = place[0] >> 1, place[0] & 1
-        for d in range(4):
-            for q in range(4):
-                for j in range(nj):
-                    piece = acc[j, pl.ds(d * ni * la, ni * la), pl.ds(q * LANES, LANES)]
-                    out[high ^ (d >> 1), q & 1, q >> 1, low ^ (d & 1), j] = piece.reshape(
-                        ni, la, LANES
-                    )
-
-
-def product(place, sources, ws):
+        store(ni, la, nj, place, out, acc)
+
+
+def product(place, sources, ws, last):
     ni = len(sources[0])
     _, lk, la, _ = sources[0][0][0].shape
     nj, width = ws[0].shape[1], ws[0].shape[3]
@@ -115,9 +133,11 @@
     kb = 8
     rows = 4 * ni * la
     flat = [pair for source in sources for pair in source]
-    out = jax.ShapeDtypeStruct((2, 2, 2, 2, nj, ni, la, LANES), jnp.float32)
-    return pl.pallas_call(
-        functools.partial(product_kernel, ni, kb, la, nj),
+    shape = (4, 4, 2, nj // 2, 32, LANES) if last else (2, 2, 2, 2, nj, ni, la, LANES)
+    store = store_turned if last else store_halves
+    out = jax.ShapeDtypeStruct(shape, jnp.bfloat16 if last else jnp.float32)
+    return pl.pallas_call(
+        functools.partial(product_kernel, store, ni, kb, la, nj),
         out_shape=out,
         grid_spec=pltpu.PrefetchScalarGridSpec(
             num_scalar_prefetch=1,
@@ -127,11 +147,11 @@
                 for _, at in flat
             ]
             + [pl.BlockSpec((kb, nj, lc, width), lambda s, place: (s, 0, 0, 0))] * 4,
-            out_specs=pl.BlockSpec(out.shape, lambda s, place: (0,) * 8),
+            out_specs=pl.BlockSpec(shape, lambda s, place: (0,) * len(shape)),
             scratch_shapes=[pltpu.VMEM((nj, rows, width), jnp.float32)],
         ),
         compiler_params=pltpu.CompilerParams(vmem_limit_bytes=60 * 2**20),
-        cost_estimate=pl.CostEstimate(flops=2 * rows * nj * width * lk * 4 * lc * 2, bytes_accessed=1000, transcendentals=0),
+        cost_estimate=pl.CostEstimate(flops=2 * rows * nj * width * lk * 4 * lc * 3, bytes_accessed=1000, transcendentals=0),
         name="product",
     )(place, *[array for array, _ in flat], *ws)
 
@@ -153,12 +173,6 @@
 def swapped(x, axis, bits=1):
     n = lax.axis_size(axis)
     return lax.ppermute(x, axis, [(s, s ^ bits) for s in range(n)])
-
-
-def exchanged(x, axis, mine, bits=1):
-    kept = lax.dynamic_index_in_dim(x, mine, 0, keepdims=False)
-    sent = lax.dynamic_index_in_dim(x, 1 - mine, 0, keepdims=False)
-    return kept + swapped(sent, axis, bits)
 
 
 def finish_kernel(nj, place, *refs):
@@ -202,6 +216,44 @@
         cost_estimate=pl.CostEstimate(flops=1000, bytes_accessed=1000, transcendentals=0),
         name="finish",
     )(place, *pieces, *args)
+
+
+def gather_kernel(nj, came, before, out):
+    block = lax.broadcasted_iota(jnp.int32, (32, LANES), 1) >> 5
+    for pair in range(nj // 2):
+        sums = []
+        for n in range(4):
+            total = came[0, n, 0, pair].astype(jnp.float32)
+            for zs in range(4):
+                for r in range(2):
+                    if zs + r > 0:
+                        total += came[zs, n, r, pair].astype(jnp.float32)
+            sums.append(total)
+        for m in range(4):
+            value = None
+            for n in range(4):
+                turned = sums[n] if n == m else pltpu.roll(sums[n], (32 * (n - m)) % LANES, 1)
+                value = turned if n == 0 else jnp.where(block == n, turned, value)
+            low = m & 1
+            out[0, 2 * pair + (m >> 1), :, low * LANES : (low + 1) * LANES] = value
+
+
+def gather(came, before, at):
+    _, nj, wide, width = before.shape
+    return pl.pallas_call(
+        functools.partial(gather_kernel, nj),
+        out_shape=jax.ShapeDtypeStruct(before.shape, before.dtype),
+        grid=(1,),
+        in_specs=[
+            pl.BlockSpec(came.shape, lambda i: (0,) * 6),
+            pl.BlockSpec(memory_space=pl.ANY),
+        ],
+        out_specs=pl.BlockSpec((1, nj, wide, width), lambda i: (at, 0, 0, 0)),
+        input_output_aliases={1: 0},
+        compiler_params=pltpu.CompilerParams(vmem_limit_bytes=60 * 2**20),
+        cost_estimate=pl.CostEstimate(flops=1000, bytes_accessed=1000, transcendentals=0),
+        name="gather",
+    )(came, before)
 
 
 def tiled_body(amplitudes, integrals):
@@ -232,18 +284,20 @@
         n += count
         two = [(moved[where[i][0]][0], where[i][1]) for i in at]
         three = [(moved[where[i][0]][1], where[i][1]) for i in at]
-        totals.append(product(place, ([(own, i) for i in at], [(one, i) for i in at], two, three), ws))
+        totals.append(product(place, ([(own, i) for i in at], [(one, i) for i in at], two, three), ws, g >= CHAINED))
 
     def exchange(total, axis, mine, bits, *after):
         kept = lax.dynamic_index_in_dim(total, mine, 0, keepdims=False)
         sent = lax.dynamic_index_in_dim(total, 1 - mine, 0, keepdims=False)
         if after:
             (sent,) = gated((sent,), *after)
+        if bits == 2:
+            return kept + swapped(sent.astype(jnp.bfloat16), axis, bits).astype(jnp.float32)
         return kept + swapped(sent, axis, bits)
 
     result = None
     rows, lows, highs = [], [], []
-    for g, total in enumerate(totals):
+    for g, total in enumerate(totals[:CHAINED]):
         rows.append(exchange(total, "row", row, 1, *rows[g - 1 : g], *lows[max(g - 2, 0) : max(g - 1, 0)]))
         lows.append(exchange(rows[g], "z", z & 1, 1, *lows[max(g - 1, 0) : g]))
         highs.append(exchange(lows[g], "z", z >> 1, 2))
@@ -253,6 +307,10 @@
             pairs = [(s, s ^ bits) for s in range(4)]
             pieces.append(lax.ppermute(total, ("x", "core"), pairs))
         result = finish(place, pieces, sum(GROUPS[:g]), ni, result)
+    for g, total in enumerate(totals[CHAINED:], CHAINED):
+        came = total.reshape(32, -1, 32, LANES)
+        came = lax.all_to_all(came, ("z", "x", "core", "row"), split_axis=0, concat_axis=0, tiled=True)
+        result = gather(came.reshape(total.shape), result, sum(GROUPS[:g]))
     return jnp.transpose(result, (0, 3, 1, 2))
 
 

time: 421 us -> 400 us (0.950)
  waiting for transfers between devices: 177 us -> 163 us
    ppermute x26 -> x20, waiting for transfers between devices: 176 us -> 149 us  [swapped(): return lax.ppermute(x, axis, [(s, s ^ bits) for s in range(n)])]
    ppermute x12 -> x6, waiting for transfers between devices: 1.61 us -> 13.2 us  [tiled_body(): pieces.append(lax.ppermute(total, ('x', 'core'), pairs))]
    all_to_all x0 -> x2, starting transfers between devices: none -> 9.64 us  [tiled_body(): lax.all_to_all(came, ('z', 'x', 'core', 'row'), split_axis=0, concat_axis...]
    pallas_call x4 -> x2, Pallas kernels: 13.3 us -> 7.82 us  [finish(): pl.pallas_call(functools.partial(finish_kernel, nj), out_shape=out, grid_...]
    add x12 -> x4, other arithmetic: 11.6 us -> 6.68 us  [exchange(): return kept + swapped(sent, axis, bits)]
    squeeze x12 -> x4, local copies, waits for them, and re-layouts: 10.7 us -> 6.51 us  [exchange(): sent = lax.dynamic_index_in_dim(total, 1 - mine, 0, keepdims=False)]
    pallas_call x4 -> x6, Pallas kernels: 70.6 us -> 74.5 us  [the longest x4 70.7 us: product(): pl.pallas_call(functools.partial(product_kernel, store, ni, kb, la, nj),...]
    ppermute x26 -> x20, starting transfers between devices: 82.8 us -> 79.8 us  [swapped(): return lax.ppermute(x, axis, [(s, s ^ bits) for s in range(n)])]
  transfers between devices with their start and end apart: 38 -> 28, of which waited for: 15 -> 9; matrix products, arithmetic and copies ran while one was open for 7% -> 6% of each run, Pallas kernels for 26% -> 27%
where the time goes in v3:
time: 400 us; the launch traced here: 399 us
  waiting for transfers between devices  163 us (41%)
  Pallas kernels  113 us (28%)
  starting transfers between devices  93.5 us (23%)
  local copies, waits for them, and re-layouts  20.5 us (5%)
  other arithmetic  8.4 us (2%)
    ppermute x20, waiting for transfers between devices, swapped(): return lax.ppermute(x, axis, [(s, s ^ bits) for s in range(n)])  149 us
    ppermute x20, starting transfers between devices, swapped(): return lax.ppermute(x, axis, [(s, s ^ bits) for s in range(n)])  79.8 us
    pallas_call x4, Pallas kernels, product(): pl.pallas_call(functools.partial(product_kernel, store, ni, kb, la, nj),...  70.7 us
    pallas_call x6, Pallas kernels, prep(): pl.pallas_call(functools.partial(prep_kernel, la, lk, n), out_shape=[out]...  31.1 us
    ppermute x6, waiting for transfers between devices, tiled_body(): pieces.append(lax.ppermute(total, ('x', 'core'), pairs))  13.2 us
    all_to_all x2, starting transfers between devices, tiled_body(): lax.all_to_all(came, ('z', 'x', 'core', 'row'), split_axis=0, concat_axis...  9.64 us
  transfers between devices with their start and end apart: 28, of which 9 were waited for; matrix products, arithmetic and copies ran while one was open for 6% of the time, Pallas kernels for 27%

profile of v3, /device:TPU:0, one launch (start us, length us, event | category | flops | bytes accessed | tf_op | source)
XLA Modules:
  0.0 398.7 jit_solution(12492601571639346234)
XLA Ops:
  0.7 3.4 prep.6
  4.0 5.0 %collective-permute-start.6 = (bf16[1,48,32,128]{3,2,1,0:T(8,128)(2,1)}, bf16[1,48,32,128]{3,2,1,0:T(8,128)(2,1)}, u32[]{:S(2)}, u32[]{:S(2)}) collective-permute-start(bf16[1,48,32,128]{3,2,1,0:T(8,128)(2,1)} %get-tuple-element.29), channel_id=1, source_target_pairs={{0,24},{8,16},{16,8},{24,0},{1,25},{9,17},{17,9},{25,1},{2,26},{10... | collective-permute-start | bytes 1179656 | tf_op jit(solution)/shard_map/ppermute | solution.py:175
  9.1 5.8 %prep.7 = (bf16[3,48,32,128]{3,2,1,0:T(8,128)(2,1)}, bf16[3,48,32,128]{3,2,1,0:T(8,128)(2,1)}) custom-call(s32[3]{0:T(128)} %pad_add_fusion.place, f32[8,1536,512]{2,1,0:T(8,128)} %bitcast.38, f32[8,1536,512]{2,1,0:T(8,128)} %bitcast.39), custom_call_target="tpu_custom_call" | custom-call | flops 30000001024 | bytes 1000 | tf_op jit(solution)/shard_map/prep/pallas_call | solution.py:62
  14.8 1.0 collective-permute-start.7
  15.9 7.6 %copy.12 = bf16[48,32,4,512]{3,1,2,0:T(8,128)(2,1)} copy(bf16[48,32,4,512]{3,2,1,0:T(4,128)(2,1)} %param.3) | data formatting | bytes 12582912 | tf_op jit(solution)/shard_map/optimization_barrier | solution.py:267
  23.4 1.5 collective-permute-start.4
  25.4 11.1 %prep.8 = (bf16[8,48,32,128]{3,2,1,0:T(8,128)(2,1)}, bf16[8,48,32,128]{3,2,1,0:T(8,128)(2,1)}) custom-call(s32[3]{0:T(128)} %gate.4.place, f32[8,1536,512]{2,1,0:T(8,128)} %bitcast.40, f32[8,1536,512]{2,1,0:T(8,128)} %bitcast.41), custom_call_target="tpu_custom_call" | custom-call | flops 80000000000 | bytes 1000 | tf_op jit(solution)/shard_map/prep/pallas_call | solution.py:62
  36.5 3.4 collective-permute-start
  39.9 3.9 prep.10
  43.8 3.6 prep.11
  47.4 32.0 %collective-permute-start.5 = (bf16[1,48,32,128]{3,2,1,0:T(8,128)(2,1)S(1)}, bf16[1,48,32,128]{3,2,1,0:T(8,128)(2,1)S(1)}, u32[]{:S(2)}, u32[]{:S(2)}) collective-permute-start(bf16[1,48,32,128]{3,2,1,0:T(8,128)(2,1)S(1)} %copy-done.13), channel_id=1, source_target_pairs={{0,16},{8,24},{16,0},{24,8},{1,17},{9,25},{17,1},{25,9},{2,18},{10... | collective-permute-start | bytes 1179656 | tf_op jit(solution)/shard_map/ppermute | solution.py:175
  79.4 3.4 prep.9
  82.7 61.4 %collective-permute-done.5.refs_1_.refs_8_ = bf16[1,48,32,128]{3,2,1,0:T(8,128)(2,1)S(1)} collective-permute-done((bf16[1,48,32,128]{3,2,1,0:T(8,128)(2,1)S(1)}, bf16[1,48,32,128]{3,2,1,0:T(8,128)(2,1)S(1)}, u32[]{:S(2)}, u32[]{:S(2)}) %collective-permute-start.5) | collective-permute-done | bytes 393248 | tf_op jit(solution)/shard_map/ppermute | solution.py:175
  144.2 1.3 collective-permute-done.refs_5_.refs_1_.refs_2_.refs_3_.refs_4_.refs_6_.refs_7_
  145.5 14.6 %collective-permute-done.4.refs_0_ = bf16[48,4,32,512]{3,2,1,0:T(8,128)(2,1)} collective-permute-done((bf16[48,4,32,512]{3,2,1,0:T(8,128)(2,1)}, bf16[48,4,32,512]{3,2,1,0:T(8,128)(2,1)}, u32[]{:S(2)}, u32[]{:S(2)}) %collective-permute-start.4) | collective-permute-done | bytes 6291488 | tf_op jit(solution)/shard_map/ppermute | solution.py:175
  160.2 1.0 copy-done.9
  161.3 2.3 collective-permute-start.12
  163.5 3.5 collective-permute-start.13
  167.0 3.7 collective-permute-done.9.refs_7_.refs_11_.refs_19_
  170.7 25.2 %product.7 = f32[2,2,2,2,4,4,32,128]{7,6,5,4,3,2,1,0:T(8,128)} custom-call(s32[3]{0:T(128)} %pad_add_fusion.place, bf16[8,48,32,128]{3,2,1,0:T(8,128)(2,1)} %get-tuple-element.25.refs_0_.refs_1_.refs_2_.refs_3_, bf16[8,48,32,128]{3,2,1,0:T(8,128)(2,1)} %get-tuple-element.25.refs_0_.refs_1_.refs_2_.refs_3_, ...), custom_call_target="tpu_custom_call" | custom-call | flops 38654705664 | bytes 1000 | tf_op jit(solution)/shard_map/product/pallas_call | solution.py:139
  195.9 3.2 dynamic-slice_bitcast_fusion
  199.1 1.5 collective-permute-start.14
  200.6 2.3 collective-permute-start.10
  202.9 3.5 collective-permute-start.11
  206.3 27.0 %collective-permute-done.12.refs_4_.refs_5_ = bf16[2,48,32,128]{3,2,1,0:T(8,128)(2,1)} collective-permute-done((bf16[2,48,32,128]{3,2,1,0:T(8,128)(2,1)S(1)}, bf16[2,48,32,128]{3,2,1,0:T(8,128)(2,1)}, u32[]{:S(2)}, u32[]{:S(2)}) %collective-permute-start.12) | collective-permute-done | bytes 786464 | tf_op jit(solution)/shard_map/ppermute | solution.py:175
  233.3 17.2 %product.6 = f32[2,2,2,2,4,2,32,128]{7,6,5,4,3,2,1,0:T(8,128)} custom-call(s32[3]{0:T(128)} %pad_add_fusion.place, bf16[8,48,32,128]{3,2,1,0:T(8,128)(2,1)} %get-tuple-element.25.refs_0_.refs_1_.refs_2_.refs_3_, bf16[8,48,32,128]{3,2,1,0:T(8,128)(2,1)} %get-tuple-element.25.refs_0_.refs_1_.refs_2_.refs_3_, bf16[8,48,32,128]{3,2,1,0:T(8,128)(2,1)} %copy-done.5, ...), custom_call_target="tpu_custom_call" | custom-call | flops 19327352832 | bytes 1000 | tf_op jit(solution)/shard_map/product/pallas_call | solution.py:139
  250.5 2.3 dynamic-slice_bitcast_fusion.2.refs_0_
  252.8 3.4 bitcast_add_fusion.refs_1_
  256.2 1.5 collective-permute-start.15
  257.7 17.6 %collective-permute-start.1 = (bf16[1,48,32,128]{3,2,1,0:T(8,128)(2,1)S(1)}, bf16[1,48,32,128]{3,2,1,0:T(8,128)(2,1)}, u32[]{:S(2)}, u32[]{:S(2)}) collective-permute-start(bf16[1,48,32,128]{3,2,1,0:T(8,128)(2,1)S(1)} %copy-done.14), channel_id=1, source_target_pairs={{0,16},{8,24},{16,0},{24,8},{1,17},{9,25},{17,1},{25,9},{2,18},{10... | collective-permute-start | bytes 1179656 | tf_op jit(solution)/shard_map/ppermute | solution.py:175
  275.4 2.1 collective-permute-start.2
  277.7 14.1 %product.5 = bf16[4,4,2,2,32,128]{5,4,3,2,1,0:T(8,128)(2,1)} custom-call(s32[3]{0:T(128)} %pad_add_fusion.place, bf16[8,48,32,128]{3,2,1,0:T(8,128)(2,1)} %get-tuple-element.25.refs_0_.refs_1_.refs_2_.refs_3_, bf16[8,48,32,128]{3,2,1,0:T(8,128)(2,1)} %copy-done.5, bf16[1,48,32,128]{3,2,1,0:T(8,128)(2,1)} %collective-permute-done.10.refs_2_, ...), custom_call_target="tpu_custom_call" | custom-call | flops 9663676416 | bytes 1000 | tf_op jit(solution)/shard_map/product/pallas_call | solution.py:139
  291.8 4.2 %all-to-all-start.1 = ((bf16[32,2,32,128]{3,2,1,0:T(8,128)(2,1)}), bf16[32,2,32,128]{3,2,1,0:T(8,128)(2,1)}, u32[]{:S(2)}, u32[]{:S(2)}) async-start(bf16[32,2,32,128]{3,2,1,0:T(8,128)(2,1)} %bitcast.50), calls=%async_computation.1 | async-start | bytes 1048576 | tf_op jit(solution)/shard_map/all_to_all | solution.py:312
  296.1 1.8 bitcast_add_fusion.2
  298.8 26.5 %collective-permute-done.16 = f32[2,2,4,4,32,128]{5,4,3,2,1,0:T(8,128)} collective-permute-done((f32[2,2,4,4,32,128]{5,4,3,2,1,0:T(8,128)S(1)}, f32[2,2,4,4,32,128]{5,4,3,2,1,0:T(8,128)}, u32[]{:S(2)}, u32[]{:S(2)}) %collective-permute-start.16) | collective-permute-done | bytes 1048608 | tf_op jit(solution)/shard_map/ppermute | solution.py:175
  325.3 1.4 bitcast_add_fusion.1.refs_1_
  327.8 14.3 %product.4 = bf16[4,4,2,2,32,128]{5,4,3,2,1,0:T(8,128)(2,1)} custom-call(s32[3]{0:T(128)} %pad_add_fusion.place, bf16[8,48,32,128]{3,2,1,0:T(8,128)(2,1)} %get-tuple-element.25.refs_0_.refs_1_.refs_2_.refs_3_, bf16[8,48,32,128]{3,2,1,0:T(8,128)(2,1)} %copy-done.5, bf16[1,48,32,128]{3,2,1,0:T(8,128)(2,1)} %collective-permute-done.1.refs_2_, ...), custom_call_target="tpu_custom_call" | custom-call | flops 9663676416 | bytes 1000 | tf_op jit(solution)/shard_map/product/pallas_call | solution.py:139
  342.1 5.4 %all-to-all-start = ((bf16[32,2,32,128]{3,2,1,0:T(8,128)(2,1)}), bf16[32,2,32,128]{3,2,1,0:T(8,128)(2,1)S(1)}, u32[]{:S(2)}, u32[]{:S(2)}) async-start(bf16[32,2,32,128]{3,2,1,0:T(8,128)(2,1)} %bitcast.49), calls=%async_computation | async-start | bytes 1048576 | tf_op jit(solution)/shard_map/all_to_all | solution.py:312
  347.5 1.0 bitcast_add_fusion.3.refs_0_
  348.5 1.6 collective-permute-start.25
  350.3 2.4 collective-permute-start.18
  353.3 14.8 %collective-permute-done.18 = bf16[2,4,2,32,128]{4,3,2,1,0:T(8,128)(2,1)S(1)} collective-permute-done((bf16[2,4,2,32,128]{4,3,2,1,0:T(8,128)(2,1)S(1)}, bf16[2,4,2,32,128]{4,3,2,1,0:T(8,128)(2,1)S(1)}, u32[]{:S(2)}, u32[]{:S(2)}) %collective-permute-start.18) | collective-permute-done | bytes 131104 | tf_op jit(solution)/shard_map/ppermute | solution.py:175
  370.1 8.6 %collective-permute-done.24.refs_2_ = f32[2,4,4,32,128]{4,3,2,1,0:T(8,128)S(1)} collective-permute-done((f32[2,4,4,32,128]{4,3,2,1,0:T(8,128)S(1)}, f32[2,4,4,32,128]{4,3,2,1,0:T(8,128)S(1)}, u32[]{:S(2)}, u32[]{:S(2)}) %collective-permute-start.24) | collective-permute-done | bytes 524320 | tf_op jit(solution)/shard_map/ppermute | solution.py:308
  380.3 4.8 %finish.2.refs_4_ = f32[8,4,32,256]{3,2,1,0:T(8,128)} custom-call(s32[3]{0:T(128)} %pad_add_fusion.place, f32[2,4,4,32,128]{4,3,2,1,0:T(8,128)} %copy-done.7, f32[2,4,4,32,128]{4,3,2,1,0:T(8,128)} %copy-done.12, f32[2,4,4,32,128]{4,3,2,1,0:T(8,128)} %copy-done.11, f32[2,4,4,32,128]{4,3,2,1,0:T(8,128)} %copy-done.10), custom_call_target="tpu_custom_call" | custom-call | flops 1000 | bytes 1000 | tf_op jit(solution)/shard_map/finish/pallas_call | solution.py:200
  385.1 4.6 %collective-permute-done.20.refs_2_ = f32[2,4,2,32,128]{4,3,2,1,0:T(8,128)S(1)} collective-permute-done((f32[2,4,2,32,128]{4,3,2,1,0:T(8,128)S(1)}, f32[2,4,2,32,128]{4,3,2,1,0:T(8,128)S(1)}, u32[]{:S(2)}, u32[]{:S(2)}) %collective-permute-start.20) | collective-permute-done | bytes 262176 | tf_op jit(solution)/shard_map/ppermute | solution.py:308
  391.1 3.1 finish.3.before
  394.1 1.9 gather.2.before
  396.8 1.9 gather.3
  (81 shorter events, 9.9 us)
Async XLA Ops:
  4.0 43.4 %collective-permute-start.6 = (bf16[1,48,32,128]{3,2,1,0:T(8,128)(2,1)}, bf16[1,48,32,128]{3,2,1,0:T(8,128)(2,1)}, u32[]{:S(2)}, u32[]{:S(2)}) collective-permute-start(bf16[1,48,32,128]{3,2,1,0:T(8,128)(2,1)} %get-tuple-element.29), channel_id=1, source_target_pairs={{0,24},{8,16},{16,8},{24,0},{1,25},{9,17},{17,9},{25,1},{2,26},{10... | collective-permute-start | bytes 1179656 | tf_op jit(solution)/shard_map/ppermute | solution.py:175
  14.8 129.3 %collective-permute-start.8 = (bf16[3,48,32,128]{3,2,1,0:T(8,128)(2,1)}, bf16[3,48,32,128]{3,2,1,0:T(8,128)(2,1)}, u32[]{:S(2)}, u32[]{:S(2)}) collective-permute-start(bf16[3,48,32,128]{3,2,1,0:T(8,128)(2,1)} %get-tuple-element.30), channel_id=1, source_target_pairs={{0,24},{8,16},{16,8},{24,0},{1,25},{9,17},{17,9},{25,1},{2,26},{10... | collective-permute-start | bytes 3538952 | tf_op jit(solution)/shard_map/ppermute | solution.py:175
  14.8 10.1 %copy-start.19 = (s32[3]{0:T(128)S(1)}, s32[3]{0:T(128)}, u32[]{:S(2)}) copy-start(s32[3]{0:T(128)} %pad_add_fusion.place) | copy-start | bytes 40
  14.8 129.3 %collective-permute-start.7 = (bf16[3,48,32,128]{3,2,1,0:T(8,128)(2,1)}, bf16[3,48,32,128]{3,2,1,0:T(8,128)(2,1)}, u32[]{:S(2)}, u32[]{:S(2)}) collective-permute-start(bf16[3,48,32,128]{3,2,1,0:T(8,128)(2,1)} %get-tuple-element.23.refs_2_), channel_id=1, source_target_pairs={{0,16},{8,24},{16,0},{24,8},{1,17},{9,25},{17,1},{25,9},{2,18},{10... | collective-permute-start | bytes 3538952 | tf_op jit(solution)/shard_map/ppermute | solution.py:175
  23.4 136.7 %collective-permute-start.4 = (bf16[48,4,32,512]{3,2,1,0:T(8,128)(2,1)}, bf16[48,4,32,512]{3,2,1,0:T(8,128)(2,1)}, u32[]{:S(2)}, u32[]{:S(2)}) collective-permute-start(bf16[48,4,32,512]{3,2,1,0:T(8,128)(2,1)} %bitcast.35.refs_3_.refs_4_.refs_8_.refs_16_), channel_id=1, source_target_pairs={{0,4},{4,0},{1,5},{5,1},{2,6},{6,2},{3,7},{7,3},{8,12},{12,8},{9,1... | collective-permute-start | bytes 18874376 | tf_op jit(solution)/shard_map/ppermute | solution.py:175
  36.5 109.0 %collective-permute-start = (bf16[8,48,32,128]{3,2,1,0:T(8,128)(2,1)}, bf16[8,48,32,128]{3,2,1,0:T(8,128)(2,1)S(1)}, u32[]{:S(2)}, u32[]{:S(2)}) collective-permute-start(bf16[8,48,32,128]{3,2,1,0:T(8,128)(2,1)} %get-tuple-element.26), channel_id=1, source_target_pairs={{0,8},{8,0},{16,24},{24,16},{1,9},{9,1},{17,25},{25,17},{2,10},{10... | collective-permute-start | bytes 9437192 | tf_op jit(solution)/shard_map/ppermute | solution.py:175
  43.8 3.6 copy-start.13
  47.4 96.8 %collective-permute-start.5 = (bf16[1,48,32,128]{3,2,1,0:T(8,128)(2,1)S(1)}, bf16[1,48,32,128]{3,2,1,0:T(8,128)(2,1)S(1)}, u32[]{:S(2)}, u32[]{:S(2)}) collective-permute-start(bf16[1,48,32,128]{3,2,1,0:T(8,128)(2,1)S(1)} %copy-done.13), channel_id=1, source_target_pairs={{0,16},{8,24},{16,0},{24,8},{1,17},{9,25},{17,1},{25,9},{2,18},{10... | collective-permute-start | bytes 1179656 | tf_op jit(solution)/shard_map/ppermute | solution.py:175
  144.1 16.0 %copy-start.15 = (bf16[1,48,32,128]{3,2,1,0:T(8,128)(2,1)}, bf16[1,48,32,128]{3,2,1,0:T(8,128)(2,1)S(1)}, u32[]{:S(2)}) copy-start(bf16[1,48,32,128]{3,2,1,0:T(8,128)(2,1)S(1)} %collective-permute-done.5.refs_1_.refs_8_) | copy-start | bytes 1179652
  144.1 22.9 %collective-permute-start.3 = (bf16[48,4,32,512]{3,2,1,0:T(8,128)(2,1)}, bf16[48,4,32,512]{3,2,1,0:T(8,128)(2,1)}, u32[]{:S(2)}, u32[]{:S(2)}) collective-permute-start(bf16[48,4,32,512]{3,2,1,0:T(8,128)(2,1)} %bitcast.35.refs_3_.refs_4_.refs_8_.refs_16_), channel_id=1, source_target_pairs={{0,2},{2,0},{1,3},{3,1},{4,6},{6,4},{5,7},{7,5},{8,10},{10,8},{9,1... | collective-permute-start | bytes 18874376 | tf_op jit(solution)/shard_map/ppermute | solution.py:175
  145.5 14.7 %copy-start.5 = (bf16[8,48,32,128]{3,2,1,0:T(8,128)(2,1)}, bf16[8,48,32,128]{3,2,1,0:T(8,128)(2,1)S(1)}, u32[]{:S(2)}) copy-start(bf16[8,48,32,128]{3,2,1,0:T(8,128)(2,1)S(1)} %collective-permute-done.refs_5_.refs_1_.refs_2_.refs_3_.refs_4_.refs_6_.refs_7_) | copy-start | bytes 9437188
  160.1 1.1 copy-start.9
  160.2 10.6 %collective-permute-start.9 = (bf16[48,4,32,512]{3,2,1,0:T(8,128)(2,1)}, bf16[48,4,32,512]{3,2,1,0:T(8,128)(2,1)}, u32[]{:S(2)}, u32[]{:S(2)}) collective-permute-start(bf16[48,4,32,512]{3,2,1,0:T(8,128)(2,1)} %gate.5.refs_6_.refs_10_.refs_18_), channel_id=1, source_target_pairs={{0,2},{2,0},{1,3},{3,1},{4,6},{6,4},{5,7},{7,5},{8,10},{10,8},{9,1... | collective-permute-start | bytes 18874376 | tf_op jit(solution)/shard_map/ppermute | solution.py:175
  161.3 72.0 %collective-permute-start.12 = (bf16[2,48,32,128]{3,2,1,0:T(8,128)(2,1)S(1)}, bf16[2,48,32,128]{3,2,1,0:T(8,128)(2,1)}, u32[]{:S(2)}, u32[]{:S(2)}) collective-permute-start(bf16[2,48,32,128]{3,2,1,0:T(8,128)(2,1)S(1)} %copy-done.9), channel_id=1, source_target_pairs={{0,16},{8,24},{16,0},{24,8},{1,17},{9,25},{17,1},{25,9},{2,18},{10... | collective-permute-start | bytes 2359304 | tf_op jit(solution)/shard_map/ppermute | solution.py:175
  163.5 42.8 %collective-permute-start.13 = (bf16[2,48,32,128]{3,2,1,0:T(8,128)(2,1)}, bf16[2,48,32,128]{3,2,1,0:T(8,128)(2,1)}, u32[]{:S(2)}, u32[]{:S(2)}) collective-permute-start(bf16[2,48,32,128]{3,2,1,0:T(8,128)(2,1)} %get-tuple-element.34), channel_id=1, source_target_pairs={{0,24},{8,16},{16,8},{24,0},{1,25},{9,17},{17,9},{25,1},{2,26},{10... | collective-permute-start | bytes 2359304 | tf_op jit(solution)/shard_map/ppermute | solution.py:175
  199.1 53.7 %collective-permute-start.14 = (f32[2,2,2,4,4,32,128]{6,5,4,3,2,1,0:T(8,128)}, f32[2,2,2,4,4,32,128]{6,5,4,3,2,1,0:T(8,128)S(1)}, u32[]{:S(2)}, u32[]{:S(2)}) collective-permute-start(f32[2,2,2,4,4,32,128]{6,5,4,3,2,1,0:T(8,128)} %dynamic-slice_bitcast_fusion), channel_id=1, source_target_pairs={{0,1},{1,0},{2,3},{3,2},{4,5},{5,4},{6,7},{7,6},{8,9},{9,8},{10,11... | collective-permute-start | bytes 6291464 | tf_op jit(solution)/shard_map/ppermute | solution.py:175
  200.6 77.1 %collective-permute-start.10 = (bf16[1,48,32,128]{3,2,1,0:T(8,128)(2,1)}, bf16[1,48,32,128]{3,2,1,0:T(8,128)(2,1)}, u32[]{:S(2)}, u32[]{:S(2)}) collective-permute-start(bf16[1,48,32,128]{3,2,1,0:T(8,128)(2,1)} %get-tuple-element.32.refs_7_), channel_id=1, source_target_pairs={{0,16},{8,24},{16,0},{24,8},{1,17},{9,25},{17,1},{25,9},{2,18},{10... | collective-permute-start | bytes 1179656 | tf_op jit(solution)/shard_map/ppermute | solution.py:175
  202.9 74.7 %collective-permute-start.11 = (bf16[1,48,32,128]{3,2,1,0:T(8,128)(2,1)}, bf16[1,48,32,128]{3,2,1,0:T(8,128)(2,1)}, u32[]{:S(2)}, u32[]{:S(2)}) collective-permute-start(bf16[1,48,32,128]{3,2,1,0:T(8,128)(2,1)} %get-tuple-element.33), channel_id=1, source_target_pairs={{0,24},{8,16},{16,8},{24,0},{1,25},{9,17},{17,9},{25,1},{2,26},{10... | collective-permute-start | bytes 1179656 | tf_op jit(solution)/shard_map/ppermute | solution.py:175
  256.2 1.5 copy-start.14
  256.2 21.3 %copy-start = (f32[2,2,2,4,4,32,128]{6,5,4,3,2,1,0:T(8,128)S(1)}, f32[2,2,2,4,4,32,128]{6,5,4,3,2,1,0:T(8,128)}, u32[]{:S(2)}) copy-start(f32[2,2,2,4,4,32,128]{6,5,4,3,2,1,0:T(8,128)} %bitcast_add_fusion.refs_1_) | copy-start | bytes 6291460
  256.2 39.9 %collective-permute-start.15 = (f32[2,2,2,4,2,32,128]{6,5,4,3,2,1,0:T(8,128)}, f32[2,2,2,4,2,32,128]{6,5,4,3,2,1,0:T(8,128)}, u32[]{:S(2)}, u32[]{:S(2)}) collective-permute-start(f32[2,2,2,4,2,32,128]{6,5,4,3,2,1,0:T(8,128)} %gate.6), channel_id=1, source_target_pairs={{0,1},{1,0},{2,3},{3,2},{4,5},{5,4},{6,7},{7,6},{8,9},{9,8},{10,11... | collective-permute-start | bytes 3145736 | tf_op jit(solution)/shard_map/ppermute | solution.py:175
  257.7 70.1 %collective-permute-start.1 = (bf16[1,48,32,128]{3,2,1,0:T(8,128)(2,1)S(1)}, bf16[1,48,32,128]{3,2,1,0:T(8,128)(2,1)}, u32[]{:S(2)}, u32[]{:S(2)}) collective-permute-start(bf16[1,48,32,128]{3,2,1,0:T(8,128)(2,1)S(1)} %copy-done.14), channel_id=1, source_target_pairs={{0,16},{8,24},{16,0},{24,8},{1,17},{9,25},{17,1},{25,9},{2,18},{10... | collective-permute-start | bytes 1179656 | tf_op jit(solution)/shard_map/ppermute | solution.py:175
  275.4 52.4 %collective-permute-start.2 = (bf16[1,48,32,128]{3,2,1,0:T(8,128)(2,1)}, bf16[1,48,32,128]{3,2,1,0:T(8,128)(2,1)}, u32[]{:S(2)}, u32[]{:S(2)}) collective-permute-start(bf16[1,48,32,128]{3,2,1,0:T(8,128)(2,1)} %get-tuple-element.28), channel_id=1, source_target_pairs={{0,24},{8,16},{16,8},{24,0},{1,25},{9,17},{17,9},{25,1},{2,26},{10... | collective-permute-start | bytes 1179656 | tf_op jit(solution)/shard_map/ppermute | solution.py:175
  277.6 47.6 %collective-permute-start.16 = (f32[2,2,4,4,32,128]{5,4,3,2,1,0:T(8,128)S(1)}, f32[2,2,4,4,32,128]{5,4,3,2,1,0:T(8,128)}, u32[]{:S(2)}, u32[]{:S(2)}) collective-permute-start(f32[2,2,4,4,32,128]{5,4,3,2,1,0:T(8,128)S(1)} %dynamic-slice_bitcast_fusion.1), channel_id=1, source_target_pairs={{0,8},{8,0},{16,24},{24,16},{1,9},{9,1},{17,25},{25,17},{2,10},{10... | collective-permute-start | bytes 3145736 | tf_op jit(solution)/shard_map/ppermute | solution.py:175
  291.8 50.3 %all-to-all-start.1 = ((bf16[32,2,32,128]{3,2,1,0:T(8,128)(2,1)}), bf16[32,2,32,128]{3,2,1,0:T(8,128)(2,1)}, u32[]{:S(2)}, u32[]{:S(2)}) async-start(bf16[32,2,32,128]{3,2,1,0:T(8,128)(2,1)} %bitcast.50), calls=%async_computation.1 | async-start | bytes 1048576 | tf_op jit(solution)/shard_map/all_to_all | solution.py:312
  297.8 28.9 %copy-start.3 = (f32[2,2,2,4,2,32,128]{6,5,4,3,2,1,0:T(8,128)}, f32[2,2,2,4,2,32,128]{6,5,4,3,2,1,0:T(8,128)S(1)}, u32[]{:S(2)}) copy-start(f32[2,2,2,4,2,32,128]{6,5,4,3,2,1,0:T(8,128)S(1)} %bitcast_add_fusion.2) | copy-start | bytes 3145732
  326.7 1.1 copy-start.1
  327.5 19.9 %collective-permute-start.22 = (bf16[2,4,4,32,128]{4,3,2,1,0:T(8,128)(2,1)}, bf16[2,4,4,32,128]{4,3,2,1,0:T(8,128)(2,1)}, u32[]{:S(2)}, u32[]{:S(2)}) collective-permute-start(bf16[2,4,4,32,128]{4,3,2,1,0:T(8,128)(2,1)} %fusion), channel_id=1, source_target_pairs={{0,16},{8,24},{16,0},{24,8},{1,17},{9,25},{17,1},{25,9},{2,18},{10... | collective-permute-start | bytes 786440 | tf_op jit(solution)/shard_map/ppermute | solution.py:175
  327.8 19.7 %copy-start.2 = (f32[2,2,4,4,32,128]{5,4,3,2,1,0:T(8,128)S(1)}, f32[2,2,4,4,32,128]{5,4,3,2,1,0:T(8,128)}, u32[]{:S(2)}) copy-start(f32[2,2,4,4,32,128]{5,4,3,2,1,0:T(8,128)} %copy-done.1) | copy-start | bytes 3145732
  327.8 22.4 %collective-permute-start.17 = (f32[2,2,4,2,32,128]{5,4,3,2,1,0:T(8,128)}, f32[2,2,4,2,32,128]{5,4,3,2,1,0:T(8,128)S(1)}, u32[]{:S(2)}, u32[]{:S(2)}) collective-permute-start(f32[2,2,4,2,32,128]{5,4,3,2,1,0:T(8,128)} %gate.7), channel_id=1, source_target_pairs={{0,8},{8,0},{16,24},{24,16},{1,9},{9,1},{17,25},{25,17},{2,10},{10... | collective-permute-start | bytes 1572872 | tf_op jit(solution)/shard_map/ppermute | solution.py:175
  342.1 8.1 %copy-start.4 = (f32[2,2,2,4,2,32,128]{6,5,4,3,2,1,0:T(8,128)S(1)}, f32[2,2,2,4,2,32,128]{6,5,4,3,2,1,0:T(8,128)}, u32[]{:S(2)}) copy-start(f32[2,2,2,4,2,32,128]{6,5,4,3,2,1,0:T(8,128)} %copy-done.3) | copy-start | bytes 3145732
  342.1 53.9 %all-to-all-start = ((bf16[32,2,32,128]{3,2,1,0:T(8,128)(2,1)}), bf16[32,2,32,128]{3,2,1,0:T(8,128)(2,1)S(1)}, u32[]{:S(2)}, u32[]{:S(2)}) async-start(bf16[32,2,32,128]{3,2,1,0:T(8,128)(2,1)} %bitcast.49), calls=%async_computation | async-start | bytes 1048576 | tf_op jit(solution)/shard_map/all_to_all | solution.py:312
  348.5 30.2 %copy-start.7 = (f32[2,4,4,32,128]{4,3,2,1,0:T(8,128)}, f32[2,4,4,32,128]{4,3,2,1,0:T(8,128)S(1)}, u32[]{:S(2)}) copy-start(f32[2,4,4,32,128]{4,3,2,1,0:T(8,128)S(1)} %bitcast_add_fusion.3.refs_0_) | copy-start | bytes 1572868
  348.5 21.2 %collective-permute-start.25 = (f32[2,4,4,32,128]{4,3,2,1,0:T(8,128)S(1)}, f32[2,4,4,32,128]{4,3,2,1,0:T(8,128)S(1)}, u32[]{:S(2)}, u32[]{:S(2)}) collective-permute-start(f32[2,4,4,32,128]{4,3,2,1,0:T(8,128)S(1)} %bitcast_add_fusion.3.refs_0_), channel_id=1, source_target_pairs={{0,6},{2,4},{4,2},{6,0},{1,7},{3,5},{5,3},{7,1},{8,14},{10,12},{12... | collective-permute-start | bytes 1572872 | tf_op jit(solution)/shard_map/ppermute | solution.py:308
  350.3 17.8 %collective-permute-start.18 = (bf16[2,4,2,32,128]{4,3,2,1,0:T(8,128)(2,1)S(1)}, bf16[2,4,2,32,128]{4,3,2,1,0:T(8,128)(2,1)S(1)}, u32[]{:S(2)}, u32[]{:S(2)}) collective-permute-start(bf16[2,4,2,32,128]{4,3,2,1,0:T(8,128)(2,1)S(1)} %fusion.1), channel_id=1, source_target_pairs={{0,16},{8,24},{16,0},{24,8},{1,17},{9,25},{17,1},{25,9},{2,18},{10... | collective-permute-start | bytes 393224 | tf_op jit(solution)/shard_map/ppermute | solution.py:175
  352.7 26.0 %collective-permute-start.24 = (f32[2,4,4,32,128]{4,3,2,1,0:T(8,128)S(1)}, f32[2,4,4,32,128]{4,3,2,1,0:T(8,128)S(1)}, u32[]{:S(2)}, u32[]{:S(2)}) collective-permute-start(f32[2,4,4,32,128]{4,3,2,1,0:T(8,128)S(1)} %bitcast_add_fusion.3.refs_0_), channel_id=1, source_target_pairs={{0,4},{2,6},{4,0},{6,2},{1,5},{3,7},{5,1},{7,3},{8,12},{10,14},{12... | collective-permute-start | bytes 1572872 | tf_op jit(solution)/shard_map/ppermute | solution.py:308
  353.3 25.4 %collective-permute-start.23 = (f32[2,4,4,32,128]{4,3,2,1,0:T(8,128)S(1)}, f32[2,4,4,32,128]{4,3,2,1,0:T(8,128)S(1)}, u32[]{:S(2)}, u32[]{:S(2)}) collective-permute-start(f32[2,4,4,32,128]{4,3,2,1,0:T(8,128)S(1)} %bitcast_add_fusion.3.refs_0_), channel_id=1, source_target_pairs={{0,2},{2,0},{4,6},{6,4},{1,3},{3,1},{5,7},{7,5},{8,10},{10,8},{12,... | collective-permute-start | bytes 1572872 | tf_op jit(solution)/shard_map/ppermute | solution.py:308
  368.1 21.5 %copy-start.8 = (f32[2,4,2,32,128]{4,3,2,1,0:T(8,128)}, f32[2,4,2,32,128]{4,3,2,1,0:T(8,128)S(1)}, u32[]{:S(2)}) copy-start(f32[2,4,2,32,128]{4,3,2,1,0:T(8,128)S(1)} %bitcast_add_fusion.5.refs_0_) | copy-start | bytes 786436
  368.1 16.9 %collective-permute-start.21 = (f32[2,4,2,32,128]{4,3,2,1,0:T(8,128)S(1)}, f32[2,4,2,32,128]{4,3,2,1,0:T(8,128)S(1)}, u32[]{:S(2)}, u32[]{:S(2)}) collective-permute-start(f32[2,4,2,32,128]{4,3,2,1,0:T(8,128)S(1)} %bitcast_add_fusion.5.refs_0_), channel_id=1, source_target_pairs={{0,6},{2,4},{4,2},{6,0},{1,7},{3,5},{5,3},{7,1},{8,14},{10,12},{12... | collective-permute-start | bytes 786440 | tf_op jit(solution)/shard_map/ppermute | solution.py:308
  368.9 20.7 %collective-permute-start.20 = (f32[2,4,2,32,128]{4,3,2,1,0:T(8,128)S(1)}, f32[2,4,2,32,128]{4,3,2,1,0:T(8,128)S(1)}, u32[]{:S(2)}, u32[]{:S(2)}) collective-permute-start(f32[2,4,2,32,128]{4,3,2,1,0:T(8,128)S(1)} %bitcast_add_fusion.5.refs_0_), channel_id=1, source_target_pairs={{0,4},{2,6},{4,0},{6,2},{1,5},{3,7},{5,1},{7,3},{8,12},{10,14},{12... | collective-permute-start | bytes 786440 | tf_op jit(solution)/shard_map/ppermute | solution.py:308
  369.7 8.9 %copy-start.10 = (f32[2,4,4,32,128]{4,3,2,1,0:T(8,128)}, f32[2,4,4,32,128]{4,3,2,1,0:T(8,128)S(1)}, u32[]{:S(2)}) copy-start(f32[2,4,4,32,128]{4,3,2,1,0:T(8,128)S(1)} %collective-permute-done.25.refs_3_) | copy-start | bytes 1572868
  369.8 19.9 %collective-permute-start.19 = (f32[2,4,2,32,128]{4,3,2,1,0:T(8,128)S(1)}, f32[2,4,2,32,128]{4,3,2,1,0:T(8,128)S(1)}, u32[]{:S(2)}, u32[]{:S(2)}) collective-permute-start(f32[2,4,2,32,128]{4,3,2,1,0:T(8,128)S(1)} %bitcast_add_fusion.5.refs_0_), channel_id=1, source_target_pairs={{0,2},{2,0},{4,6},{6,4},{1,3},{3,1},{5,7},{7,5},{8,10},{10,8},{12,... | collective-permute-start | bytes 786440 | tf_op jit(solution)/shard_map/ppermute | solution.py:308
  378.7 0.8 copy-start.11
  379.5 0.8 copy-start.12
  385.1 4.6 %copy-start.16 = (f32[2,4,2,32,128]{4,3,2,1,0:T(8,128)}, f32[2,4,2,32,128]{4,3,2,1,0:T(8,128)S(1)}, u32[]{:S(2)}) copy-start(f32[2,4,2,32,128]{4,3,2,1,0:T(8,128)S(1)} %collective-permute-done.21.refs_3_) | copy-start | bytes 786436
  389.7 0.7 copy-start.17
  390.4 0.7 copy-start.18
  396.0 0.8 copy-start.6

commit v4 on v3

--- a/solution.py
+++ b/solution.py
@@ -263,10 +263,14 @@
     amps = amplitudes.reshape(ni, la * lk, full_c)
     counts = CHUNKS
     starts = [sum(counts[:n]) for n in range(len(counts))]
-    parts = [prep(amps, place, la, lk, s, c, (2, 3)) for s, c in zip(starts, counts)]
-    integrals, *parts[0] = lax.optimization_barrier((integrals, *parts[0]))
+    first = prep(amps, place, la, lk, 0, counts[0], (2, 3))
+    integrals, *first = lax.optimization_barrier((integrals, *first))
+    w_own = jnp.transpose(integrals, (0, 2, 1, 3))
+    (next_place,) = gated((place,), w_own)
+    parts = [first]
+    for s, c in zip(starts[1:], counts[1:]):
+        parts.append(prep(amps, next_place, la, lk, s, c, (2, 3)))
     moved = [(swapped(two, "z", 2), swapped(three, "z", 3)) for two, three in parts]
-    w_own = jnp.transpose(integrals, (0, 2, 1, 3))
     w_x = swapped(w_own, "x")
     w_core = swapped(w_own, "core")
     (later,) = gated((place,), parts[0][0], parts[1][0], w_own)

time: 400 us -> 393 us (0.983)
  waiting for transfers between devices: 163 us -> 156 us
    ppermute x20, waiting for transfers between devices: 149 us -> 143 us  [swapped(): return lax.ppermute(x, axis, [(s, s ^ bits) for s in range(n)])]
  transfers between devices with their start and end apart: 28 -> 28, of which waited for: 9 -> 9; matrix products, arithmetic and copies ran while one was open for 6% -> 6% of each run, Pallas kernels for 27% -> 28%
where the time goes in v4:
time: 393 us; the launch traced here: 392 us
  waiting for transfers between devices  156 us (40%)
  Pallas kernels  114 us (29%)
  starting transfers between devices  90.9 us (23%)
  local copies, waits for them, and re-layouts  22.5 us (6%)
  other arithmetic  8.4 us (2%)
    ppermute x20, waiting for transfers between devices, swapped(): return lax.ppermute(x, axis, [(s, s ^ bits) for s in range(n)])  143 us
    ppermute x20, starting transfers between devices, swapped(): return lax.ppermute(x, axis, [(s, s ^ bits) for s in range(n)])  80.9 us
    pallas_call x4, Pallas kernels, product(): pl.pallas_call(functools.partial(product_kernel, store, ni, kb, la, nj),...  70.6 us
    pallas_call x6, Pallas kernels, prep(): pl.pallas_call(functools.partial(prep_kernel, la, lk, n), out_shape=[out]...  31.4 us
    ppermute x6, waiting for transfers between devices, tiled_body(): pieces.append(lax.ppermute(total, ('x', 'core'), pairs))  13.1 us
  transfers between devices with their start and end apart: 28, of which 9 were waited for; matrix products, arithmetic and copies ran while one was open for 6% of the time, Pallas kernels for 28%

profile of v4, /device:TPU:0, one launch (start us, length us, event | category | flops | bytes accessed | tf_op | source)
XLA Modules:
  0.0 391.7 jit_solution(10154772307334044189)
XLA Ops:
  0.7 3.5 prep.6
  4.2 5.0 %collective-permute-start.6 = (bf16[1,48,32,128]{3,2,1,0:T(8,128)(2,1)}, bf16[1,48,32,128]{3,2,1,0:T(8,128)(2,1)}, u32[]{:S(2)}, u32[]{:S(2)}) collective-permute-start(bf16[1,48,32,128]{3,2,1,0:T(8,128)(2,1)} %get-tuple-element.29), channel_id=1, source_target_pairs={{0,24},{8,16},{16,8},{24,0},{1,25},{9,17},{17,9},{25,1},{2,26},{10... | collective-permute-start | bytes 1179656 | tf_op jit(solution)/shard_map/ppermute | solution.py:175
  9.7 7.6 %copy.13 = bf16[48,32,4,512]{3,1,2,0:T(8,128)(2,1)} copy(bf16[48,32,4,512]{3,2,1,0:T(4,128)(2,1)} %param.3) | data formatting | bytes 12582912 | tf_op jit(solution)/shard_map/optimization_barrier | solution.py:267
  17.3 1.5 collective-permute-start.4
  18.8 5.9 %prep.7 = (bf16[3,48,32,128]{3,2,1,0:T(8,128)(2,1)}, bf16[3,48,32,128]{3,2,1,0:T(8,128)(2,1)}) custom-call(s32[3]{0:T(128)} %gate.5.place, f32[8,1536,512]{2,1,0:T(8,128)} %bitcast.38, f32[8,1536,512]{2,1,0:T(8,128)} %bitcast.39), custom_call_target="tpu_custom_call" | custom-call | flops 30000001024 | bytes 1000 | tf_op jit(solution)/shard_map/prep/pallas_call | solution.py:62
  26.2 11.1 %prep.8 = (bf16[8,48,32,128]{3,2,1,0:T(8,128)(2,1)}, bf16[8,48,32,128]{3,2,1,0:T(8,128)(2,1)}) custom-call(s32[3]{0:T(128)} %gate.6.place, f32[8,1536,512]{2,1,0:T(8,128)} %bitcast.40, f32[8,1536,512]{2,1,0:T(8,128)} %bitcast.41), custom_call_target="tpu_custom_call" | custom-call | flops 80000000000 | bytes 1000 | tf_op jit(solution)/shard_map/prep/pallas_call | solution.py:62
  37.3 3.4 collective-permute-start
  40.7 3.9 %prep.10 = (bf16[2,48,32,128]{3,2,1,0:T(8,128)(2,1)}, bf16[2,48,32,128]{3,2,1,0:T(8,128)(2,1)}) custom-call(s32[3]{0:T(128)} %gate.5.place, f32[8,1536,512]{2,1,0:T(8,128)} %bitcast.42, f32[8,1536,512]{2,1,0:T(8,128)} %bitcast.43), custom_call_target="tpu_custom_call" | custom-call | flops 20000000000 | bytes 1000 | tf_op jit(solution)/shard_map/prep/pallas_call | solution.py:62
  44.6 3.6 prep.11
  48.2 30.4 %collective-permute-start.5 = (bf16[1,48,32,128]{3,2,1,0:T(8,128)(2,1)S(1)}, bf16[1,48,32,128]{3,2,1,0:T(8,128)(2,1)S(1)}, u32[]{:S(2)}, u32[]{:S(2)}) collective-permute-start(bf16[1,48,32,128]{3,2,1,0:T(8,128)(2,1)S(1)} %copy-done.13), channel_id=1, source_target_pairs={{0,16},{8,24},{16,0},{24,8},{1,17},{9,25},{17,1},{25,9},{2,18},{10... | collective-permute-start | bytes 1179656 | tf_op jit(solution)/shard_map/ppermute | solution.py:175
  78.6 3.4 prep.9
  82.0 69.1 %collective-permute-done.5.refs_1_.refs_8_ = bf16[1,48,32,128]{3,2,1,0:T(8,128)(2,1)S(1)} collective-permute-done((bf16[1,48,32,128]{3,2,1,0:T(8,128)(2,1)S(1)}, bf16[1,48,32,128]{3,2,1,0:T(8,128)(2,1)S(1)}, u32[]{:S(2)}, u32[]{:S(2)}) %collective-permute-start.5) | collective-permute-done | bytes 393248 | tf_op jit(solution)/shard_map/ppermute | solution.py:175
  151.1 4.0 %collective-permute-done.refs_5_.refs_1_.refs_2_.refs_3_.refs_4_.refs_6_.refs_7_ = bf16[8,48,32,128]{3,2,1,0:T(8,128)(2,1)S(1)} collective-permute-done((bf16[8,48,32,128]{3,2,1,0:T(8,128)(2,1)}, bf16[8,48,32,128]{3,2,1,0:T(8,128)(2,1)S(1)}, u32[]{:S(2)}, u32[]{:S(2)}) %collective-permute-start) | collective-permute-done | bytes 3145760 | tf_op jit(solution)/shard_map/ppermute | solution.py:175
  155.1 1.6 copy-done.5
  156.8 1.1 copy-done.9
  157.9 3.0 collective-permute-start.13
  161.6 9.0 %collective-permute-done.9.refs_7_.refs_11_.refs_19_ = bf16[48,4,32,512]{3,2,1,0:T(8,128)(2,1)} collective-permute-done((bf16[48,4,32,512]{3,2,1,0:T(8,128)(2,1)}, bf16[48,4,32,512]{3,2,1,0:T(8,128)(2,1)}, u32[]{:S(2)}, u32[]{:S(2)}) %collective-permute-start.9) | collective-permute-done | bytes 6291488 | tf_op jit(solution)/shard_map/ppermute | solution.py:175
  170.6 25.2 %product.7 = f32[2,2,2,2,4,4,32,128]{7,6,5,4,3,2,1,0:T(8,128)} custom-call(s32[3]{0:T(128)} %pad_add_fusion.place, bf16[8,48,32,128]{3,2,1,0:T(8,128)(2,1)} %get-tuple-element.25.refs_0_.refs_1_.refs_2_.refs_3_, bf16[8,48,32,128]{3,2,1,0:T(8,128)(2,1)} %get-tuple-element.25.refs_0_.refs_1_.refs_2_.refs_3_, ...), custom_call_target="tpu_custom_call" | custom-call | flops 38654705664 | bytes 1000 | tf_op jit(solution)/shard_map/product/pallas_call | solution.py:139
  195.7 3.2 dynamic-slice_bitcast_fusion
  198.9 1.5 collective-permute-start.14
  200.5 3.4 collective-permute-start.10
  203.8 3.5 collective-permute-start.11
  207.4 22.1 %collective-permute-done.12.refs_4_.refs_5_ = bf16[2,48,32,128]{3,2,1,0:T(8,128)(2,1)} collective-permute-done((bf16[2,48,32,128]{3,2,1,0:T(8,128)(2,1)S(1)}, bf16[2,48,32,128]{3,2,1,0:T(8,128)(2,1)}, u32[]{:S(2)}, u32[]{:S(2)}) %collective-permute-start.12) | collective-permute-done | bytes 786464 | tf_op jit(solution)/shard_map/ppermute | solution.py:175
  229.5 17.2 %product.6 = f32[2,2,2,2,4,2,32,128]{7,6,5,4,3,2,1,0:T(8,128)} custom-call(s32[3]{0:T(128)} %pad_add_fusion.place, bf16[8,48,32,128]{3,2,1,0:T(8,128)(2,1)} %get-tuple-element.25.refs_0_.refs_1_.refs_2_.refs_3_, bf16[8,48,32,128]{3,2,1,0:T(8,128)(2,1)} %get-tuple-element.25.refs_0_.refs_1_.refs_2_.refs_3_, bf16[8,48,32,128]{3,2,1,0:T(8,128)(2,1)} %copy-done.5, ...), custom_call_target="tpu_custom_call" | custom-call | flops 19327352832 | bytes 1000 | tf_op jit(solution)/shard_map/product/pallas_call | solution.py:139
  246.7 2.3 dynamic-slice_bitcast_fusion.2.refs_0_
  249.0 3.4 bitcast_add_fusion.refs_1_
  252.4 1.5 collective-permute-start.15
  253.9 16.5 %collective-permute-start.1 = (bf16[1,48,32,128]{3,2,1,0:T(8,128)(2,1)S(1)}, bf16[1,48,32,128]{3,2,1,0:T(8,128)(2,1)}, u32[]{:S(2)}, u32[]{:S(2)}) collective-permute-start(bf16[1,48,32,128]{3,2,1,0:T(8,128)(2,1)S(1)} %copy-done.14), channel_id=1, source_target_pairs={{0,16},{8,24},{16,0},{24,8},{1,17},{9,25},{17,1},{25,9},{2,18},{10... | collective-permute-start | bytes 1179656 | tf_op jit(solution)/shard_map/ppermute | solution.py:175
  270.4 3.3 collective-permute-start.2
  273.9 14.1 %product.5 = bf16[4,4,2,2,32,128]{5,4,3,2,1,0:T(8,128)(2,1)} custom-call(s32[3]{0:T(128)} %pad_add_fusion.place, bf16[8,48,32,128]{3,2,1,0:T(8,128)(2,1)} %get-tuple-element.25.refs_0_.refs_1_.refs_2_.refs_3_, bf16[8,48,32,128]{3,2,1,0:T(8,128)(2,1)} %copy-done.5, bf16[1,48,32,128]{3,2,1,0:T(8,128)(2,1)} %collective-permute-done.10.refs_2_, ...), custom_call_target="tpu_custom_call" | custom-call | flops 9663676416 | bytes 1000 | tf_op jit(solution)/shard_map/product/pallas_call | solution.py:139
  288.0 3.3 all-to-all-start.1
  291.3 1.8 bitcast_add_fusion.2
  294.0 23.3 %collective-permute-done.16 = f32[2,2,4,4,32,128]{5,4,3,2,1,0:T(8,128)} collective-permute-done((f32[2,2,4,4,32,128]{5,4,3,2,1,0:T(8,128)S(1)}, f32[2,2,4,4,32,128]{5,4,3,2,1,0:T(8,128)}, u32[]{:S(2)}, u32[]{:S(2)}) %collective-permute-start.16) | collective-permute-done | bytes 1048608 | tf_op jit(solution)/shard_map/ppermute | solution.py:175
  317.3 1.4 bitcast_add_fusion.1.refs_1_
  319.6 1.5 collective-permute-start.22
  321.1 2.6 collective-permute-start.17
  323.7 14.1 %product.4 = bf16[4,4,2,2,32,128]{5,4,3,2,1,0:T(8,128)(2,1)} custom-call(s32[3]{0:T(128)} %pad_add_fusion.place, bf16[8,48,32,128]{3,2,1,0:T(8,128)(2,1)} %get-tuple-element.25.refs_0_.refs_1_.refs_2_.refs_3_, bf16[8,48,32,128]{3,2,1,0:T(8,128)(2,1)} %copy-done.5, bf16[1,48,32,128]{3,2,1,0:T(8,128)(2,1)} %collective-permute-done.1.refs_2_, ...), custom_call_target="tpu_custom_call" | custom-call | flops 9663676416 | bytes 1000 | tf_op jit(solution)/shard_map/product/pallas_call | solution.py:139
  337.9 2.8 all-to-all-start
  340.6 1.0 bitcast_add_fusion.3.refs_0_
  341.7 1.5 collective-permute-start.25
  343.3 2.6 collective-permute-start.18
  346.4 14.8 %collective-permute-done.18 = bf16[2,4,2,32,128]{4,3,2,1,0:T(8,128)(2,1)S(1)} collective-permute-done((bf16[2,4,2,32,128]{4,3,2,1,0:T(8,128)(2,1)S(1)}, bf16[2,4,2,32,128]{4,3,2,1,0:T(8,128)(2,1)S(1)}, u32[]{:S(2)}, u32[]{:S(2)}) %collective-permute-start.18) | collective-permute-done | bytes 131104 | tf_op jit(solution)/shard_map/ppermute | solution.py:175
  363.2 8.4 %collective-permute-done.24.refs_2_ = f32[2,4,4,32,128]{4,3,2,1,0:T(8,128)S(1)} collective-permute-done((f32[2,4,4,32,128]{4,3,2,1,0:T(8,128)S(1)}, f32[2,4,4,32,128]{4,3,2,1,0:T(8,128)S(1)}, u32[]{:S(2)}, u32[]{:S(2)}) %collective-permute-start.24) | collective-permute-done | bytes 524320 | tf_op jit(solution)/shard_map/ppermute | solution.py:312
  373.2 4.8 %finish.2.refs_4_ = f32[8,4,32,256]{3,2,1,0:T(8,128)} custom-call(s32[3]{0:T(128)} %pad_add_fusion.place, f32[2,4,4,32,128]{4,3,2,1,0:T(8,128)} %copy-done.7, f32[2,4,4,32,128]{4,3,2,1,0:T(8,128)} %copy-done.12, f32[2,4,4,32,128]{4,3,2,1,0:T(8,128)} %copy-done.11, f32[2,4,4,32,128]{4,3,2,1,0:T(8,128)} %copy-done.10), custom_call_target="tpu_custom_call" | custom-call | flops 1000 | bytes 1000 | tf_op jit(solution)/shard_map/finish/pallas_call | solution.py:200
  378.0 4.7 %collective-permute-done.20.refs_2_ = f32[2,4,2,32,128]{4,3,2,1,0:T(8,128)S(1)} collective-permute-done((f32[2,4,2,32,128]{4,3,2,1,0:T(8,128)S(1)}, f32[2,4,2,32,128]{4,3,2,1,0:T(8,128)S(1)}, u32[]{:S(2)}, u32[]{:S(2)}) %collective-permute-start.20) | collective-permute-done | bytes 262176 | tf_op jit(solution)/shard_map/ppermute | solution.py:312
  384.1 3.1 finish.3.before
  387.1 1.9 gather.2.before
  389.8 1.9 gather.3
  (83 shorter events, 11.8 us)
Async XLA Ops:
  0.7 8.6 %copy-start.19 = (s32[3]{0:T(128)S(1)}, s32[3]{0:T(128)}, u32[]{:S(2)}) copy-start(s32[3]{0:T(128)} %pad_add_fusion.place) | copy-start | bytes 40
  4.2 44.0 %collective-permute-start.6 = (bf16[1,48,32,128]{3,2,1,0:T(8,128)(2,1)}, bf16[1,48,32,128]{3,2,1,0:T(8,128)(2,1)}, u32[]{:S(2)}, u32[]{:S(2)}) collective-permute-start(bf16[1,48,32,128]{3,2,1,0:T(8,128)(2,1)} %get-tuple-element.29), channel_id=1, source_target_pairs={{0,24},{8,16},{16,8},{24,0},{1,25},{9,17},{17,9},{25,1},{2,26},{10... | collective-permute-start | bytes 1179656 | tf_op jit(solution)/shard_map/ppermute | solution.py:175
  17.3 137.8 %collective-permute-start.4 = (bf16[48,4,32,512]{3,2,1,0:T(8,128)(2,1)}, bf16[48,4,32,512]{3,2,1,0:T(8,128)(2,1)}, u32[]{:S(2)}, u32[]{:S(2)}) collective-permute-start(bf16[48,4,32,512]{3,2,1,0:T(8,128)(2,1)} %bitcast.35.refs_1_.refs_3_.refs_4_.refs_8_.refs_16_), channel_id=1, source_target_pairs={{0,4},{4,0},{1,5},{5,1},{2,6},{6,2},{3,7},{7,3},{8,12},{12,8},{9,1... | collective-permute-start | bytes 18874376 | tf_op jit(solution)/shard_map/ppermute | solution.py:175
  24.7 126.4 %collective-permute-start.8 = (bf16[3,48,32,128]{3,2,1,0:T(8,128)(2,1)}, bf16[3,48,32,128]{3,2,1,0:T(8,128)(2,1)}, u32[]{:S(2)}, u32[]{:S(2)}) collective-permute-start(bf16[3,48,32,128]{3,2,1,0:T(8,128)(2,1)} %get-tuple-element.30), channel_id=1, source_target_pairs={{0,24},{8,16},{16,8},{24,0},{1,25},{9,17},{17,9},{25,1},{2,26},{10... | collective-permute-start | bytes 3538952 | tf_op jit(solution)/shard_map/ppermute | solution.py:175
  24.9 126.2 %collective-permute-start.7 = (bf16[3,48,32,128]{3,2,1,0:T(8,128)(2,1)}, bf16[3,48,32,128]{3,2,1,0:T(8,128)(2,1)}, u32[]{:S(2)}, u32[]{:S(2)}) collective-permute-start(bf16[3,48,32,128]{3,2,1,0:T(8,128)(2,1)} %get-tuple-element.24.refs_2_), channel_id=1, source_target_pairs={{0,16},{8,24},{16,0},{24,8},{1,17},{9,25},{17,1},{25,9},{2,18},{10... | collective-permute-start | bytes 3538952 | tf_op jit(solution)/shard_map/ppermute | solution.py:175
  37.3 117.7 %collective-permute-start = (bf16[8,48,32,128]{3,2,1,0:T(8,128)(2,1)}, bf16[8,48,32,128]{3,2,1,0:T(8,128)(2,1)S(1)}, u32[]{:S(2)}, u32[]{:S(2)}) collective-permute-start(bf16[8,48,32,128]{3,2,1,0:T(8,128)(2,1)} %get-tuple-element.26), channel_id=1, source_target_pairs={{0,8},{8,0},{16,24},{24,16},{1,9},{9,1},{17,25},{25,17},{2,10},{10... | collective-permute-start | bytes 9437192 | tf_op jit(solution)/shard_map/ppermute | solution.py:175
  44.6 3.6 copy-start.13
  48.2 102.9 %collective-permute-start.5 = (bf16[1,48,32,128]{3,2,1,0:T(8,128)(2,1)S(1)}, bf16[1,48,32,128]{3,2,1,0:T(8,128)(2,1)S(1)}, u32[]{:S(2)}, u32[]{:S(2)}) collective-permute-start(bf16[1,48,32,128]{3,2,1,0:T(8,128)(2,1)S(1)} %copy-done.13), channel_id=1, source_target_pairs={{0,16},{8,24},{16,0},{24,8},{1,17},{9,25},{17,1},{25,9},{2,18},{10... | collective-permute-start | bytes 1179656 | tf_op jit(solution)/shard_map/ppermute | solution.py:175
  151.1 4.0 %copy-start.15 = (bf16[1,48,32,128]{3,2,1,0:T(8,128)(2,1)}, bf16[1,48,32,128]{3,2,1,0:T(8,128)(2,1)S(1)}, u32[]{:S(2)}) copy-start(bf16[1,48,32,128]{3,2,1,0:T(8,128)(2,1)S(1)} %collective-permute-done.5.refs_1_.refs_8_) | copy-start | bytes 1179652
  151.1 10.5 %collective-permute-start.3 = (bf16[48,4,32,512]{3,2,1,0:T(8,128)(2,1)}, bf16[48,4,32,512]{3,2,1,0:T(8,128)(2,1)}, u32[]{:S(2)}, u32[]{:S(2)}) collective-permute-start(bf16[48,4,32,512]{3,2,1,0:T(8,128)(2,1)} %bitcast.35.refs_1_.refs_3_.refs_4_.refs_8_.refs_16_), channel_id=1, source_target_pairs={{0,2},{2,0},{1,3},{3,1},{4,6},{6,4},{5,7},{7,5},{8,10},{10,8},{9,1... | collective-permute-start | bytes 18874376 | tf_op jit(solution)/shard_map/ppermute | solution.py:175
  155.1 1.6 copy-start.5
  156.7 1.1 copy-start.9
  156.7 13.8 %collective-permute-start.9 = (bf16[48,4,32,512]{3,2,1,0:T(8,128)(2,1)}, bf16[48,4,32,512]{3,2,1,0:T(8,128)(2,1)}, u32[]{:S(2)}, u32[]{:S(2)}) collective-permute-start(bf16[48,4,32,512]{3,2,1,0:T(8,128)(2,1)} %gate.7.refs_6_.refs_10_.refs_18_), channel_id=1, source_target_pairs={{0,2},{2,0},{1,3},{3,1},{4,6},{6,4},{5,7},{7,5},{8,10},{10,8},{9,1... | collective-permute-start | bytes 18874376 | tf_op jit(solution)/shard_map/ppermute | solution.py:175
  157.9 71.6 %collective-permute-start.12 = (bf16[2,48,32,128]{3,2,1,0:T(8,128)(2,1)S(1)}, bf16[2,48,32,128]{3,2,1,0:T(8,128)(2,1)}, u32[]{:S(2)}, u32[]{:S(2)}) collective-permute-start(bf16[2,48,32,128]{3,2,1,0:T(8,128)(2,1)S(1)} %copy-done.9), channel_id=1, source_target_pairs={{0,16},{8,24},{16,0},{24,8},{1,17},{9,25},{17,1},{25,9},{2,18},{10... | collective-permute-start | bytes 2359304 | tf_op jit(solution)/shard_map/ppermute | solution.py:175
  157.9 49.5 %collective-permute-start.13 = (bf16[2,48,32,128]{3,2,1,0:T(8,128)(2,1)}, bf16[2,48,32,128]{3,2,1,0:T(8,128)(2,1)}, u32[]{:S(2)}, u32[]{:S(2)}) collective-permute-start(bf16[2,48,32,128]{3,2,1,0:T(8,128)(2,1)} %get-tuple-element.34), channel_id=1, source_target_pairs={{0,24},{8,16},{16,8},{24,0},{1,25},{9,17},{17,9},{25,1},{2,26},{10... | collective-permute-start | bytes 2359304 | tf_op jit(solution)/shard_map/ppermute | solution.py:175
  198.9 50.0 %collective-permute-start.14 = (f32[2,2,2,4,4,32,128]{6,5,4,3,2,1,0:T(8,128)}, f32[2,2,2,4,4,32,128]{6,5,4,3,2,1,0:T(8,128)S(1)}, u32[]{:S(2)}, u32[]{:S(2)}) collective-permute-start(f32[2,2,2,4,4,32,128]{6,5,4,3,2,1,0:T(8,128)} %dynamic-slice_bitcast_fusion), channel_id=1, source_target_pairs={{0,1},{1,0},{2,3},{3,2},{4,5},{5,4},{6,7},{7,6},{8,9},{9,8},{10,11... | collective-permute-start | bytes 6291464 | tf_op jit(solution)/shard_map/ppermute | solution.py:175
  200.5 73.4 %collective-permute-start.10 = (bf16[1,48,32,128]{3,2,1,0:T(8,128)(2,1)}, bf16[1,48,32,128]{3,2,1,0:T(8,128)(2,1)}, u32[]{:S(2)}, u32[]{:S(2)}) collective-permute-start(bf16[1,48,32,128]{3,2,1,0:T(8,128)(2,1)} %get-tuple-element.32.refs_7_), channel_id=1, source_target_pairs={{0,16},{8,24},{16,0},{24,8},{1,17},{9,25},{17,1},{25,9},{2,18},{10... | collective-permute-start | bytes 1179656 | tf_op jit(solution)/shard_map/ppermute | solution.py:175
  203.8 69.9 %collective-permute-start.11 = (bf16[1,48,32,128]{3,2,1,0:T(8,128)(2,1)}, bf16[1,48,32,128]{3,2,1,0:T(8,128)(2,1)}, u32[]{:S(2)}, u32[]{:S(2)}) collective-permute-start(bf16[1,48,32,128]{3,2,1,0:T(8,128)(2,1)} %get-tuple-element.33), channel_id=1, source_target_pairs={{0,24},{8,16},{16,8},{24,0},{1,25},{9,17},{17,9},{25,1},{2,26},{10... | collective-permute-start | bytes 1179656 | tf_op jit(solution)/shard_map/ppermute | solution.py:175
  252.4 1.5 copy-start.14
  252.4 21.3 %copy-start = (f32[2,2,2,4,4,32,128]{6,5,4,3,2,1,0:T(8,128)S(1)}, f32[2,2,2,4,4,32,128]{6,5,4,3,2,1,0:T(8,128)}, u32[]{:S(2)}) copy-start(f32[2,2,2,4,4,32,128]{6,5,4,3,2,1,0:T(8,128)} %bitcast_add_fusion.refs_1_) | copy-start | bytes 6291460
  252.4 39.0 %collective-permute-start.15 = (f32[2,2,2,4,2,32,128]{6,5,4,3,2,1,0:T(8,128)}, f32[2,2,2,4,2,32,128]{6,5,4,3,2,1,0:T(8,128)}, u32[]{:S(2)}, u32[]{:S(2)}) collective-permute-start(f32[2,2,2,4,2,32,128]{6,5,4,3,2,1,0:T(8,128)} %gate.8), channel_id=1, source_target_pairs={{0,1},{1,0},{2,3},{3,2},{4,5},{5,4},{6,7},{7,6},{8,9},{9,8},{10,11... | collective-permute-start | bytes 3145736 | tf_op jit(solution)/shard_map/ppermute | solution.py:175
  253.9 69.8 %collective-permute-start.1 = (bf16[1,48,32,128]{3,2,1,0:T(8,128)(2,1)S(1)}, bf16[1,48,32,128]{3,2,1,0:T(8,128)(2,1)}, u32[]{:S(2)}, u32[]{:S(2)}) collective-permute-start(bf16[1,48,32,128]{3,2,1,0:T(8,128)(2,1)S(1)} %copy-done.14), channel_id=1, source_target_pairs={{0,16},{8,24},{16,0},{24,8},{1,17},{9,25},{17,1},{25,9},{2,18},{10... | collective-permute-start | bytes 1179656 | tf_op jit(solution)/shard_map/ppermute | solution.py:175
  270.4 53.3 %collective-permute-start.2 = (bf16[1,48,32,128]{3,2,1,0:T(8,128)(2,1)}, bf16[1,48,32,128]{3,2,1,0:T(8,128)(2,1)}, u32[]{:S(2)}, u32[]{:S(2)}) collective-permute-start(bf16[1,48,32,128]{3,2,1,0:T(8,128)(2,1)} %get-tuple-element.28), channel_id=1, source_target_pairs={{0,24},{8,16},{16,8},{24,0},{1,25},{9,17},{17,9},{25,1},{2,26},{10... | collective-permute-start | bytes 1179656 | tf_op jit(solution)/shard_map/ppermute | solution.py:175
  273.8 43.5 %collective-permute-start.16 = (f32[2,2,4,4,32,128]{5,4,3,2,1,0:T(8,128)S(1)}, f32[2,2,4,4,32,128]{5,4,3,2,1,0:T(8,128)}, u32[]{:S(2)}, u32[]{:S(2)}) collective-permute-start(f32[2,2,4,4,32,128]{5,4,3,2,1,0:T(8,128)S(1)} %dynamic-slice_bitcast_fusion.1), channel_id=1, source_target_pairs={{0,8},{8,0},{16,24},{24,16},{1,9},{9,1},{17,25},{25,17},{2,10},{10... | collective-permute-start | bytes 3145736 | tf_op jit(solution)/shard_map/ppermute | solution.py:175
  288.0 49.9 %all-to-all-start.1 = ((bf16[32,2,32,128]{3,2,1,0:T(8,128)(2,1)}), bf16[32,2,32,128]{3,2,1,0:T(8,128)(2,1)}, u32[]{:S(2)}, u32[]{:S(2)}) async-start(bf16[32,2,32,128]{3,2,1,0:T(8,128)(2,1)} %bitcast.50), calls=%async_computation.1 | async-start | bytes 1048576 | tf_op jit(solution)/shard_map/all_to_all | solution.py:316
  293.1 25.6 %copy-start.3 = (f32[2,2,2,4,2,32,128]{6,5,4,3,2,1,0:T(8,128)}, f32[2,2,2,4,2,32,128]{6,5,4,3,2,1,0:T(8,128)S(1)}, u32[]{:S(2)}) copy-start(f32[2,2,2,4,2,32,128]{6,5,4,3,2,1,0:T(8,128)S(1)} %bitcast_add_fusion.2) | copy-start | bytes 3145732
  318.7 2.4 copy-start.1
  319.6 21.1 %collective-permute-start.22 = (bf16[2,4,4,32,128]{4,3,2,1,0:T(8,128)(2,1)}, bf16[2,4,4,32,128]{4,3,2,1,0:T(8,128)(2,1)}, u32[]{:S(2)}, u32[]{:S(2)}) collective-permute-start(bf16[2,4,4,32,128]{4,3,2,1,0:T(8,128)(2,1)} %fusion), channel_id=1, source_target_pairs={{0,16},{8,24},{16,0},{24,8},{1,17},{9,25},{17,1},{25,9},{2,18},{10... | collective-permute-start | bytes 786440 | tf_op jit(solution)/shard_map/ppermute | solution.py:175
  321.1 19.6 %copy-start.2 = (f32[2,2,4,4,32,128]{5,4,3,2,1,0:T(8,128)S(1)}, f32[2,2,4,4,32,128]{5,4,3,2,1,0:T(8,128)}, u32[]{:S(2)}) copy-start(f32[2,2,4,4,32,128]{5,4,3,2,1,0:T(8,128)} %copy-done.1) | copy-start | bytes 3145732
  321.1 22.1 %collective-permute-start.17 = (f32[2,2,4,2,32,128]{5,4,3,2,1,0:T(8,128)}, f32[2,2,4,2,32,128]{5,4,3,2,1,0:T(8,128)S(1)}, u32[]{:S(2)}, u32[]{:S(2)}) collective-permute-start(f32[2,2,4,2,32,128]{5,4,3,2,1,0:T(8,128)} %gate.9), channel_id=1, source_target_pairs={{0,8},{8,0},{16,24},{24,16},{1,9},{9,1},{17,25},{25,17},{2,10},{10... | collective-permute-start | bytes 1572872 | tf_op jit(solution)/shard_map/ppermute | solution.py:175
  337.8 5.3 %copy-start.4 = (f32[2,2,2,4,2,32,128]{6,5,4,3,2,1,0:T(8,128)S(1)}, f32[2,2,2,4,2,32,128]{6,5,4,3,2,1,0:T(8,128)}, u32[]{:S(2)}) copy-start(f32[2,2,2,4,2,32,128]{6,5,4,3,2,1,0:T(8,128)} %copy-done.3) | copy-start | bytes 3145732
  337.9 51.2 %all-to-all-start = ((bf16[32,2,32,128]{3,2,1,0:T(8,128)(2,1)}), bf16[32,2,32,128]{3,2,1,0:T(8,128)(2,1)S(1)}, u32[]{:S(2)}, u32[]{:S(2)}) async-start(bf16[32,2,32,128]{3,2,1,0:T(8,128)(2,1)} %bitcast.49), calls=%async_computation | async-start | bytes 1048576 | tf_op jit(solution)/shard_map/all_to_all | solution.py:316
  341.7 29.9 %copy-start.7 = (f32[2,4,4,32,128]{4,3,2,1,0:T(8,128)}, f32[2,4,4,32,128]{4,3,2,1,0:T(8,128)S(1)}, u32[]{:S(2)}) copy-start(f32[2,4,4,32,128]{4,3,2,1,0:T(8,128)S(1)} %bitcast_add_fusion.3.refs_0_) | copy-start | bytes 1572868
  341.7 21.2 %collective-permute-start.25 = (f32[2,4,4,32,128]{4,3,2,1,0:T(8,128)S(1)}, f32[2,4,4,32,128]{4,3,2,1,0:T(8,128)S(1)}, u32[]{:S(2)}, u32[]{:S(2)}) collective-permute-start(f32[2,4,4,32,128]{4,3,2,1,0:T(8,128)S(1)} %bitcast_add_fusion.3.refs_0_), channel_id=1, source_target_pairs={{0,6},{2,4},{4,2},{6,0},{1,7},{3,5},{5,3},{7,1},{8,14},{10,12},{12... | collective-permute-start | bytes 1572872 | tf_op jit(solution)/shard_map/ppermute | solution.py:312
  343.3 17.9 %collective-permute-start.18 = (bf16[2,4,2,32,128]{4,3,2,1,0:T(8,128)(2,1)S(1)}, bf16[2,4,2,32,128]{4,3,2,1,0:T(8,128)(2,1)S(1)}, u32[]{:S(2)}, u32[]{:S(2)}) collective-permute-start(bf16[2,4,2,32,128]{4,3,2,1,0:T(8,128)(2,1)S(1)} %fusion.1), channel_id=1, source_target_pairs={{0,16},{8,24},{16,0},{24,8},{1,17},{9,25},{17,1},{25,9},{2,18},{10... | collective-permute-start | bytes 393224 | tf_op jit(solution)/shard_map/ppermute | solution.py:175
  345.9 25.8 %collective-permute-start.24 = (f32[2,4,4,32,128]{4,3,2,1,0:T(8,128)S(1)}, f32[2,4,4,32,128]{4,3,2,1,0:T(8,128)S(1)}, u32[]{:S(2)}, u32[]{:S(2)}) collective-permute-start(f32[2,4,4,32,128]{4,3,2,1,0:T(8,128)S(1)} %bitcast_add_fusion.3.refs_0_), channel_id=1, source_target_pairs={{0,4},{2,6},{4,0},{6,2},{1,5},{3,7},{5,1},{7,3},{8,12},{10,14},{12... | collective-permute-start | bytes 1572872 | tf_op jit(solution)/shard_map/ppermute | solution.py:312
  346.4 25.2 %collective-permute-start.23 = (f32[2,4,4,32,128]{4,3,2,1,0:T(8,128)S(1)}, f32[2,4,4,32,128]{4,3,2,1,0:T(8,128)S(1)}, u32[]{:S(2)}, u32[]{:S(2)}) collective-permute-start(f32[2,4,4,32,128]{4,3,2,1,0:T(8,128)S(1)} %bitcast_add_fusion.3.refs_0_), channel_id=1, source_target_pairs={{0,2},{2,0},{4,6},{6,4},{1,3},{3,1},{5,7},{7,5},{8,10},{10,8},{12,... | collective-permute-start | bytes 1572872 | tf_op jit(solution)/shard_map/ppermute | solution.py:312
  361.3 21.4 %copy-start.8 = (f32[2,4,2,32,128]{4,3,2,1,0:T(8,128)}, f32[2,4,2,32,128]{4,3,2,1,0:T(8,128)S(1)}, u32[]{:S(2)}) copy-start(f32[2,4,2,32,128]{4,3,2,1,0:T(8,128)S(1)} %bitcast_add_fusion.5.refs_0_) | copy-start | bytes 786436
  361.3 16.7 %collective-permute-start.21 = (f32[2,4,2,32,128]{4,3,2,1,0:T(8,128)S(1)}, f32[2,4,2,32,128]{4,3,2,1,0:T(8,128)S(1)}, u32[]{:S(2)}, u32[]{:S(2)}) collective-permute-start(f32[2,4,2,32,128]{4,3,2,1,0:T(8,128)S(1)} %bitcast_add_fusion.5.refs_0_), channel_id=1, source_target_pairs={{0,6},{2,4},{4,2},{6,0},{1,7},{3,5},{5,3},{7,1},{8,14},{10,12},{12... | collective-permute-start | bytes 786440 | tf_op jit(solution)/shard_map/ppermute | solution.py:312
  362.1 20.6 %collective-permute-start.20 = (f32[2,4,2,32,128]{4,3,2,1,0:T(8,128)S(1)}, f32[2,4,2,32,128]{4,3,2,1,0:T(8,128)S(1)}, u32[]{:S(2)}, u32[]{:S(2)}) collective-permute-start(f32[2,4,2,32,128]{4,3,2,1,0:T(8,128)S(1)} %bitcast_add_fusion.5.refs_0_), channel_id=1, source_target_pairs={{0,4},{2,6},{4,0},{6,2},{1,5},{3,7},{5,1},{7,3},{8,12},{10,14},{12... | collective-permute-start | bytes 786440 | tf_op jit(solution)/shard_map/ppermute | solution.py:312
  362.9 8.7 %copy-start.10 = (f32[2,4,4,32,128]{4,3,2,1,0:T(8,128)}, f32[2,4,4,32,128]{4,3,2,1,0:T(8,128)S(1)}, u32[]{:S(2)}) copy-start(f32[2,4,4,32,128]{4,3,2,1,0:T(8,128)S(1)} %collective-permute-done.25.refs_3_) | copy-start | bytes 1572868
  362.9 19.8 %collective-permute-start.19 = (f32[2,4,2,32,128]{4,3,2,1,0:T(8,128)S(1)}, f32[2,4,2,32,128]{4,3,2,1,0:T(8,128)S(1)}, u32[]{:S(2)}, u32[]{:S(2)}) collective-permute-start(f32[2,4,2,32,128]{4,3,2,1,0:T(8,128)S(1)} %bitcast_add_fusion.5.refs_0_), channel_id=1, source_target_pairs={{0,2},{2,0},{4,6},{6,4},{1,3},{3,1},{5,7},{7,5},{8,10},{10,8},{12,... | collective-permute-start | bytes 786440 | tf_op jit(solution)/shard_map/ppermute | solution.py:312
  371.6 0.8 copy-start.11
  372.4 0.8 copy-start.12
  378.0 4.7 %copy-start.16 = (f32[2,4,2,32,128]{4,3,2,1,0:T(8,128)}, f32[2,4,2,32,128]{4,3,2,1,0:T(8,128)S(1)}, u32[]{:S(2)}) copy-start(f32[2,4,2,32,128]{4,3,2,1,0:T(8,128)S(1)} %collective-permute-done.21.refs_3_) | copy-start | bytes 786436
  382.7 0.7 copy-start.17
  383.4 0.7 copy-start.18
  389.0 0.8 copy-start.6
